TPU v7x, 32 devices: a whole 2x2x4 slice. The times are simulated.
32 devices in a mesh: groups: 2 (over y), cell: 4 (over z), frame: 4 (over x, core).
Axes of the slice: x: 2, y: 2, z: 4, core: 2. Of those that a mesh axis runs over, the one named last changes fastest.
Arguments:
- frames: bfloat16 [32768, 1024], P(('groups', 'cell', 'frame')), parts along dimension 0, may hold values from -6 to 6
- labels: int32 [32768, 1], P(('groups', 'cell', 'frame')), parts along dimension 0, may hold values from 0 to 23, as said below
- centroids: bfloat16 [24, 256, 1024], P('cell'), may hold values from -0.6 to 0.6
- sharpness: float32 [24], P('cell'), may hold values from 0.5 to 2
Outputs:
- new_centroids: float32 [48, 256, 1024], P(('groups', 'cell'), 'frame'), parts along dimension 0
- child_mass: float32 [48, 256], P(('groups', 'cell'), 'frame'), parts along dimension 0
- frame_score: float32 [32768], P(('groups', 'cell', 'frame')), parts along dimension 0
There are 2 independent parts, one for each index of `groups`. A program takes and returns all parts, laid end to end along the dimension named above; an argument that names none is the same for every part. Nothing has to cross between parts.
Inputs may be any that keep to these rules, and one draw needn't show every extreme that they name: Among the frames of one device (aligned blocks of 1024 rows) no label occurs more than 128 times, and the labels c with the same c // 6 occur at most 512 times together; in every such block some label occurs exactly 128 times and some group of labels with the same c // 6 exactly 512 times.
All inputs are finite; a program needn't handle non-finite values.
Results may differ from a plain program's by a relative error of at most 0.0026.
Values may be sent and summed in bfloat16 or wider, within the bound.
No kernel may reach another device: no remote copies, remote signals or barrier semaphores. Data moves between devices by JAX's collectives and lax.ppermute only.
A program may use at most 128 MiB of HBM per device.

v0:
```python
import jax
import jax.numpy as jnp
from jax import lax
from jax.sharding import PartitionSpec as P

prior_mass = 1.0


def on_device(frames, labels, centroids, sharpness):
    cell_count = lax.axis_size("cell")
    cells_local = centroids.shape[0]
    kids_count = centroids.shape[1]
    feat_width = centroids.shape[2]
    rows_local = frames.shape[0]
    cells_total = cells_local * cell_count
    slot_count = 3 * rows_local // cells_total
    block_rows = cell_count * slot_count
    frame_label = labels[:, 0]
    label_hits = (frame_label[:, None] == jnp.arange(cells_total, dtype=jnp.int32)[None, :]).astype(
        jnp.int32
    )
    ranking = jnp.sum(jnp.cumsum(label_hits, axis=0) * label_hits, axis=1) - 1
    label_counts = jnp.sum(label_hits, axis=0)
    owner_index = frame_label // cells_local
    count_grid = label_counts.reshape(cell_count, cells_local)
    count_upper = (count_grid // 128).astype(jnp.bfloat16)
    count_lower = (count_grid % 128).astype(jnp.bfloat16)
    owner_slots = 2 * rows_local // cell_count
    start_grid = jnp.cumsum(count_grid, axis=1) - count_grid
    position = jnp.sum(label_hits * start_grid.reshape(-1)[None, :], axis=1) + ranking
    flat_slot = owner_index * owner_slots + position
    outgoing = (
        jnp.zeros((cell_count * owner_slots, feat_width), jnp.bfloat16).at[flat_slot].set(frames)
    )
    outgoing = outgoing.reshape(cell_count, owner_slots, feat_width)
    incoming, upper_in, lower_in = (
        lax.all_to_all(outgoing, "cell", split_axis=0, concat_axis=0, tiled=True),
        lax.all_to_all(count_upper, "cell", split_axis=0, concat_axis=0, tiled=True),
        lax.all_to_all(count_lower, "cell", split_axis=0, concat_axis=0, tiled=True),
    )
    held_grid = upper_in.astype(jnp.int32) * 128 + lower_in.astype(jnp.int32)
    end_grid = jnp.cumsum(held_grid, axis=1)
    begin_grid = end_grid - held_grid
    slot_place = jnp.arange(owner_slots, dtype=jnp.int32)
    cell_pick = jnp.sum(
        (slot_place[None, :, None] >= end_grid[:, None, :]).astype(jnp.int32), axis=2
    )
    in_use = cell_pick < cells_local
    pick_hits = cell_pick[:, :, None] == jnp.arange(cells_local, dtype=jnp.int32)[None, None, :]
    begin_row = jnp.sum(jnp.where(pick_hits, begin_grid[:, None, :], 0), axis=2)
    source_ids = jnp.arange(cell_count, dtype=jnp.int32)[:, None]
    dump_row = cells_local * block_rows
    destination = jnp.where(
        in_use,
        cell_pick * block_rows + source_ids * slot_count + slot_place[None, :] - begin_row,
        dump_row,
    )
    arranged = (
        jnp.zeros((dump_row + 1, feat_width), jnp.bfloat16)
        .at[destination.reshape(-1)]
        .set(incoming.reshape(-1, feat_width))
    )
    arranged = arranged[:dump_row].reshape(cells_local, block_rows, feat_width)
    held_rows = held_grid.T.astype(jnp.float32)
    slot_ids = jnp.arange(slot_count, dtype=jnp.float32)
    numerators = []
    masses = []
    partitions = []
    for local_cell in range(cells_local):
        chosen = arranged[local_cell]
        is_valid = (slot_ids[None, :] < held_rows[local_cell][:, None]).reshape(-1)
        centre = centroids[local_cell]
        products = lax.dot_general(
            chosen, centre, (((1,), (1,)), ((), ())), preferred_element_type=jnp.float32
        )
        centre_wide = centre.astype(jnp.float32)
        half_norm = 0.5 * jnp.sum(centre_wide * centre_wide, axis=1)
        scores_cell = sharpness[local_cell] * (products - half_norm[None, :])
        highest = jnp.max(scores_cell, axis=1, keepdims=True)
        exponent = jnp.exp(scores_cell - highest)
        totals = jnp.sum(exponent, axis=1, keepdims=True)
        partitions.append((highest[:, 0] + jnp.log(totals[:, 0])).reshape(cell_count, slot_count))
        responsibility = jnp.where(is_valid[:, None], exponent / totals, 0.0)
        numerators.append(
            lax.dot_general(
                responsibility.astype(jnp.bfloat16),
                chosen,
                (((0,), (0,)), ((), ())),
                preferred_element_type=jnp.float32,
            )
        )
        masses.append(jnp.sum(responsibility, axis=0))
    numer_all = jnp.stack(numerators, axis=0)
    mass_all = jnp.stack(masses, axis=0)
    gathered_scores = jnp.stack(partitions, axis=0).reshape(-1)[jnp.where(in_use, destination, 0)]
    returned = lax.all_to_all(gathered_scores, "cell", split_axis=0, concat_axis=0, tiled=True)
    frame_score = returned.reshape(-1)[flat_slot]
    kid_share = kids_count // lax.axis_size("frame")
    first_kid = lax.axis_index("frame") * kid_share
    numer_sum, mass_sum = lax.psum((numer_all, mass_all), "frame")
    numer_mine = lax.dynamic_slice_in_dim(numer_sum, first_kid, kid_share, 1)
    mass_mine = lax.dynamic_slice_in_dim(mass_sum, first_kid, kid_share, 1)
    previous = lax.dynamic_slice_in_dim(centroids, first_kid, kid_share, 1).astype(jnp.float32)
    updated = (numer_mine + prior_mass * previous) / (mass_mine[:, :, None] + prior_mass)
    return (updated, mass_mine, frame_score)


def solution(mesh):
    return jax.shard_map(
        on_device,
        mesh=mesh,
        in_specs=(
            P(("groups", "cell", "frame"), None),
            P(("groups", "cell", "frame"), None),
            P("cell", None, None),
            P("cell"),
        ),
        out_specs=(
            P(("groups", "cell"), "frame", None),
            P(("groups", "cell"), "frame"),
            P(("groups", "cell", "frame")),
        ),
        check_vma=False,
    )
```

profile of v0, /device:TPU:0, one launch (start us, length us, event | category | flops | bytes accessed | tf_op | source)
XLA Modules:
  0.0 298.7 jit_solution(4664068034045748534)
XLA Ops:
  7.2 0.8 convert_reduce_fusion
  8.7 6.3 %all-to-all-start.1 = ((bf16[4,1,6]{2,1,0:T(2,128)(2,1)}), bf16[4,1,6]{2,1,0:T(2,128)(2,1)S(1)}, u32[]{:S(2)}, u32[]{:S(2)}) async-start(bf16[4,1,6]{2,1,0:T(2,128)(2,1)} %copy.17), calls=%async_computation.1 | async-start | bytes 4096 | tf_op jit(solution)/shard_map/all_to_all | solution.py:39
  16.0 6.8 %reduce-window.6 = s32[24,8,128]{2,1,0:T(8,128)S(1)} reduce-window(s32[24,8,128]{2,1,0:T(8,128)S(1)} %fusion.60, s32[]{:T(128)} %constant.32.clone.1), window={size=1x1x128 pad=0_0x0_0x127_0}, to_apply=%region_6.7 | reduce-window | flops 3121152 | bytes 196612 | tf_op jit(solution)/shard_map/reduce-window
  25.3 5.1 %all-to-all-start = ((bf16[4,1,6]{2,1,0:T(2,128)(2,1)}), bf16[4,1,6]{2,1,0:T(2,128)(2,1)S(1)}, u32[]{:S(2)}, u32[]{:S(2)}) async-start(bf16[4,1,6]{2,1,0:T(2,128)(2,1)} %copy.15), calls=%async_computation | async-start | bytes 4096 | tf_op jit(solution)/shard_map/all_to_all | solution.py:38
  30.4 8.8 %scatter_custom_fusion = bf16[2048,1024]{1,0:T(8,128)(2,1)} fusion(s32[1024]{0:T(1024)S(1)} %bitcast.165, bf16[1024,1024]{1,0:T(8,128)(2,1)} %param.4, bf16[]{:T(256)} %constant.70.clone.1), kind=kCustom, calls=%fused_computation.6 | custom fusion | bytes 4194816 | tf_op jit(solution)/shard_map/scatter | solution.py:33
  39.3 5.1 %all-to-all-start.2 = ((bf16[4,512,1024]{2,1,0:T(8,128)(2,1)}), bf16[4,512,1024]{2,1,0:T(8,128)(2,1)}, u32[]{:S(2)}, u32[]{:S(2)}) async-start(bf16[4,512,1024]{2,1,0:T(8,128)(2,1)} %bitcast.156), calls=%async_computation.2 | async-start | bytes 8388608 | tf_op jit(solution)/shard_map/all_to_all | solution.py:37
  46.9 89.9 %all-to-all-done.2 = bf16[4,512,1024]{2,1,0:T(8,128)(2,1)} async-done(((bf16[4,512,1024]{2,1,0:T(8,128)(2,1)}), bf16[4,512,1024]{2,1,0:T(8,128)(2,1)}, u32[]{:S(2)}, u32[]{:S(2)}) %all-to-all-start.2) | async-done | bytes 4194336 | tf_op jit(solution)/shard_map/all_to_all | solution.py:37
  136.9 14.2 %scatter_custom_fusion.1 = bf16[3073,1024]{1,0:T(8,128)(2,1)} fusion(s32[2048]{0:T(1024)S(1)} %bitcast.167, bf16[2048,1024]{1,0:T(8,128)(2,1)} %bitcast.14, bf16[]{:T(256)} %constant.70.clone.1), kind=kCustom, calls=%fused_computation.4 | custom fusion | bytes 6294016 | tf_op jit(solution)/shard_map/scatter | solution.py:61
  151.1 2.6 fusion.87
  153.9 2.3 fusion.86
  156.3 1.2 fusion.85
  157.6 1.2 fusion.84
  158.9 1.2 fusion.83
  160.2 1.1 fusion.82
  161.4 1.4 fusion.9
  162.8 1.4 fusion.8
  164.3 1.5 fusion.7
  165.8 1.4 fusion.6
  167.2 1.4 fusion.5
  168.6 1.4 fusion.4
  170.2 20.5 %gather_fusion = f32[2048]{0:T(1024)} fusion(f32[3072]{0:T(1024)S(1)} %bitcast.154, s32[2048]{0:T(1024)S(1)} %broadcast_clamp_fusion), kind=kCustom, calls=%fused_computation | custom fusion | bytes 24576 | tf_op jit(solution)/shard_map/gather | solution.py:95
  190.8 3.2 %all-to-all-start.3 = ((f32[4,1,512]{2,1,0:T(1,128)}), f32[4,1,512]{2,1,0:T(1,128)S(1)}, u32[]{:S(2)}, u32[]{:S(2)}) async-start(f32[4,1,512]{2,1,0:T(1,128)} %bitcast.53), calls=%async_computation.3 | async-start | bytes 16384 | tf_op jit(solution)/shard_map/all_to_all | solution.py:96
  194.0 1.2 fusion.57
  195.2 1.2 fusion.56
  196.5 1.2 fusion.55
  197.7 1.2 fusion.54
  198.9 1.2 fusion.53
  200.2 1.2 fusion.52
  201.5 7.0 %psum.15 = f32[6,256]{1,0:T(8,128)S(1)} all-reduce(f32[6,256]{1,0:T(8,128)S(1)} %stack.58), channel_id=1, replica_groups=mesh['groups'=2,'cell'=4,'frame'=4] {'frame'}, use_global_device_ids=true, to_apply=%region_36.37 | all-reduce | flops 1536 | bytes 12288 | tf_op jit(solution)/shard_map/psum | solution.py:100
  209.2 10.5 %gather_fusion.1 = f32[1024]{0:T(1024)} fusion(f32[2048]{0:T(1024)S(1)} %bitcast.155, s32[1024]{0:T(1024)S(1)} %broadcast_clamp_fusion.1), kind=kCustom, calls=%fused_computation.1 | custom fusion | bytes 12288 | tf_op jit(solution)/shard_map/gather | solution.py:97
  219.7 69.3 %all-reduce.2.cloned.1.call-done = f32[6,256,1024]{2,1,0:T(8,128)} async-done(((f32[6,256,1024]{2,1,0:T(8,128)}), f32[6,256,1024]{2,1,0:T(8,128)}) %all-reduce.2.cloned.1.call-update) | async-done | bytes 6291472 | tf_op jit(solution)/shard_map/psum | solution.py:100
  289.0 2.8 add_divide_fusion
  (79 shorter events, 8.3 us)
Async XLA Ops:
  8.7 16.7 %all-to-all-start.1 = ((bf16[4,1,6]{2,1,0:T(2,128)(2,1)}), bf16[4,1,6]{2,1,0:T(2,128)(2,1)S(1)}, u32[]{:S(2)}, u32[]{:S(2)}) async-start(bf16[4,1,6]{2,1,0:T(2,128)(2,1)} %copy.17), calls=%async_computation.1 | async-start | bytes 4096 | tf_op jit(solution)/shard_map/all_to_all | solution.py:39
  25.3 13.9 %all-to-all-start = ((bf16[4,1,6]{2,1,0:T(2,128)(2,1)}), bf16[4,1,6]{2,1,0:T(2,128)(2,1)S(1)}, u32[]{:S(2)}, u32[]{:S(2)}) async-start(bf16[4,1,6]{2,1,0:T(2,128)(2,1)} %copy.15), calls=%async_computation | async-start | bytes 4096 | tf_op jit(solution)/shard_map/all_to_all | solution.py:38
  30.4 13.9 %copy-start.8 = (f32[6]{0:T(128)S(1)}, f32[6]{0:T(128)}, u32[]{:S(2)}) copy-start(f32[6]{0:T(128)} %param.7) | copy-start | bytes 76
  30.4 14.6 %copy-start.1 = (bf16[6,256,1024]{2,1,0:T(8,128)(2,1)S(1)}, bf16[6,256,1024]{2,1,0:T(8,128)(2,1)}, u32[]{:S(2)}) copy-start(bf16[6,256,1024]{2,1,0:T(8,128)(2,1)} %param.6) | copy-start | bytes 9437188
  39.3 97.6 %all-to-all-start.2 = ((bf16[4,512,1024]{2,1,0:T(8,128)(2,1)}), bf16[4,512,1024]{2,1,0:T(8,128)(2,1)}, u32[]{:S(2)}, u32[]{:S(2)}) async-start(bf16[4,512,1024]{2,1,0:T(8,128)(2,1)} %bitcast.156), calls=%async_computation.2 | async-start | bytes 8388608 | tf_op jit(solution)/shard_map/all_to_all | solution.py:37
  44.4 244.7 %all-reduce.2.cloned.1.call-start = ((), (), s32[]{:S(2)}) async-start(), calls=%async_computation.4 | async-start | bytes 12582912 | tf_op jit(solution)/shard_map/psum | solution.py:100
  151.1 5.2 %copy-start = (bf16[3073,1024]{1,0:T(8,128)(2,1)S(1)}, bf16[3073,1024]{1,0:T(8,128)(2,1)}, u32[]{:S(2)}) copy-start(bf16[3073,1024]{1,0:T(8,128)(2,1)} %scatter_custom_fusion.1) | copy-start | bytes 18880516
  153.7 14.9 %copy-start.2 = (f32[512,256]{0,1:T(8,128)}, f32[512,256]{0,1:T(8,128)S(1)}, u32[]{:S(2)}) copy-start(f32[512,256]{0,1:T(8,128)S(1)} %get-tuple-element.40) | copy-start | bytes 1572868
  156.2 11.0 %copy-start.3 = (f32[512,256]{0,1:T(8,128)}, f32[512,256]{0,1:T(8,128)S(1)}, u32[]{:S(2)}) copy-start(f32[512,256]{0,1:T(8,128)S(1)} %get-tuple-element.38) | copy-start | bytes 1572868
  157.5 8.3 %copy-start.4 = (f32[512,256]{0,1:T(8,128)}, f32[512,256]{0,1:T(8,128)S(1)}, u32[]{:S(2)}) copy-start(f32[512,256]{0,1:T(8,128)S(1)} %get-tuple-element.36) | copy-start | bytes 1572868
  158.8 5.5 %copy-start.5 = (f32[512,256]{0,1:T(8,128)}, f32[512,256]{0,1:T(8,128)S(1)}, u32[]{:S(2)}) copy-start(f32[512,256]{0,1:T(8,128)S(1)} %get-tuple-element.34) | copy-start | bytes 1572868
  160.1 4.2 %copy-start.6 = (f32[512,256]{0,1:T(8,128)}, f32[512,256]{0,1:T(8,128)S(1)}, u32[]{:S(2)}) copy-start(f32[512,256]{0,1:T(8,128)S(1)} %get-tuple-element.32) | copy-start | bytes 1572868
  161.3 4.5 %copy-start.7 = (f32[512,256]{0,1:T(8,128)}, f32[512,256]{0,1:T(8,128)S(1)}, u32[]{:S(2)}) copy-start(f32[512,256]{0,1:T(8,128)S(1)} %get-tuple-element.30) | copy-start | bytes 1572868
  190.8 18.4 %all-to-all-start.3 = ((f32[4,1,512]{2,1,0:T(1,128)}), f32[4,1,512]{2,1,0:T(1,128)S(1)}, u32[]{:S(2)}, u32[]{:S(2)}) async-start(f32[4,1,512]{2,1,0:T(1,128)} %bitcast.53), calls=%async_computation.3 | async-start | bytes 16384 | tf_op jit(solution)/shard_map/all_to_all | solution.py:96
Sparse Core Ops, SparseCore 0:
  170.2 118.8 all-reduce.1
where the time goes:
time: 300 us; the launch traced here: 299 us
  waiting for transfers between devices  159 us (53%)
  local copies, waits for them, and re-layouts  57 us (19%)
  other arithmetic  23.2 us (8%)
  starting transfers between devices  19.8 us (7%)
  matrix products  18.2 us (6%)
  between operations  14.2 us (5%)
  blocking collectives  7.04 us (2%)
    all_to_all x1, waiting for transfers between devices, on_device(): lax.all_to_all(outgoing, 'cell', split_axis=0, concat_axis=0, tiled=True)  89.9 us
    psum x1, waiting for transfers between devices, on_device(): numer_sum, mass_sum = lax.psum((numer_all, mass_all), 'frame')  69.3 us
    gather x1, local copies, waits for them, and re-layouts, on_device(): jnp.stack(partitions, axis=0).reshape(-1)[jnp.where(in_use, destination, 0)]  20.5 us
    scatter x1, local copies, waits for them, and re-layouts, on_device(): arranged = jnp.zeros((dump_row + 1, feat_width), jnp.bfloat16).at[destina...  14.2 us
    gather x1, local copies, waits for them, and re-layouts, on_device(): frame_score = returned.reshape(-1)[flat_slot]  10.5 us
    dot_general x6, matrix products, on_device(): lax.dot_general(chosen, centre, (((1,), (1,)), ((), ())), preferred_eleme...  9.54 us
    scatter x1, local copies, waits for them, and re-layouts, on_device(): jnp.zeros((cell_count * owner_slots, feat_width), jnp.bfloat16)  8.84 us
    dot_general x6, matrix products, on_device(): lax.dot_general(responsibility.astype(jnp.bfloat16), chosen, (((0,), (0,)...  8.62 us
  transfers between devices with their start and end apart: 5, of which 2 were waited for; matrix products, arithmetic and copies ran while one was open for 20% of the time, Pallas kernels for 0%

commit v1 on v0

v1 whole, which is shorter than its diff:
```python
import functools

import jax
import jax.numpy as jnp
from jax import lax
from jax.experimental import pallas as pl
from jax.experimental.pallas import tpu as pltpu
from jax.sharding import PartitionSpec as P

prior_mass = 1.0
cores = 2
wire = jnp.bfloat16
vmem_limit = 48 * 1024 * 1024


def _hot(flat_row, segment, own_slots):
    rows = flat_row.shape[1]
    slot = lax.broadcasted_iota(jnp.int32, (own_slots, rows), 0) + segment * own_slots
    return jnp.where(slot == flat_row, 1.0, 0.0).astype(jnp.bfloat16)


def _pick(flat_row, frames_ref, segment, out_ref):
    hot = _hot(flat_row, segment, out_ref.shape[0])
    out_ref[...] = jnp.dot(hot, frames_ref[...], preferred_element_type=jnp.float32).astype(
        jnp.bfloat16
    )


def _place_kernel(
    cells_local, window, own_slots, segments, rel_ref, frames_ref, flat_ref, off_ref, meta_ref, *outs
):
    rows = rel_ref.shape[1]
    cells = meta_ref.shape[0]
    rel = rel_ref[...]
    cell = lax.broadcasted_iota(jnp.int32, (cells, rows), 0)
    base = jnp.zeros_like(cell)
    segment = jnp.zeros_like(rel)
    for g in range(1, cells // cells_local):
        base += jnp.where(cell >= g * cells_local, cells_local, 0)
        segment += jnp.where(rel >= g * cells_local, 1, 0)
    hits = jnp.where(rel == cell, 1, 0)
    lane = lax.broadcasted_iota(jnp.int32, (cells, rows), 1)
    running = hits
    step = 1
    while step < rows:
        running += jnp.where(lane >= step, pltpu.roll(running, step, 1), 0)
        step *= 2
    count = jnp.sum(hits, axis=1, keepdims=True)
    start = jnp.sum(jnp.where((rel < cell) & (rel >= base), 1, 0), axis=1, keepdims=True)
    first = jnp.minimum((start >> 4) << 4, own_slots - window)
    position = jnp.sum(hits * (running + (start - 1)), axis=0, keepdims=True)
    flat = segment * own_slots + position
    flat_ref[...] = flat
    off_ref[...] = jnp.sum(hits * (running + (start - first - 1)), axis=0, keepdims=True)
    column = lax.broadcasted_iota(jnp.int32, meta_ref.shape, 1)
    meta_ref[...] = jnp.where(
        column == 0, first, jnp.where(column == 1, start - first, jnp.where(column == 2, count, 0))
    )
    for g, out_ref in zip(segments, outs, strict=True):
        _pick(flat, frames_ref, g, out_ref)


def _pick_kernel(segments, flat_ref, frames_ref, *outs):
    flat = flat_ref[...]
    for g, out_ref in zip(segments, outs, strict=True):
        _pick(flat, frames_ref, g, out_ref)


def _cell_kernel(sources, window, pieces, share, lanes, *refs):
    meta = refs[:sources]
    sharp_ref = refs[sources + 1]
    refs = refs[sources + 2 :]
    centre_refs, refs = refs[:pieces], refs[pieces:]
    row_refs, refs = refs[:sources], refs[sources:]
    keep_ref, mass_ref, score_ref = refs[:3]
    send_refs, (held, sems) = refs[3:-2], refs[-2:]
    copies = []
    for s in range(sources):
        first = pl.multiple_of(meta[s][lanes[s], 0], 16)
        copies.append(
            pltpu.make_async_copy(
                row_refs[s].at[pl.ds(first, window)],
                held.at[pl.ds(s * window, window)],
                sems.at[s],
            )
        )
    for copy in copies:
        copy.start()
    centre = jnp.concatenate([c[...].reshape(c.shape[-2:]) for c in centre_refs], axis=0)
    wide = centre.astype(jnp.float32)
    half_norm = 0.5 * jnp.sum(wide * wide, axis=1, keepdims=True)
    slot = lax.broadcasted_iota(jnp.int32, (1, sources * window), 1)
    valid = slot < 0
    for s in range(sources):
        begin = s * window + meta[s][lanes[s], 1]
        valid = valid | ((slot >= begin) & (slot < begin + meta[s][lanes[s], 2]))
    for copy in copies:
        copy.wait()
    chosen = held[...]
    products = lax.dot_general(
        centre, chosen, (((1,), (1,)), ((), ())), preferred_element_type=jnp.float32
    )
    scores = sharp_ref[0] * (products - half_norm)
    top = jnp.max(scores, axis=0, keepdims=True)
    exponent = jnp.exp(scores - top)
    total = jnp.sum(exponent, axis=0, keepdims=True)
    score_ref[...] = jnp.broadcast_to(
        jnp.where(valid, top + jnp.log(total), 0.0), score_ref.shape
    )
    resp = exponent * jnp.where(valid, 1.0 / total, 0.0)
    mass = jnp.sum(resp, axis=1, keepdims=True)
    mass_ref[...] = jnp.broadcast_to(mass, (mass.shape[0], 128)).T[: mass_ref.shape[0]]
    low = resp.astype(jnp.bfloat16)
    numer = jnp.dot(low, chosen, preferred_element_type=jnp.float32)
    keep_ref[...] = numer[:share]
    for n, ref in enumerate(send_refs):
        ref[...] = numer[(n + 1) * share : (n + 2) * share].astype(ref.dtype)


def _score_kernel(cells, window, rel_ref, off_ref, values_ref, out_ref):
    rows = rel_ref.shape[1]
    hot = jnp.where(
        lax.broadcasted_iota(jnp.int32, (window, rows), 0) == off_ref[...], 1.0, 0.0
    ).astype(jnp.bfloat16)
    rest = values_ref[...]
    mine = lax.broadcasted_iota(jnp.int32, (cells, rows), 0) == rel_ref[...]
    total = jnp.zeros((cells, rows), jnp.float32)
    for _ in range(3):
        term = rest.astype(jnp.bfloat16)
        rest = rest - term.astype(jnp.float32)
        total += jnp.dot(term, hot, preferred_element_type=jnp.float32)
    out_ref[...] = jnp.sum(jnp.where(mine, total, 0.0), axis=0, keepdims=True)


def _params():
    return pltpu.CompilerParams(vmem_limit_bytes=vmem_limit)


def _cell_call(meta, code, sharp, centre_in, row_blocks, window, lanes, kids, share, sends):
    sources = len(row_blocks)
    width = row_blocks[0].shape[1]
    pieces = len(centre_in)
    arrays, specs = zip(*centre_in, strict=True)
    whole = lambda shape: pl.BlockSpec(shape, lambda g, *_: (0,) * len(shape))
    out_shape = [
        jax.ShapeDtypeStruct((share, width), jnp.float32),
        jax.ShapeDtypeStruct((8, kids), jnp.float32),
        jax.ShapeDtypeStruct((8, sources * window), jnp.float32),
    ] + [jax.ShapeDtypeStruct((share, width), wire)] * sends
    rows = sources * window
    return pl.pallas_call(
        functools.partial(_cell_kernel, sources, window, pieces, share, lanes),
        grid_spec=pltpu.PrefetchScalarGridSpec(
            num_scalar_prefetch=sources + 2,
            grid=(1,),
            in_specs=list(specs) + [pl.BlockSpec(memory_space=pl.ANY)] * sources,
            out_specs=[whole(o.shape) for o in out_shape],
            scratch_shapes=[
                pltpu.VMEM((rows, width), jnp.bfloat16),
                pltpu.SemaphoreType.DMA((sources,)),
            ],
        ),
        out_shape=out_shape,
        compiler_params=_params(),
        cost_estimate=pl.CostEstimate(
            flops=4 * kids * rows * width,
            bytes_accessed=2 * (kids + rows) * width + 6 * kids * width,
            transcendentals=kids * rows,
        ),
    )(*meta, code, sharp, *arrays, *row_blocks)


def on_device(frames, labels, centroids, sharpness):
    cell_count = lax.axis_size("cell")
    frame_count = lax.axis_size("frame")
    group_count = lax.axis_size("groups")
    cells_local, kids, width = centroids.shape
    rows = frames.shape[0]
    cells_total = cells_local * cell_count
    half = cell_count // 2
    chips = frame_count // cores
    per_core = cells_local // cores
    cell_cap = 3 * rows // cells_total
    own_slots = 2 * rows // cell_count
    sources = half * cores
    window = -(-(cell_cap + 16) // 16) * 16
    while sources * window % 128:
        window += 16
    window = min(window, own_slots)
    share = kids // chips
    piece = share // group_count

    z = lax.axis_index("cell")
    j = lax.axis_index("frame")
    y = lax.axis_index("groups")
    x, k = j // cores, j % cores
    p, h = z % half, z // half

    def at(zz, xx, kk):
        return zz * frame_count + xx * cores + kk

    def hop_core(v):
        return lax.ppermute(v, "frame", [(i, i ^ 1) for i in range(frame_count)])

    def hop_chip(v, s):
        return lax.ppermute(
            v,
            "frame",
            [(a * cores + c, (a + s) % chips * cores + c) for a in range(chips) for c in range(cores)],
        )

    def hop_member(v, s):
        return lax.ppermute(
            v, "cell", [(b * half + i, b * half + (i + s) % half) for b in range(2) for i in range(half)]
        )

    def hop_partner(v):
        return lax.ppermute(v, "cell", [(i, (i + half) % cell_count) for i in range(cell_count)])

    def hop_group(v):
        return lax.ppermute(v, "groups", [(i, (i + 1) % group_count) for i in range(group_count)])

    def hop_any(v, s, kk):
        pairs = [
            (at(b * half + i, a, c), at(b * half + (i + s) % half, a, c ^ kk))
            for b in range(2)
            for i in range(half)
            for a in range(chips)
            for c in range(cores)
        ]
        return lax.ppermute(v, ("cell", "frame"), pairs)

    foreign_sharp = hop_partner(sharpness)
    foreign_pieces = []
    for i in range(per_core):
        mine = lax.dynamic_slice(
            centroids, (k * per_core + i, (x * group_count + y) * piece, 0), (1, piece, width)
        )
        first = hop_partner(mine[0])
        found = {(0, 0): first}
        for s in range(1, chips):
            found[s, 0] = hop_chip(first, -s)
        for g in range(1, group_count):
            for s in range(chips):
                found[s, g] = hop_group(found[s, g - 1])
        foreign_pieces.append([found[s, g] for s in range(chips) for g in range(group_count)])

    label = labels.reshape(1, rows)
    owner, local = label // cells_local, label % cells_local
    member = (owner % half - p + half) % half
    foreign = (owner // half != h).astype(jnp.int32)
    other = (local // per_core) ^ k
    rel = ((member * 2 + foreign) * 2 + other) * per_core + local % per_core

    seg = lambda s, t: s * 2 + t
    first_segs = [seg(s, 1) for s in range(1, half)]
    next_segs = [seg(s, 0) for s in range(1, half)]
    last_segs = [seg(0, 1), seg(0, 0)]
    block = jax.ShapeDtypeStruct((own_slots, width), jnp.bfloat16)
    pick_cost = lambda n: pl.CostEstimate(
        flops=2 * n * own_slots * rows * width,
        bytes_accessed=2 * width * (rows + n * own_slots),
        transcendentals=0,
    )
    flat, off, meta, *blocks = pl.pallas_call(
        functools.partial(_place_kernel, cells_local, window, own_slots, first_segs),
        out_shape=[
            jax.ShapeDtypeStruct((1, rows), jnp.int32),
            jax.ShapeDtypeStruct((1, rows), jnp.int32),
            jax.ShapeDtypeStruct((cells_total, 128), jnp.int32),
        ]
        + [block] * len(first_segs),
        compiler_params=_params(),
        cost_estimate=pick_cost(len(first_segs)),
    )(rel, frames)
    segments = dict(zip(first_segs, blocks, strict=True))
    for group in (last_segs, next_segs):
        blocks = pl.pallas_call(
            functools.partial(_pick_kernel, group),
            out_shape=[block] * len(group),
            compiler_params=_params(),
            cost_estimate=pick_cost(len(group)),
        )(flat, frames)
        segments.update(zip(group, blocks, strict=True))

    metas = []
    for s in range(half):
        part = meta[seg(s, 0) * cells_local : (seg(s, 1) + 1) * cells_local]
        for kk in range(cores):
            metas.append(part if s == kk == 0 else hop_any(part, s, kk))
    held = {}
    for t in (1, 0):
        held[t] = []
        for s in range(half):
            mine = segments[seg(s, t)]
            if s:
                mine = hop_member(mine, s)
            held[t] += [mine, hop_core(mine)]

    code = jnp.stack([x, y, k]).astype(jnp.int32)
    results = {}
    for t in (1, 0):
        for i in range(per_core):
            lanes = [t * cells_local + (n % cores) * per_core + i for n in range(sources)]
            sharp = lax.dynamic_slice(
                foreign_sharp if t else sharpness, (k * per_core + i,), (1,)
            )
            centre_in = []
            for s in range(chips):
                for g in range(group_count):
                    if t:
                        spec = pl.BlockSpec((piece, width), lambda n, *_: (0, 0))
                        centre_in.append((foreign_pieces[i][s * group_count + g], spec))
                    else:

                        def where_from(n, *scalars, s=s, g=g, i=i):
                            c = scalars[sources]
                            chip = lax.rem(c[0] + s, chips)
                            return c[2] * per_core + i, chip * group_count + lax.rem(c[1] + g, group_count), 0

                        centre_in.append((centroids, pl.BlockSpec((1, piece, width), where_from)))
            results[t, i] = _cell_call(
                metas, code, sharp, centre_in, held[t], window, lanes, kids, share, chips - 1
            )

    def over_chips(t, i):
        keep, _, _, *sends = results[t, i]
        for s in range(1, chips):
            keep = keep + hop_chip(sends[s - 1], s).astype(jnp.float32)
        return keep

    numer = []
    for i in range(per_core):
        numer.append(hop_partner(over_chips(1, i).astype(wire)))
    for i in range(per_core):
        numer[i] = over_chips(0, i) + numer[i].astype(jnp.float32)

    order = [(t, i) for t in (1, 0) for i in range(per_core)]
    mass_all = jnp.stack([results[o][1][0] for o in order])
    mass_sum = mass_all[:, :share]
    for s in range(1, chips):
        mass_sum = mass_sum + hop_chip(mass_all[:, s * share : (s + 1) * share], s)
    mass = mass_sum[per_core:] + hop_partner(mass_sum[:per_core])

    score_all = jnp.stack([results[o][2][0] for o in order])
    back = {}
    for s in range(half):
        for kk in range(cores):
            n = s * cores + kk
            part = score_all[:, n * window : (n + 1) * window]
            back[s, kk] = part if n == 0 else hop_any(part, -s, kk)
    values = []
    for s in range(half):
        for t in range(2):
            for kk in range(cores):
                at_row = 0 if t else per_core
                values.append(back[s, kk][at_row : at_row + per_core])
    frame_score = pl.pallas_call(
        functools.partial(_score_kernel, cells_total, window),
        out_shape=jax.ShapeDtypeStruct((1, rows), jnp.float32),
        compiler_params=_params(),
        cost_estimate=pl.CostEstimate(
            flops=6 * cells_total * window * rows, bytes_accessed=4 * cells_total * window, transcendentals=0
        ),
    )(rel, off, jnp.concatenate(values, axis=0)).reshape(rows)

    updated = []
    for i in range(per_core):
        previous = jnp.concatenate(
            [
                lax.dynamic_slice(
                    centroids,
                    (k * per_core + i, (x * group_count + (y + g) % group_count) * piece, 0),
                    (1, piece, width),
                )
                for g in range(group_count)
            ],
            axis=1,
        )[0].astype(jnp.float32)
        updated.append(
            (numer[i] + prior_mass * previous) / (mass[i][:, None] + prior_mass)
        )
    updated = jnp.stack(updated)
    mine_at = ((k - y) % group_count) * piece
    theirs_at = ((1 - k - y) % group_count) * piece

    def swap(v):
        mine = lax.dynamic_slice_in_dim(v, mine_at, piece, 1)
        theirs = hop_core(lax.dynamic_slice_in_dim(v, theirs_at, piece, 1))
        return jnp.where(
            k == 0, jnp.concatenate([mine, theirs], 0), jnp.concatenate([theirs, mine], 0)
        )

    return swap(updated), swap(mass), frame_score


def solution(mesh):
    return jax.shard_map(
        on_device,
        mesh=mesh,
        in_specs=(
            P(("groups", "cell", "frame"), None),
            P(("groups", "cell", "frame"), None),
            P("cell", None, None),
            P("cell"),
        ),
        out_specs=(
            P(("groups", "cell"), "frame", None),
            P(("groups", "cell"), "frame"),
            P(("groups", "cell", "frame")),
        ),
        check_vma=False,
    )
```

time: 300 us -> 221 us (0.74)
  local copies, waits for them, and re-layouts: 57 us -> 10.9 us
  Pallas kernels: 0 us -> 41 us
  waiting for transfers between devices: 159 us -> 125 us
  other arithmetic: 23.2 us -> 3.59 us
  starting transfers between devices: 19.8 us -> 39 us
  matrix products: 18.2 us -> 0 us
  between operations: 14.2 us -> 1.22 us
  blocking collectives: 7.04 us -> 0 us
    ppermute x0 -> x38, waiting for transfers between devices: none -> 125 us  [the longest x8 69.5 us: hop_partner(): lax.ppermute(v, 'cell', [(i, (i + half) % cell_count) for i in range(cell...]
    all_to_all x4 -> x0, waiting for transfers between devices: 89.9 us -> none  [the longest x1 89.9 us: on_device(): lax.all_to_all(outgoing, 'cell', split_axis=0, concat_axis=0, tiled=True)]
    psum x1 -> x0, waiting for transfers between devices: 69.3 us -> none  [on_device(): numer_sum, mass_sum = lax.psum((numer_all, mass_all), 'frame')]
    pallas_call x0 -> x10, Pallas kernels: none -> 41 us  [the longest x6 33.7 us: _cell_call(): pl.pallas_call(functools.partial(_cell_kernel, sources, window, pieces, s...]
    ppermute x0 -> x38, starting transfers between devices: none -> 39 us  [the longest x10 12.4 us: hop_chip(): lax.ppermute(v, 'frame', [(a * cores + c, (a + s) % chips * cores + c) fo...]
    gather x2 -> x0, local copies, waits for them, and re-layouts: 31.1 us -> none  [the longest x1 20.5 us: on_device(): jnp.stack(partitions, axis=0).reshape(-1)[jnp.where(in_use, destination, 0)]]
    scatter x2 -> x0, local copies, waits for them, and re-layouts: 23.1 us -> none  [the longest x1 14.2 us: on_device(): arranged = jnp.zeros((dump_row + 1, feat_width), jnp.bfloat16).at[destina...]
    all_to_all x4 -> x0, starting transfers between devices: 19.7 us -> none  [the longest x1 6.32 us: on_device(): lax.all_to_all(count_lower, 'cell', split_axis=0, concat_axis=0, tiled=True)]
  transfers between devices with their start and end apart: 5 -> 38, of which waited for: 2 -> 18; matrix products, arithmetic and copies ran while one was open for 20% -> 3% of each run, Pallas kernels for 0% -> 14%
where the time goes in v1:
time: 221 us
  waiting for transfers between devices  125 us (57%)
  Pallas kernels  41 us (19%)
  starting transfers between devices  39 us (18%)
  local copies, waits for them, and re-layouts  10.9 us (5%)
  other arithmetic  3.59 us (2%)
    ppermute x8, waiting for transfers between devices, hop_partner(): lax.ppermute(v, 'cell', [(i, (i + half) % cell_count) for i in range(cell...  69.5 us
    pallas_call x6, Pallas kernels, _cell_call(): pl.pallas_call(functools.partial(_cell_kernel, sources, window, pieces, s...  33.7 us
    ppermute x10, waiting for transfers between devices, hop_chip(): lax.ppermute(v, 'frame', [(a * cores + c, (a + s) % chips * cores + c) fo...  27.7 us
    ppermute x2, waiting for transfers between devices, hop_member(): lax.ppermute(v, 'cell', [(b * half + i, b * half + (i + s) % half) for b...  21.5 us
    ppermute x10, starting transfers between devices, hop_chip(): lax.ppermute(v, 'frame', [(a * cores + c, (a + s) % chips * cores + c) fo...  12.4 us
    ppermute x8, starting transfers between devices, hop_partner(): lax.ppermute(v, 'cell', [(i, (i + half) % cell_count) for i in range(cell...  7.62 us
    ppermute x6, starting transfers between devices, hop_any(): return lax.ppermute(v, ('cell', 'frame'), pairs)  7.52 us
    ppermute x6, starting transfers between devices, hop_group(): lax.ppermute(v, 'groups', [(i, (i + 1) % group_count) for i in range(grou...  6.9 us
  transfers between devices with their start and end apart: 38, of which 18 were waited for; matrix products, arithmetic and copies ran while one was open for 3% of the time, Pallas kernels for 14%

profile of v1, /device:TPU:0, one launch (start us, length us, event | category | flops | bytes accessed | tf_op | source)
XLA Modules:
  0.0 220.9 jit_solution(3946552635000961203)
XLA Ops:
  1.5 1.6 copy-done.10
  3.1 2.8 %shard_map.67 = (s32[1,1024]{1,0:T(1,128)S(1)}, s32[1,1024]{1,0:T(1,128)S(1)}, s32[24,128]{1,0:T(8,128)S(1)}, bf16[512,1024]{1,0:T(8,128)(2,1)}) custom-call(s32[1,1024]{1,0:T(1,128)S(1)} %fusion.7.rel_ref, bf16[1024,1024]{1,0:T(8,128)(2,1)S(1)} %copy-done.10), custom_call_target="tpu_custom_call" | custom-call | flops 1073741824 | bytes 3145728 | tf_op jit(solution)/shard_map/pallas_call | solution.py:265
  7.2 3.1 %collective-permute-start.4 = (bf16[512,1024]{1,0:T(8,128)(2,1)S(1)}, bf16[512,1024]{1,0:T(8,128)(2,1)S(1)}, u32[]{:S(2)}, u32[]{:S(2)}) collective-permute-start(bf16[512,1024]{1,0:T(8,128)(2,1)S(1)} %shard_map.69), channel_id=1, source_target_pairs={{0,4},{4,0},{8,12},{12,8},{1,5},{5,1},{9,13},{13,9},{2,6},{6,2},{1... | collective-permute-start | bytes 3145736 | tf_op jit(solution)/shard_map/ppermute | solution.py:213
  10.3 2.4 %shard_map.68 = (bf16[512,1024]{1,0:T(8,128)(2,1)}, bf16[512,1024]{1,0:T(8,128)(2,1)S(1)}) custom-call(s32[1,1024]{1,0:T(1,128)S(1)} %get-tuple-element.34.flat_ref, bf16[1024,1024]{1,0:T(8,128)(2,1)S(1)} %copy-done.10), custom_call_target="tpu_custom_call" | custom-call | flops 2147483648 | bytes 4194304 | tf_op jit(solution)/shard_map/pallas_call | solution.py:278
  12.8 21.5 %collective-permute-done.4.refs_12_ = bf16[512,1024]{1,0:T(8,128)(2,1)S(1)} collective-permute-done((bf16[512,1024]{1,0:T(8,128)(2,1)S(1)}, bf16[512,1024]{1,0:T(8,128)(2,1)S(1)}, u32[]{:S(2)}, u32[]{:S(2)}) %collective-permute-start.4) | collective-permute-done | bytes 1048608 | tf_op jit(solution)/shard_map/ppermute | solution.py:213
  34.2 3.1 %collective-permute-start.7 = (f32[6]{0:T(128)S(1)}, f32[6]{0:T(128)S(1)}, u32[]{:S(2)}, u32[]{:S(2)}) collective-permute-start(f32[6]{0:T(128)S(1)} %copy-done.23), channel_id=1, source_target_pairs={{0,8},{4,12},{8,0},{12,4},{1,9},{5,13},{9,1},{13,5},{2,10},{6,14},... | collective-permute-start | bytes 80 | tf_op jit(solution)/shard_map/ppermute | solution.py:218
  37.5 17.7 %collective-permute-done.7 = f32[6]{0:T(128)S(1)} collective-permute-done((f32[6]{0:T(128)S(1)}, f32[6]{0:T(128)S(1)}, u32[]{:S(2)}, u32[]{:S(2)}) %collective-permute-start.7) | collective-permute-done | bytes 56 | tf_op jit(solution)/shard_map/ppermute | solution.py:218
  55.2 1.7 collective-permute-start.2
  58.3 3.4 %collective-permute-start.1 = (s32[12,128]{1,0:T(8,128)S(1)}, s32[12,128]{1,0:T(8,128)S(1)}, u32[]{:S(2)}, u32[]{:S(2)}) collective-permute-start(s32[12,128]{1,0:T(8,128)S(1)} %get-tuple-element.77), channel_id=1, source_target_pairs={{0,4},{1,5},{2,6},{3,7},{4,0},{5,1},{6,2},{7,3},{8,12},{9,13},{10,... | collective-permute-start | bytes 18440 | tf_op jit(solution)/shard_map/ppermute | solution.py:231
  61.7 1.6 collective-permute-done.1.refs_2_
  63.8 2.2 %constant_dynamic-slice_fusion.9 = (bf16[1,64,1024]{2,1,0:T(8,128)(2,1)}, bf16[1,64,1024]{2,1,0:T(8,128)(2,1)}, bf16[1,64,1024]{2,1,0:T(8,128)(2,1)}, bf16[64,10...) fusion(bf16[6,256,1024]{2,1,0:T(8,128)(2,1)} %refs_9_.5, ...), kind=kLoop, calls=%fused_computation.55 | loop fusion | bytes 2359320 | tf_op jit(solution)/shard_map/dynamic_slice | solution.py:371
  66.1 1.9 collective-permute-start.21
  68.0 7.2 %collective-permute-done.21.refs_6_ = bf16[64,1024]{1,0:T(8,128)(2,1)S(1)} collective-permute-done((bf16[64,1024]{1,0:T(8,128)(2,1)S(1)}, bf16[64,1024]{1,0:T(8,128)(2,1)S(1)}, u32[]{:S(2)}, u32[]{:S(2)}) %collective-permute-start.21) | collective-permute-done | bytes 131104 | tf_op jit(solution)/shard_map/ppermute | solution.py:218
  75.2 7.7 %collective-permute-done.17.refs_6_ = bf16[64,1024]{1,0:T(8,128)(2,1)S(1)} collective-permute-done((bf16[64,1024]{1,0:T(8,128)(2,1)S(1)}, bf16[64,1024]{1,0:T(8,128)(2,1)S(1)}, u32[]{:S(2)}, u32[]{:S(2)}) %collective-permute-start.17) | collective-permute-done | bytes 131104 | tf_op jit(solution)/shard_map/ppermute | solution.py:218
  82.9 8.2 %collective-permute-done.8.refs_6_ = bf16[64,1024]{1,0:T(8,128)(2,1)S(1)} collective-permute-done((bf16[64,1024]{1,0:T(8,128)(2,1)S(1)}, bf16[64,1024]{1,0:T(8,128)(2,1)S(1)}, u32[]{:S(2)}, u32[]{:S(2)}) %collective-permute-start.8) | collective-permute-done | bytes 131104 | tf_op jit(solution)/shard_map/ppermute | solution.py:218
  92.6 4.0 %collective-permute-done.23.refs_8_ = bf16[64,1024]{1,0:T(8,128)(2,1)} collective-permute-done((bf16[64,1024]{1,0:T(8,128)(2,1)S(1)}, bf16[64,1024]{1,0:T(8,128)(2,1)}, u32[]{:S(2)}, u32[]{:S(2)}) %collective-permute-start.23) | collective-permute-done | bytes 131104 | tf_op jit(solution)/shard_map/ppermute | solution.py:206
  98.7 2.9 %collective-permute-done.22.refs_7_ = bf16[64,1024]{1,0:T(8,128)(2,1)S(1)} collective-permute-done((bf16[64,1024]{1,0:T(8,128)(2,1)S(1)}, bf16[64,1024]{1,0:T(8,128)(2,1)S(1)}, u32[]{:S(2)}, u32[]{:S(2)}) %collective-permute-start.22) | collective-permute-done | bytes 131104 | tf_op jit(solution)/shard_map/ppermute | solution.py:221
  107.1 5.7 %shard_map.75 = (f32[128,1024]{1,0:T(8,128)S(1)}, f32[8,256]{1,0:T(8,128)S(1)}, f32[8,640]{1,0:T(8,128)S(1)}, bf16[128,1024]{1,0:T(8,128)(2,1)S(1)}) custom-call(s32[12,128]{1,0:T(8,128)S(1)} %get-tuple-element.78.refs_0_, s32[12,128]{1,0:T(8,128)S(1)} %collective-permute-done.refs_1_, s32[12,128]{1,0:T(8,128)S(1)} %collective-permute-done.1.refs_2_, ...), custom_call_target="tpu_custom_call" | custom-call | flops 671088640 | bytes 3407872 | tf_op jit(solution)/shard_map/pallas_call | solution.py:151
  116.4 5.6 %shard_map.74 = (f32[128,1024]{1,0:T(8,128)S(1)}, f32[8,256]{1,0:T(8,128)S(1)}, f32[8,640]{1,0:T(8,128)S(1)}, bf16[128,1024]{1,0:T(8,128)(2,1)S(1)}) custom-call(s32[12,128]{1,0:T(8,128)S(1)} %get-tuple-element.78.refs_0_, s32[12,128]{1,0:T(8,128)S(1)} %collective-permute-done.refs_1_, s32[12,128]{1,0:T(8,128)S(1)} %collective-permute-done.1.refs_2_, ...), custom_call_target="tpu_custom_call" | custom-call | flops 671088640 | bytes 3407872 | tf_op jit(solution)/shard_map/pallas_call | solution.py:151
  125.5 5.7 %shard_map.70 = (f32[128,1024]{1,0:T(8,128)S(1)}, f32[8,256]{1,0:T(8,128)S(1)}, f32[8,640]{1,0:T(8,128)S(1)}, bf16[128,1024]{1,0:T(8,128)(2,1)S(1)}) custom-call(s32[12,128]{1,0:T(8,128)S(1)} %get-tuple-element.78.refs_0_, s32[12,128]{1,0:T(8,128)S(1)} %collective-permute-done.refs_1_, s32[12,128]{1,0:T(8,128)S(1)} %collective-permute-done.1.refs_2_, ...), custom_call_target="tpu_custom_call" | custom-call | flops 671088640 | bytes 3407872 | tf_op jit(solution)/shard_map/pallas_call | solution.py:151
  132.1 5.6 %shard_map.73 = (f32[128,1024]{1,0:T(8,128)S(1)}, f32[8,256]{1,0:T(8,128)S(1)}, f32[8,640]{1,0:T(8,128)S(1)}, bf16[128,1024]{1,0:T(8,128)(2,1)S(1)}) custom-call(s32[12,128]{1,0:T(8,128)S(1)} %get-tuple-element.78.refs_0_, s32[12,128]{1,0:T(8,128)S(1)} %collective-permute-done.refs_1_, s32[12,128]{1,0:T(8,128)S(1)} %collective-permute-done.1.refs_2_, ...), custom_call_target="tpu_custom_call" | custom-call | flops 671088640 | bytes 3407872 | tf_op jit(solution)/shard_map/pallas_call | solution.py:151
  137.8 5.5 %shard_map.72 = (f32[128,1024]{1,0:T(8,128)S(1)}, f32[8,256]{1,0:T(8,128)S(1)}, f32[8,640]{1,0:T(8,128)S(1)}, bf16[128,1024]{1,0:T(8,128)(2,1)S(1)}) custom-call(s32[12,128]{1,0:T(8,128)S(1)} %get-tuple-element.78.refs_0_, s32[12,128]{1,0:T(8,128)S(1)} %collective-permute-done.refs_1_, s32[12,128]{1,0:T(8,128)S(1)} %collective-permute-done.1.refs_2_, ...), custom_call_target="tpu_custom_call" | custom-call | flops 671088640 | bytes 3407872 | tf_op jit(solution)/shard_map/pallas_call | solution.py:151
  143.3 5.6 %shard_map.71 = (f32[128,1024]{1,0:T(8,128)S(1)}, f32[8,256]{1,0:T(8,128)S(1)}, f32[8,640]{1,0:T(8,128)S(1)}, bf16[128,1024]{1,0:T(8,128)(2,1)S(1)}) custom-call(s32[12,128]{1,0:T(8,128)S(1)} %get-tuple-element.78.refs_0_, s32[12,128]{1,0:T(8,128)S(1)} %collective-permute-done.refs_1_, s32[12,128]{1,0:T(8,128)S(1)} %collective-permute-done.1.refs_2_, ...), custom_call_target="tpu_custom_call" | custom-call | flops 671088640 | bytes 3407872 | tf_op jit(solution)/shard_map/pallas_call | solution.py:151
  149.0 1.6 collective-permute-start.25
  150.7 2.0 collective-permute-done.25
  152.8 1.6 collective-permute-start.30
  158.8 19.6 %collective-permute-done.31 = bf16[128,1024]{1,0:T(8,128)(2,1)S(1)} collective-permute-done((bf16[128,1024]{1,0:T(8,128)(2,1)S(1)}, bf16[128,1024]{1,0:T(8,128)(2,1)S(1)}, u32[]{:S(2)}, u32[]{:S(2)}) %collective-permute-start.31) | collective-permute-done | bytes 262176 | tf_op jit(solution)/shard_map/ppermute | solution.py:206
  181.2 2.6 %collective-permute-start.32 = (bf16[128,1024]{1,0:T(8,128)(2,1)S(1)}, bf16[128,1024]{1,0:T(8,128)(2,1)S(1)}, u32[]{:S(2)}, u32[]{:S(2)}) collective-permute-start(bf16[128,1024]{1,0:T(8,128)(2,1)S(1)} %add_convert_fusion), channel_id=1, source_target_pairs={{0,8},{4,12},{8,0},{12,4},{1,9},{5,13},{9,1},{13,5},{2,10},{6,14},... | collective-permute-start | bytes 786440 | tf_op jit(solution)/shard_map/ppermute | solution.py:218
  184.9 2.4 %collective-permute-start.36 = (f32[6,160]{1,0:T(8,128)S(1)}, f32[6,160]{1,0:T(8,128)S(1)}, u32[]{:S(2)}, u32[]{:S(2)}) collective-permute-start(f32[6,160]{1,0:T(8,128)S(1)} %get-tuple-element.75), channel_id=1, source_target_pairs={{0,4},{1,5},{2,6},{3,7},{4,0},{5,1},{6,2},{7,3},{8,12},{9,13},{10,... | collective-permute-start | bytes 11528 | tf_op jit(solution)/shard_map/ppermute | solution.py:231
  187.3 4.3 %collective-permute-done.32 = bf16[128,1024]{1,0:T(8,128)(2,1)S(1)} collective-permute-done((bf16[128,1024]{1,0:T(8,128)(2,1)S(1)}, bf16[128,1024]{1,0:T(8,128)(2,1)S(1)}, u32[]{:S(2)}, u32[]{:S(2)}) %collective-permute-start.32) | collective-permute-done | bytes 262176 | tf_op jit(solution)/shard_map/ppermute | solution.py:218
  191.9 14.6 %collective-permute-done.29 = bf16[128,1024]{1,0:T(8,128)(2,1)S(1)} collective-permute-done((bf16[128,1024]{1,0:T(8,128)(2,1)S(1)}, bf16[128,1024]{1,0:T(8,128)(2,1)S(1)}, u32[]{:S(2)}, u32[]{:S(2)}) %collective-permute-start.29) | collective-permute-done | bytes 262176 | tf_op jit(solution)/shard_map/ppermute | solution.py:218
  206.7 9.5 %collective-permute-done.16 = bf16[128,1024]{1,0:T(8,128)(2,1)S(1)} collective-permute-done((bf16[128,1024]{1,0:T(8,128)(2,1)S(1)}, bf16[128,1024]{1,0:T(8,128)(2,1)S(1)}, u32[]{:S(2)}, u32[]{:S(2)}) %collective-permute-start.16) | collective-permute-done | bytes 262176 | tf_op jit(solution)/shard_map/ppermute | solution.py:218
  (144 shorter events, 34.8 us)
Async XLA Ops:
  7.2 27.1 %collective-permute-start.4 = (bf16[512,1024]{1,0:T(8,128)(2,1)S(1)}, bf16[512,1024]{1,0:T(8,128)(2,1)S(1)}, u32[]{:S(2)}, u32[]{:S(2)}) collective-permute-start(bf16[512,1024]{1,0:T(8,128)(2,1)S(1)} %shard_map.69), channel_id=1, source_target_pairs={{0,4},{4,0},{8,12},{12,8},{1,5},{5,1},{9,13},{13,9},{2,6},{6,2},{1... | collective-permute-start | bytes 3145736 | tf_op jit(solution)/shard_map/ppermute | solution.py:213
  10.3 53.1 %collective-permute-start.13 = (bf16[512,1024]{1,0:T(8,128)(2,1)}, bf16[512,1024]{1,0:T(8,128)(2,1)}, u32[]{:S(2)}, u32[]{:S(2)}) collective-permute-start(bf16[512,1024]{1,0:T(8,128)(2,1)} %get-tuple-element.39), channel_id=1, source_target_pairs={{0,4},{4,0},{8,12},{12,8},{1,5},{5,1},{9,13},{13,9},{2,6},{6,2},{1... | collective-permute-start | bytes 3145736 | tf_op jit(solution)/shard_map/ppermute | solution.py:213
  12.7 91.1 %collective-permute-start.3 = (bf16[512,1024]{1,0:T(8,128)(2,1)S(1)}, bf16[512,1024]{1,0:T(8,128)(2,1)S(1)}, u32[]{:S(2)}, u32[]{:S(2)}) collective-permute-start(bf16[512,1024]{1,0:T(8,128)(2,1)S(1)} %get-tuple-element.35.refs_10_), channel_id=1, source_target_pairs={{0,1},{1,0},{2,3},{3,2},{4,5},{5,4},{6,7},{7,6},{8,9},{9,8},{10,11... | collective-permute-start | bytes 3145736 | tf_op jit(solution)/shard_map/ppermute | solution.py:203
  34.2 70.1 %collective-permute-start.5 = (bf16[512,1024]{1,0:T(8,128)(2,1)S(1)}, bf16[512,1024]{1,0:T(8,128)(2,1)}, u32[]{:S(2)}, u32[]{:S(2)}) collective-permute-start(bf16[512,1024]{1,0:T(8,128)(2,1)S(1)} %collective-permute-done.4.refs_12_), channel_id=1, source_target_pairs={{0,1},{1,0},{2,3},{3,2},{4,5},{5,4},{6,7},{7,6},{8,9},{9,8},{10,11... | collective-permute-start | bytes 3145736 | tf_op jit(solution)/shard_map/ppermute | solution.py:203
  34.2 21.0 %collective-permute-start.7 = (f32[6]{0:T(128)S(1)}, f32[6]{0:T(128)S(1)}, u32[]{:S(2)}, u32[]{:S(2)}) collective-permute-start(f32[6]{0:T(128)S(1)} %copy-done.23), channel_id=1, source_target_pairs={{0,8},{4,12},{8,0},{12,4},{1,9},{5,13},{9,1},{13,5},{2,10},{6,14},... | collective-permute-start | bytes 80 | tf_op jit(solution)/shard_map/ppermute | solution.py:218
  37.3 86.8 %collective-permute-start.12 = (bf16[512,1024]{1,0:T(8,128)(2,1)}, bf16[512,1024]{1,0:T(8,128)(2,1)}, u32[]{:S(2)}, u32[]{:S(2)}) collective-permute-start(bf16[512,1024]{1,0:T(8,128)(2,1)} %get-tuple-element.38.refs_10_), channel_id=1, source_target_pairs={{0,1},{1,0},{2,3},{3,2},{4,5},{5,4},{6,7},{7,6},{8,9},{9,8},{10,11... | collective-permute-start | bytes 3145736 | tf_op jit(solution)/shard_map/ppermute | solution.py:203
  58.3 5.0 %collective-permute-start.1 = (s32[12,128]{1,0:T(8,128)S(1)}, s32[12,128]{1,0:T(8,128)S(1)}, u32[]{:S(2)}, u32[]{:S(2)}) collective-permute-start(s32[12,128]{1,0:T(8,128)S(1)} %get-tuple-element.77), channel_id=1, source_target_pairs={{0,4},{1,5},{2,6},{3,7},{4,0},{5,1},{6,2},{7,3},{8,12},{9,13},{10,... | collective-permute-start | bytes 18440 | tf_op jit(solution)/shard_map/ppermute | solution.py:231
  63.3 68.7 %collective-permute-start.14 = (bf16[512,1024]{1,0:T(8,128)(2,1)}, bf16[512,1024]{1,0:T(8,128)(2,1)}, u32[]{:S(2)}, u32[]{:S(2)}) collective-permute-start(bf16[512,1024]{1,0:T(8,128)(2,1)} %collective-permute-done.13.refs_12_), channel_id=1, source_target_pairs={{0,1},{1,0},{2,3},{3,2},{4,5},{5,4},{6,7},{7,6},{8,9},{9,8},{10,11... | collective-permute-start | bytes 3145736 | tf_op jit(solution)/shard_map/ppermute | solution.py:203
  66.1 9.2 %collective-permute-start.21 = (bf16[64,1024]{1,0:T(8,128)(2,1)S(1)}, bf16[64,1024]{1,0:T(8,128)(2,1)S(1)}, u32[]{:S(2)}, u32[]{:S(2)}) collective-permute-start(bf16[64,1024]{1,0:T(8,128)(2,1)S(1)} %get-tuple-element.66), channel_id=1, source_target_pairs={{0,8},{4,12},{8,0},{12,4},{1,9},{5,13},{9,1},{13,5},{2,10},{6,14},... | collective-permute-start | bytes 393224 | tf_op jit(solution)/shard_map/ppermute | solution.py:218
  75.2 7.7 %collective-permute-start.17 = (bf16[64,1024]{1,0:T(8,128)(2,1)S(1)}, bf16[64,1024]{1,0:T(8,128)(2,1)S(1)}, u32[]{:S(2)}, u32[]{:S(2)}) collective-permute-start(bf16[64,1024]{1,0:T(8,128)(2,1)S(1)} %get-tuple-element.67), channel_id=1, source_target_pairs={{0,8},{4,12},{8,0},{12,4},{1,9},{5,13},{9,1},{13,5},{2,10},{6,14},... | collective-permute-start | bytes 393224 | tf_op jit(solution)/shard_map/ppermute | solution.py:218
  82.9 8.2 %collective-permute-start.8 = (bf16[64,1024]{1,0:T(8,128)(2,1)S(1)}, bf16[64,1024]{1,0:T(8,128)(2,1)S(1)}, u32[]{:S(2)}, u32[]{:S(2)}) collective-permute-start(bf16[64,1024]{1,0:T(8,128)(2,1)S(1)} %get-tuple-element.69), channel_id=1, source_target_pairs={{0,8},{4,12},{8,0},{12,4},{1,9},{5,13},{9,1},{13,5},{2,10},{6,14},... | collective-permute-start | bytes 393224 | tf_op jit(solution)/shard_map/ppermute | solution.py:218
  91.1 5.5 %collective-permute-start.23 = (bf16[64,1024]{1,0:T(8,128)(2,1)S(1)}, bf16[64,1024]{1,0:T(8,128)(2,1)}, u32[]{:S(2)}, u32[]{:S(2)}) collective-permute-start(bf16[64,1024]{1,0:T(8,128)(2,1)S(1)} %collective-permute-done.21.refs_6_), channel_id=1, source_target_pairs={{0,2},{1,3},{2,0},{3,1},{4,6},{5,7},{6,4},{7,5},{8,10},{9,11},{10,... | collective-permute-start | bytes 393224 | tf_op jit(solution)/shard_map/ppermute | solution.py:206
  96.7 5.0 %collective-permute-start.22 = (bf16[64,1024]{1,0:T(8,128)(2,1)S(1)}, bf16[64,1024]{1,0:T(8,128)(2,1)S(1)}, u32[]{:S(2)}, u32[]{:S(2)}) collective-permute-start(bf16[64,1024]{1,0:T(8,128)(2,1)S(1)} %collective-permute-done.21.refs_6_), channel_id=1, source_target_pairs={{0,16},{16,0},{1,17},{17,1},{2,18},{18,2},{3,19},{19,3},{4,20},{20... | collective-permute-start | bytes 393224 | tf_op jit(solution)/shard_map/ppermute | solution.py:221
  102.3 12.0 %collective-permute-start.19 = (bf16[64,1024]{1,0:T(8,128)(2,1)S(1)}, bf16[64,1024]{1,0:T(8,128)(2,1)}, u32[]{:S(2)}, u32[]{:S(2)}) collective-permute-start(bf16[64,1024]{1,0:T(8,128)(2,1)S(1)} %collective-permute-done.17.refs_6_), channel_id=1, source_target_pairs={{0,2},{1,3},{2,0},{3,1},{4,6},{5,7},{6,4},{7,5},{8,10},{9,11},{10,... | collective-permute-start | bytes 393224 | tf_op jit(solution)/shard_map/ppermute | solution.py:206
  103.8 11.2 %collective-permute-start.10 = (bf16[64,1024]{1,0:T(8,128)(2,1)S(1)}, bf16[64,1024]{1,0:T(8,128)(2,1)}, u32[]{:S(2)}, u32[]{:S(2)}) collective-permute-start(bf16[64,1024]{1,0:T(8,128)(2,1)S(1)} %collective-permute-done.8.refs_6_), channel_id=1, source_target_pairs={{0,2},{1,3},{2,0},{3,1},{4,6},{5,7},{6,4},{7,5},{8,10},{9,11},{10,... | collective-permute-start | bytes 393224 | tf_op jit(solution)/shard_map/ppermute | solution.py:206
  104.3 19.2 %collective-permute-start.24 = (bf16[64,1024]{1,0:T(8,128)(2,1)}, bf16[64,1024]{1,0:T(8,128)(2,1)}, u32[]{:S(2)}, u32[]{:S(2)}) collective-permute-start(bf16[64,1024]{1,0:T(8,128)(2,1)} %collective-permute-done.23.refs_8_), channel_id=1, source_target_pairs={{0,16},{16,0},{1,17},{17,1},{2,18},{18,2},{3,19},{19,3},{4,20},{20... | collective-permute-start | bytes 393224 | tf_op jit(solution)/shard_map/ppermute | solution.py:221
  114.3 23.4 %collective-permute-start.18 = (bf16[64,1024]{1,0:T(8,128)(2,1)S(1)}, bf16[64,1024]{1,0:T(8,128)(2,1)S(1)}, u32[]{:S(2)}, u32[]{:S(2)}) collective-permute-start(bf16[64,1024]{1,0:T(8,128)(2,1)S(1)} %collective-permute-done.17.refs_6_), channel_id=1, source_target_pairs={{0,16},{16,0},{1,17},{17,1},{2,18},{18,2},{3,19},{19,3},{4,20},{20... | collective-permute-start | bytes 393224 | tf_op jit(solution)/shard_map/ppermute | solution.py:221
  114.9 22.8 %collective-permute-start.20 = (bf16[64,1024]{1,0:T(8,128)(2,1)}, bf16[64,1024]{1,0:T(8,128)(2,1)S(1)}, u32[]{:S(2)}, u32[]{:S(2)}) collective-permute-start(bf16[64,1024]{1,0:T(8,128)(2,1)} %collective-permute-done.19.refs_8_), channel_id=1, source_target_pairs={{0,16},{16,0},{1,17},{17,1},{2,18},{18,2},{3,19},{19,3},{4,20},{20... | collective-permute-start | bytes 393224 | tf_op jit(solution)/shard_map/ppermute | solution.py:221
  123.5 19.8 %collective-permute-start.9 = (bf16[64,1024]{1,0:T(8,128)(2,1)S(1)}, bf16[64,1024]{1,0:T(8,128)(2,1)S(1)}, u32[]{:S(2)}, u32[]{:S(2)}) collective-permute-start(bf16[64,1024]{1,0:T(8,128)(2,1)S(1)} %collective-permute-done.8.refs_6_), channel_id=1, source_target_pairs={{0,16},{16,0},{1,17},{17,1},{2,18},{18,2},{3,19},{19,3},{4,20},{20... | collective-permute-start | bytes 393224 | tf_op jit(solution)/shard_map/ppermute | solution.py:221
  124.1 19.2 %collective-permute-start.11 = (bf16[64,1024]{1,0:T(8,128)(2,1)}, bf16[64,1024]{1,0:T(8,128)(2,1)S(1)}, u32[]{:S(2)}, u32[]{:S(2)}) collective-permute-start(bf16[64,1024]{1,0:T(8,128)(2,1)} %collective-permute-done.10.refs_8_), channel_id=1, source_target_pairs={{0,16},{16,0},{1,17},{17,1},{2,18},{18,2},{3,19},{19,3},{4,20},{20... | collective-permute-start | bytes 393224 | tf_op jit(solution)/shard_map/ppermute | solution.py:221
  152.8 32.0 %collective-permute-start.30 = (bf16[128,1024]{1,0:T(8,128)(2,1)S(1)}, bf16[128,1024]{1,0:T(8,128)(2,1)S(1)}, u32[]{:S(2)}, u32[]{:S(2)}) collective-permute-start(bf16[128,1024]{1,0:T(8,128)(2,1)S(1)} %copy-done.16), channel_id=1, source_target_pairs={{0,2},{1,3},{2,0},{3,1},{4,6},{5,7},{6,4},{7,5},{8,10},{9,11},{10,... | collective-permute-start | bytes 786440 | tf_op jit(solution)/shard_map/ppermute | solution.py:206
  154.5 37.3 %collective-permute-start.27 = (bf16[128,1024]{1,0:T(8,128)(2,1)S(1)}, bf16[128,1024]{1,0:T(8,128)(2,1)S(1)}, u32[]{:S(2)}, u32[]{:S(2)}) collective-permute-start(bf16[128,1024]{1,0:T(8,128)(2,1)S(1)} %copy-done.14), channel_id=1, source_target_pairs={{0,2},{1,3},{2,0},{3,1},{4,6},{5,7},{6,4},{7,5},{8,10},{9,11},{10,... | collective-permute-start | bytes 786440 | tf_op jit(solution)/shard_map/ppermute | solution.py:206
  154.9 51.7 %collective-permute-start.6 = (bf16[128,1024]{1,0:T(8,128)(2,1)S(1)}, bf16[128,1024]{1,0:T(8,128)(2,1)S(1)}, u32[]{:S(2)}, u32[]{:S(2)}) collective-permute-start(bf16[128,1024]{1,0:T(8,128)(2,1)S(1)} %copy-done.12), channel_id=1, source_target_pairs={{0,2},{1,3},{2,0},{3,1},{4,6},{5,7},{6,4},{7,5},{8,10},{9,11},{10,... | collective-permute-start | bytes 786440 | tf_op jit(solution)/shard_map/ppermute | solution.py:206
  156.5 21.9 %collective-permute-start.31 = (bf16[128,1024]{1,0:T(8,128)(2,1)S(1)}, bf16[128,1024]{1,0:T(8,128)(2,1)S(1)}, u32[]{:S(2)}, u32[]{:S(2)}) collective-permute-start(bf16[128,1024]{1,0:T(8,128)(2,1)S(1)} %get-tuple-element.55), channel_id=1, source_target_pairs={{0,2},{1,3},{2,0},{3,1},{4,6},{5,7},{6,4},{7,5},{8,10},{9,11},{10,... | collective-permute-start | bytes 786440 | tf_op jit(solution)/shard_map/ppermute | solution.py:206
  157.3 24.0 %collective-permute-start.28 = (bf16[128,1024]{1,0:T(8,128)(2,1)S(1)}, bf16[128,1024]{1,0:T(8,128)(2,1)S(1)}, u32[]{:S(2)}, u32[]{:S(2)}) collective-permute-start(bf16[128,1024]{1,0:T(8,128)(2,1)S(1)} %get-tuple-element.51), channel_id=1, source_target_pairs={{0,2},{1,3},{2,0},{3,1},{4,6},{5,7},{6,4},{7,5},{8,10},{9,11},{10,... | collective-permute-start | bytes 786440 | tf_op jit(solution)/shard_map/ppermute | solution.py:206
  178.4 6.4 %collective-permute-start.15 = (bf16[128,1024]{1,0:T(8,128)(2,1)S(1)}, bf16[128,1024]{1,0:T(8,128)(2,1)S(1)}, u32[]{:S(2)}, u32[]{:S(2)}) collective-permute-start(bf16[128,1024]{1,0:T(8,128)(2,1)S(1)} %get-tuple-element.41), channel_id=1, source_target_pairs={{0,2},{1,3},{2,0},{3,1},{4,6},{5,7},{6,4},{7,5},{8,10},{9,11},{10,... | collective-permute-start | bytes 786440 | tf_op jit(solution)/shard_map/ppermute | solution.py:206
  181.2 10.3 %collective-permute-start.32 = (bf16[128,1024]{1,0:T(8,128)(2,1)S(1)}, bf16[128,1024]{1,0:T(8,128)(2,1)S(1)}, u32[]{:S(2)}, u32[]{:S(2)}) collective-permute-start(bf16[128,1024]{1,0:T(8,128)(2,1)S(1)} %add_convert_fusion), channel_id=1, source_target_pairs={{0,8},{4,12},{8,0},{12,4},{1,9},{5,13},{9,1},{13,5},{2,10},{6,14},... | collective-permute-start | bytes 786440 | tf_op jit(solution)/shard_map/ppermute | solution.py:218
  184.8 31.9 %collective-permute-start.37 = (f32[6,160]{1,0:T(8,128)S(1)}, f32[6,160]{1,0:T(8,128)S(1)}, u32[]{:S(2)}, u32[]{:S(2)}) collective-permute-start(f32[6,160]{1,0:T(8,128)S(1)} %get-tuple-element.74), channel_id=1, source_target_pairs={{0,5},{1,4},{2,7},{3,6},{4,1},{5,0},{6,3},{7,2},{8,13},{9,12},{10,... | collective-permute-start | bytes 11528 | tf_op jit(solution)/shard_map/ppermute | solution.py:231
  184.9 31.9 %collective-permute-start.36 = (f32[6,160]{1,0:T(8,128)S(1)}, f32[6,160]{1,0:T(8,128)S(1)}, u32[]{:S(2)}, u32[]{:S(2)}) collective-permute-start(f32[6,160]{1,0:T(8,128)S(1)} %get-tuple-element.75), channel_id=1, source_target_pairs={{0,4},{1,5},{2,6},{3,7},{4,0},{5,1},{6,2},{7,3},{8,12},{9,13},{10,... | collective-permute-start | bytes 11528 | tf_op jit(solution)/shard_map/ppermute | solution.py:231
  191.6 14.9 %collective-permute-start.29 = (bf16[128,1024]{1,0:T(8,128)(2,1)S(1)}, bf16[128,1024]{1,0:T(8,128)(2,1)S(1)}, u32[]{:S(2)}, u32[]{:S(2)}) collective-permute-start(bf16[128,1024]{1,0:T(8,128)(2,1)S(1)} %add_convert_fusion.1), channel_id=1, source_target_pairs={{0,8},{4,12},{8,0},{12,4},{1,9},{5,13},{9,1},{13,5},{2,10},{6,14},... | collective-permute-start | bytes 786440 | tf_op jit(solution)/shard_map/ppermute | solution.py:218
  191.8 25.0 %collective-permute-start.35 = (f32[6,160]{1,0:T(8,128)S(1)}, f32[6,160]{1,0:T(8,128)S(1)}, u32[]{:S(2)}, u32[]{:S(2)}) collective-permute-start(f32[6,160]{1,0:T(8,128)S(1)} %get-tuple-element.76), channel_id=1, source_target_pairs={{0,1},{1,0},{2,3},{3,2},{4,5},{5,4},{6,7},{7,6},{8,9},{9,8},{10,11... | collective-permute-start | bytes 11528 | tf_op jit(solution)/shard_map/ppermute | solution.py:231
  206.5 9.7 %collective-permute-start.16 = (bf16[128,1024]{1,0:T(8,128)(2,1)S(1)}, bf16[128,1024]{1,0:T(8,128)(2,1)S(1)}, u32[]{:S(2)}, u32[]{:S(2)}) collective-permute-start(bf16[128,1024]{1,0:T(8,128)(2,1)S(1)} %add_convert_fusion.2), channel_id=1, source_target_pairs={{0,8},{4,12},{8,0},{12,4},{1,9},{5,13},{9,1},{13,5},{2,10},{6,14},... | collective-permute-start | bytes 786440 | tf_op jit(solution)/shard_map/ppermute | solution.py:218
  (30 other events, 276.9 us)

commit v2 on v1

v2 whole, which is shorter than its diff:
```python
import functools

import jax
import jax.numpy as jnp
from jax import lax
from jax.experimental import pallas as pl
from jax.experimental.pallas import tpu as pltpu
from jax.sharding import PartitionSpec as P

prior_mass = 1.0
cores = 2
wire = jnp.bfloat16
vmem_limit = 16 * 1024 * 1024
anywhere = pl.BlockSpec(memory_space=pl.ANY)
cheap = pl.CostEstimate(flops=1, bytes_accessed=1, transcendentals=0)
dear = pl.CostEstimate(flops=20_000_000_000, bytes_accessed=1, transcendentals=0)
meta_extra = 16


def _hot(flat_row, segment, own_slots):
    rows = flat_row.shape[1]
    slot = lax.broadcasted_iota(jnp.int32, (own_slots, rows), 0) + segment * own_slots
    return jnp.where(slot == flat_row, 1.0, 0.0).astype(jnp.bfloat16)


def _pick(flat_row, meta, frames_ref, segment, out_ref):
    own_slots = out_ref.shape[0] - meta_extra
    hot = _hot(flat_row, segment, own_slots)
    out_ref[pl.ds(0, own_slots)] = jnp.dot(
        hot, frames_ref[...], preferred_element_type=jnp.float32
    ).astype(jnp.bfloat16)
    out_ref[pl.ds(own_slots, meta_extra)] = jnp.zeros((meta_extra, out_ref.shape[1]), jnp.bfloat16)
    out_ref[pl.ds(own_slots, meta_extra), pl.ds(0, 128)] = meta[
        segment * meta_extra : (segment + 1) * meta_extra
    ].astype(jnp.bfloat16)


def _place_kernel(
    cells_local, window, own_slots, segments, rel_ref, frames_ref, flat_ref, off_ref, meta_ref, *outs
):
    rows = rel_ref.shape[1]
    lines = meta_ref.shape[0]
    rel = rel_ref[...]
    line = lax.broadcasted_iota(jnp.int32, (lines, rows), 0)
    base = (line // meta_extra) * meta_extra
    segment = rel // meta_extra
    hits = jnp.where(rel == line, 1, 0)
    lane = lax.broadcasted_iota(jnp.int32, (lines, rows), 1)
    running = hits
    step = 1
    while step < rows:
        running += jnp.where(lane >= step, pltpu.roll(running, step, 1), 0)
        step *= 2
    count = jnp.sum(hits, axis=1, keepdims=True)
    start = jnp.sum(jnp.where((rel < line) & (rel >= base), 1, 0), axis=1, keepdims=True)
    first = jnp.minimum((start >> 4) << 4, own_slots - window)
    position = jnp.sum(hits * (running + (start - 1)), axis=0, keepdims=True)
    flat = segment * own_slots + position
    flat_ref[...] = flat
    off_ref[...] = jnp.sum(hits * (running + (start - first - 1)), axis=0, keepdims=True)
    column = lax.broadcasted_iota(jnp.int32, meta_ref.shape, 1)
    meta = jnp.where(
        column == 0,
        first >> 4,
        jnp.where(column == 1, start - first, jnp.where(column == 2, count, 0)),
    ).astype(jnp.float32)
    meta_ref[...] = meta
    for g, out_ref in zip(segments, outs, strict=True):
        _pick(flat, meta, frames_ref, g, out_ref)


def _pick_kernel(segments, separate, flat_ref, meta_ref, frames_ref, *outs):
    flat, meta = flat_ref[...], meta_ref[...]
    size = outs[0].shape[0] // (1 if separate else len(segments))
    for n, g in enumerate(segments):
        target = outs[n] if separate else outs[0].at[pl.ds(n * size, size)]
        _pick(flat, meta, frames_ref, g, target)


def _split(lines, rows):
    high = lines.astype(jnp.bfloat16).astype(jnp.float32)
    middle = (lines - high).astype(jnp.bfloat16).astype(jnp.float32)
    rest = jnp.zeros((rows - 3 * lines.shape[0], lines.shape[1]), jnp.float32)
    return jnp.concatenate([high, middle, lines - high - middle, rest], axis=0)


def _round(value):
    return lax.reduce_precision(value, 8, 7)


def _note_kernel(score_ref, out_ref):
    out_ref[...] = score_ref[:, 0]


def _prior_kernel(group_count, code_ref, *refs):
    for g in range(group_count):
        size = refs[g].shape[1]
        refs[-1][:, g * size : (g + 1) * size] = refs[g][...].astype(jnp.float32)


def _cell_kernel(sources, window, pieces, share, steps, per_core, begin, span, bases, earlier, tail, *refs):
    code_ref, sharp_ref = refs[:2]
    refs = refs[2:]
    centre_refs, refs = refs[:pieces], refs[pieces:]
    row_refs, refs = refs[:sources], refs[sources:]
    earlier_refs, refs = refs[:earlier], refs[earlier:]
    keep_ref, mass_ref, score_ref = refs[:3]
    send_refs, (held, sems, meta_low, meta_wide, meta_ref, meta_sems) = refs[3:-6], refs[-6:]
    step = pl.program_id(0)

    def entry(n, at_step, field):
        return meta_ref[n * meta_extra + (n % cores) * per_core + begin + at_step, field]

    def copies(at_step, half):
        found = []
        for n in range(sources):
            first = entry(n, at_step, 0) * 16 + bases[n]
            found.append(
                pltpu.make_async_copy(
                    row_refs[n].at[pl.ds(pl.multiple_of(first, 16), window)],
                    held.at[half, pl.ds(n * window, window)],
                    sems.at[half, n],
                )
            )
        return found

    now = lax.rem(step, 2)

    @pl.when(step == 0)
    def _():
        lines = [
            pltpu.make_async_copy(
                row_refs[n].at[pl.ds(bases[n] + span - meta_extra, meta_extra), pl.ds(0, 128)],
                meta_low.at[pl.ds(n * meta_extra, meta_extra)],
                meta_sems.at[n],
            )
            for n in range(sources)
        ]
        for copy in lines:
            copy.start()
        for copy in lines:
            copy.wait()
        meta_wide[...] = meta_low[...].astype(jnp.float32).astype(jnp.int32)
        to_scalars = pltpu.make_async_copy(meta_wide, meta_ref, meta_sems.at[sources])
        to_scalars.start()
        to_scalars.wait()
        for copy in copies(0, 0):
            copy.start()

    if steps > 1:

        @pl.when(step + 1 < steps)
        def _():
            for copy in copies(step + 1, 1 - now):
                copy.start()

    centre = jnp.concatenate([c[0] for c in centre_refs], axis=0)
    wide = centre.astype(jnp.float32)
    half_norm = 0.5 * jnp.sum(wide * wide, axis=1, keepdims=True)
    slot = lax.broadcasted_iota(jnp.int32, (1, sources * window), 1)
    valid = slot < 0
    for n in range(sources):
        low = n * window + entry(n, step, 1)
        valid = valid | ((slot >= low) & (slot < low + entry(n, step, 2)))
    for copy in copies(step, now):
        copy.wait()
    chosen = held[now]
    products = lax.dot_general(
        centre, chosen, (((1,), (1,)), ((), ())), preferred_element_type=jnp.float32
    )
    scores = sharp_ref[code_ref[2] * per_core + begin + step] * (products - half_norm)
    top = jnp.max(scores, axis=0, keepdims=True)
    exponent = jnp.exp(scores - top)
    total = jnp.sum(exponent, axis=0, keepdims=True)
    score_ref[0] = jnp.broadcast_to(
        jnp.where(valid, top + jnp.log(total), 0.0), score_ref.shape[1:]
    )
    resp = exponent * jnp.where(valid, 1.0 / total, 0.0)
    mass = jnp.sum(resp, axis=1, keepdims=True)
    mass_ref[step] = jnp.broadcast_to(mass, (mass.shape[0], 128)).T[: mass_ref.shape[1]]
    low = resp.astype(jnp.bfloat16)
    numer = jnp.dot(low, chosen, preferred_element_type=jnp.float32)
    keep_ref[0] = numer[:share]
    for n, ref in enumerate(send_refs):
        at_row = pl.multiple_of(step * share, share)
        ref[pl.ds(at_row, share)] = numer[(n + 1) * share : (n + 2) * share].astype(ref.dtype)

    if tail:

        @pl.when(step == steps - 1)
        def _():
            lines = [r[i, :1] for r in (*earlier_refs, mass_ref) for i in range(r.shape[0])]
            for n, ref in enumerate(send_refs):
                part = [v[:, (n + 1) * share : (n + 2) * share] for v in lines]
                rows = _split(jnp.concatenate(part, axis=0), tail)
                ref[pl.ds(steps * share, tail)] = jnp.zeros((tail, ref.shape[1]), ref.dtype)
                ref[pl.ds(steps * share, tail), pl.ds(0, share)] = rows.astype(ref.dtype)


def _pack_kernel(sources, window, *refs):
    line = 0
    for score_ref in refs[:-sources]:
        size = score_ref.shape[0]
        for n, out_ref in enumerate(refs[-sources:]):
            out_ref[line : line + size] = score_ref[:, n * window : (n + 1) * window]
        line += size


def _score_kernel(cells, window, rel_ref, off_ref, values_ref, out_ref):
    rows = rel_ref.shape[1]
    hot = jnp.where(
        lax.broadcasted_iota(jnp.int32, (window, rows), 0) == off_ref[...], 1.0, 0.0
    ).astype(jnp.bfloat16)
    rest = values_ref[...]
    mine = lax.broadcasted_iota(jnp.int32, (cells, rows), 0) == rel_ref[...]
    total = jnp.zeros((cells, rows), jnp.float32)
    for _ in range(3):
        term = rest.astype(jnp.bfloat16)
        rest = rest - term.astype(jnp.float32)
        total += jnp.dot(term, hot, preferred_element_type=jnp.float32)
    out_ref[...] = jnp.sum(jnp.where(mine, total, 0.0), axis=0, keepdims=True)


def _after(value, *others):
    return lax.optimization_barrier((value, *others))[0]


def _params():
    return pltpu.CompilerParams(vmem_limit_bytes=vmem_limit)


def _cell_call(code, sharp, centre_in, row_blocks, window, per_core, begin, steps, kids, share, sends, earlier, tail):
    sources = len(row_blocks)
    row_arrays, bases = zip(*row_blocks, strict=True)
    width = row_arrays[0].shape[1]
    arrays, specs = zip(*centre_in, strict=True)
    span = row_arrays[0].shape[0] // 2
    rows = sources * window
    out_shape = [
        jax.ShapeDtypeStruct((steps, share, width), jnp.float32),
        jax.ShapeDtypeStruct((steps, 8, kids), jnp.float32),
        jax.ShapeDtypeStruct((steps, 8, rows), jnp.float32),
    ] + [jax.ShapeDtypeStruct((steps * share + tail, width), wire)] * sends
    fixed = lambda shape: pl.BlockSpec(shape, lambda n, *_: (0,) * len(shape))
    moving = lambda shape: pl.BlockSpec((1, *shape[1:]), lambda n, *_: (n, 0, 0))
    return pl.pallas_call(
        functools.partial(
            _cell_kernel, sources, window, len(arrays), share, steps, per_core, begin, span, bases, len(earlier), tail
        ),
        grid_spec=pltpu.PrefetchScalarGridSpec(
            num_scalar_prefetch=2,
            grid=(steps,),
            in_specs=list(specs) + [anywhere] * sources + [fixed(v.shape) for v in earlier],
            out_specs=[
                (moving if n in (0, 2) else fixed)(o.shape) for n, o in enumerate(out_shape)
            ],
            scratch_shapes=[
                pltpu.VMEM((min(steps, 2), rows, width), jnp.bfloat16),
                pltpu.SemaphoreType.DMA((min(steps, 2), sources)),
                pltpu.VMEM((sources * meta_extra, 128), jnp.bfloat16),
                pltpu.VMEM((sources * meta_extra, 128), jnp.int32),
                pltpu.SMEM((sources * meta_extra, 128), jnp.int32),
                pltpu.SemaphoreType.DMA((sources + 1,)),
            ],
        ),
        out_shape=out_shape,
        compiler_params=_params(),
        cost_estimate=cheap,
    )(code, sharp, *arrays, *row_arrays, *earlier)


def on_device(frames, labels, centroids, sharpness):
    cell_count = lax.axis_size("cell")
    frame_count = lax.axis_size("frame")
    group_count = 2
    cells_local, kids, width = centroids.shape
    rows = frames.shape[0]
    cells_total = cells_local * cell_count
    half = cell_count // 2
    chips = frame_count // cores
    per_core = cells_local // cores
    cell_cap = 3 * rows // cells_total
    own_slots = 2 * rows // cell_count
    sources = half * cores
    window = -(-(cell_cap + 16) // 16) * 16
    while sources * window % 128:
        window += 16
    window = min(window, own_slots)
    share = kids // chips
    piece = share // group_count

    z = lax.axis_index("cell")
    j = lax.axis_index("frame")
    y = lax.axis_index("groups")
    x, k = j // cores, j % cores
    p, h = z % half, z // half

    def at(zz, xx, kk):
        return zz * frame_count + xx * cores + kk

    def hop_core(v):
        return lax.ppermute(v, "frame", [(i, i ^ 1) for i in range(frame_count)])

    def hop_chip(v, s):
        return lax.ppermute(
            v,
            "frame",
            [(a * cores + c, (a + s) % chips * cores + c) for a in range(chips) for c in range(cores)],
        )

    def hop_member(v, s):
        return lax.ppermute(
            v, "cell", [(b * half + i, b * half + (i + s) % half) for b in range(2) for i in range(half)]
        )

    def hop_partner(v):
        return lax.ppermute(v, "cell", [(i, (i + half) % cell_count) for i in range(cell_count)])

    def hop_group(v):
        return lax.ppermute(v, "groups", [(i, 1 - i) for i in range(2)])

    def hop_any(v, s, kk):
        pairs = [
            (at(b * half + i, a, c), at(b * half + (i + s) % half, a, c ^ kk))
            for b in range(2)
            for i in range(half)
            for a in range(chips)
            for c in range(cores)
        ]
        return lax.ppermute(v, ("cell", "frame"), pairs)

    parts = [(0, 1), (1, per_core - 1)]
    foreign_sharp = hop_partner(sharpness)
    first = hop_partner(
        lax.dynamic_slice(
            centroids,
            (k * per_core, (x * group_count + y) * piece, 0),
            (per_core, piece, width),
        )
    )
    by_chip = [first] + [hop_chip(first, -s) for s in range(1, chips)]
    foreign_pieces = [v for c in by_chip for v in (c, hop_group(c))]
    around = by_chip[1:] + foreign_pieces[1:2]

    label = labels.reshape(1, rows)
    owner, local = label // cells_local, label % cells_local
    member = (owner % half - p + half) % half
    foreign = (owner // half != h).astype(jnp.int32)
    other = (local // per_core) ^ k
    rel = (member * 2 + foreign) * meta_extra + other * per_core + local % per_core

    seg = lambda s, t: s * 2 + t
    first_segs = [seg(s, 1) for s in range(1, half)]
    next_segs = [seg(s, 0) for s in range(1, half)]
    last_segs = [seg(0, 1), seg(0, 0)]
    span = own_slots + meta_extra
    block = jax.ShapeDtypeStruct((span, width), jnp.bfloat16)
    lines = cell_count * meta_extra
    flat, off, meta, *blocks = pl.pallas_call(
        functools.partial(_place_kernel, cells_local, window, own_slots, first_segs),
        out_shape=[
            jax.ShapeDtypeStruct((1, rows), jnp.int32),
            jax.ShapeDtypeStruct((1, rows), jnp.int32),
            jax.ShapeDtypeStruct((lines, 128), jnp.float32),
        ]
        + [block] * len(first_segs),
        compiler_params=_params(),
        cost_estimate=dear,
    )(rel, frames)
    segments = dict(zip(first_segs, blocks, strict=True))

    blocks = pl.pallas_call(
        functools.partial(_pick_kernel, next_segs, len(next_segs)),
        out_shape=[block] * len(next_segs),
        compiler_params=_params(),
        cost_estimate=dear,
    )(_after(flat, first), meta, frames)
    segments.update(zip(next_segs, blocks, strict=True))
    here = pl.pallas_call(
        functools.partial(_pick_kernel, last_segs, 0),
        out_shape=[jax.ShapeDtypeStruct((2 * span, width), jnp.bfloat16)],
        compiler_params=_params(),
        cost_estimate=dear,
    )(_after(flat, *blocks, foreign_sharp, *around), meta, frames)[0]

    here_other = hop_core(here)
    received = {t: [hop_member(segments[seg(s, t)], s) for s in range(1, half)] for t in (1, 0)}

    def held_of(t, *gate):
        base = 0 if t else span
        held = [(here, base), (here_other, base)]
        for v in received[t]:
            v = _after(v, *gate)
            held += [(v, 0), (hop_core(v), 0)]
        return held

    held = {1: held_of(1, *around)}

    code = jnp.stack([x, y, k]).astype(jnp.int32)
    tail = -(-3 * per_core // 16) * 16

    def masses_in(rows):
        rows = rows[:, :share].astype(jnp.float32)
        return sum(rows[n * per_core : (n + 1) * per_core] for n in range(3))

    def over_chips(result, steps, earlier, extra):
        keep, mass, _, *sends = result
        mass = jnp.concatenate([*earlier, mass])[:, 0, :share]
        for s in range(1, chips):
            got = hop_chip(sends[s - 1], s)
            keep = keep + got[: steps * share].reshape(keep.shape).astype(jnp.float32)
            if extra:
                mass = mass + masses_in(got[steps * share :])
        return keep, mass

    results, totals, masses, theirs, notes = [], [], [], [], []
    for t, begin, size in [(1, *part) for part in parts] + [(0, 0, per_core)]:
        code_here = _after(code, notes[-1] if t else totals[1]) if results else code
        if not t:
            held[0] = held_of(0, totals[0])
        centre_in = []
        for s in range(chips):
            for g in range(group_count):
                if t:
                    spec = pl.BlockSpec((1, piece, width), lambda n, *_, o=begin: (o + n, 0, 0))
                    centre_in.append((foreign_pieces[s * group_count + g], spec))
                else:

                    def where_from(n, c, sharp_ref, s=s, g=g, o=begin):
                        chip = lax.rem(c[0] + s, chips)
                        return c[2] * per_core + o + n, chip * group_count + lax.rem(c[1] + g, group_count), 0

                    centre_in.append((centroids, pl.BlockSpec((1, piece, width), where_from)))
        earlier = [r[1] for r in results] if t else []
        extra = 0 if t and begin + size < per_core else tail
        results.append(
            _cell_call(
                code_here, foreign_sharp if t else sharpness, centre_in, held[t], window, per_core,
                begin, size, kids, share, chips - 1, earlier if extra else [], extra,
            )
        )
        if t:
            scores = results[-1][2]
            if totals:
                scores = _after(scores, totals[0])
            notes.append(
                pl.pallas_call(
                    _note_kernel,
                    out_shape=jax.ShapeDtypeStruct((size, sources * window), jnp.float32),
                    compiler_params=_params(),
                    cost_estimate=dear,
                )(scores)
            )
        else:
            results[-1] = [*results[-1][:3], *(_after(v, theirs[0]) for v in results[-1][3:])]
        total, mass = over_chips(results[-1], size, earlier, extra)
        if t and extra:
            total = _after(total, notes[-1])
        masses.append(mass)
        if t:
            total = total.astype(wire).reshape(size * share, width)
            if extra:
                high = _round(mass)
                middle = _round(mass - high)
                terms = jnp.concatenate([high, middle, mass - high - middle])
                behind = jnp.pad(
                    terms.astype(wire), ((0, tail - terms.shape[0]), (0, width - share))
                )
                total = jnp.concatenate([total, behind])
            theirs.append(hop_partner(total))
        totals.append(total)
    theirs = [_after(v, totals[-1]) for v in theirs]
    got = jnp.concatenate([v[: size * share] for v, (_, size) in zip(theirs, parts, strict=True)])
    numer = totals[-1] + got.reshape(totals[-1].shape).astype(jnp.float32)
    mass = masses[-1] + masses_in(theirs[-1][-tail:])

    score_parts = pl.pallas_call(
        functools.partial(_pack_kernel, sources, window),
        out_shape=[jax.ShapeDtypeStruct((2 * per_core, window), jnp.float32)] * sources,
        compiler_params=_params(),
        cost_estimate=dear,
    )(*notes, results[-1][2][:, 0])

    back = {}
    for s in range(half):
        for kk in range(cores):
            n = s * cores + kk
            back[s, kk] = score_parts[n] if n == 0 else hop_any(score_parts[n], -s, kk)
    values = []
    for s in range(half):
        for t in range(2):
            at_row = 0 if t else per_core
            for kk in range(cores):
                values.append(back[s, kk][at_row : at_row + per_core])
            values.append(jnp.zeros((meta_extra - cells_local, window), jnp.float32))
    frame_score = pl.pallas_call(
        functools.partial(_score_kernel, lines, window),
        out_shape=jax.ShapeDtypeStruct((1, rows), jnp.float32),
        compiler_params=_params(),
        cost_estimate=dear,
    )(rel, off, jnp.concatenate(values, axis=0)).reshape(rows)

    def prior_from(n, c, g=0):
        return c[2], c[0] * group_count + lax.rem(c[1] + g, group_count), 0

    previous = pl.pallas_call(
        functools.partial(_prior_kernel, group_count),
        grid_spec=pltpu.PrefetchScalarGridSpec(
            num_scalar_prefetch=1,
            grid=(1,),
            in_specs=[
                pl.BlockSpec((per_core, piece, width), functools.partial(prior_from, g=g))
                for g in range(group_count)
            ],
            out_specs=pl.BlockSpec((per_core, share, width), lambda n, c: (0, 0, 0)),
        ),
        out_shape=jax.ShapeDtypeStruct((per_core, share, width), jnp.float32),
        compiler_params=_params(),
        cost_estimate=dear,
    )(code, *([centroids] * group_count))
    updated = (numer + prior_mass * previous) / (mass[:, :, None] + prior_mass)
    mine_at = ((k - y) % group_count) * piece
    theirs_at = ((1 - k - y) % group_count) * piece

    def both(at_kid):
        lines = jnp.pad(
            lax.dynamic_slice_in_dim(mass, at_kid, piece, 1), ((0, 0), (0, width - piece))
        )
        return lax.dynamic_slice_in_dim(updated, at_kid, piece, 1), lines

    mine, mass_mine = both(mine_at)
    theirs, mass_theirs = both(theirs_at)
    swapped = hop_core(
        jnp.concatenate([theirs, jnp.broadcast_to(mass_theirs[:, None], (per_core, 8, width))], 1)
    )

    def ordered(a, b):
        return jnp.where(k == 0, jnp.concatenate([a, b], 0), jnp.concatenate([b, a], 0))

    return (
        ordered(mine, swapped[:, :piece]),
        ordered(mass_mine[:, :piece], swapped[:, piece, :piece]),
        frame_score,
    )


def solution(mesh):
    return jax.shard_map(
        on_device,
        mesh=mesh,
        in_specs=(
            P(("groups", "cell", "frame"), None),
            P(("groups", "cell", "frame"), None),
            P("cell", None, None),
            P("cell"),
        ),
        out_specs=(
            P(("groups", "cell"), "frame", None),
            P(("groups", "cell"), "frame"),
            P(("groups", "cell", "frame")),
        ),
        check_vma=False,
    )
```

time: 221 us -> 121 us (0.55)
  waiting for transfers between devices: 125 us -> 56.7 us
  starting transfers between devices: 39 us -> 16.2 us
  Pallas kernels: 41 us -> 32.5 us
    ppermute x8 -> x4, waiting for transfers between devices: 69.5 us -> 13.6 us  [hop_partner(): lax.ppermute(v, 'cell', [(i, (i + half) % cell_count) for i in range(cell...]
    ppermute x2, waiting for transfers between devices: 21.5 us -> 2.25 us  [hop_member(): lax.ppermute(v, 'cell', [(b * half + i, b * half + (i + s) % half) for b...]
    ppermute x10 -> x4, waiting for transfers between devices: 27.7 us -> 14.8 us  [hop_chip(): lax.ppermute(v, 'frame', [(a * cores + c, (a + s) % chips * cores + c) fo...]
    ppermute x6 -> x2, waiting for transfers between devices: 2.91 us -> 12.5 us  [hop_group(): return lax.ppermute(v, 'groups', [(i, 1 - i) for i in range(2)])]
    ppermute x6 -> x3, waiting for transfers between devices: 3.06 us -> 12.1 us  [hop_any(): return lax.ppermute(v, ('cell', 'frame'), pairs)]
    ppermute x10 -> x4, starting transfers between devices: 12.4 us -> 4.26 us  [hop_chip(): lax.ppermute(v, 'frame', [(a * cores + c, (a + s) % chips * cores + c) fo...]
    pallas_call x9 -> x10, Pallas kernels: 38.2 us -> 30.5 us  [the longest x3 23.9 us: _cell_call(): pl.pallas_call(functools.partial(_cell_kernel, sources, window, len(array...]
    ppermute x6 -> x2, starting transfers between devices: 6.9 us -> 2.48 us  [hop_group(): return lax.ppermute(v, 'groups', [(i, 1 - i) for i in range(2)])]
  transfers between devices with their start and end apart: 38 -> 19, of which waited for: 18 -> 11; matrix products, arithmetic and copies ran while one was open for 3% -> 3% of each run, Pallas kernels for 14% -> 27%
where the time goes in v2:
time: 121 us
  waiting for transfers between devices  56.7 us (47%)
  Pallas kernels  32.5 us (27%)
  starting transfers between devices  16.2 us (13%)
  local copies, waits for them, and re-layouts  9.17 us (8%)
  other arithmetic  5.32 us (4%)
    pallas_call x3, Pallas kernels, _cell_call(): pl.pallas_call(functools.partial(_cell_kernel, sources, window, len(array...  23.9 us
    ppermute x4, waiting for transfers between devices, hop_chip(): lax.ppermute(v, 'frame', [(a * cores + c, (a + s) % chips * cores + c) fo...  14.8 us
    ppermute x4, waiting for transfers between devices, hop_partner(): lax.ppermute(v, 'cell', [(i, (i + half) % cell_count) for i in range(cell...  13.6 us
    ppermute x2, waiting for transfers between devices, hop_group(): return lax.ppermute(v, 'groups', [(i, 1 - i) for i in range(2)])  12.5 us
    ppermute x3, waiting for transfers between devices, hop_any(): return lax.ppermute(v, ('cell', 'frame'), pairs)  12.1 us
    unnamed x25, local copies, waits for them, and re-layouts  6.02 us
    ppermute x4, starting transfers between devices, hop_partner(): lax.ppermute(v, 'cell', [(i, (i + half) % cell_count) for i in range(cell...  4.3 us
    ppermute x4, starting transfers between devices, hop_chip(): lax.ppermute(v, 'frame', [(a * cores + c, (a + s) % chips * cores + c) fo...  4.26 us
  transfers between devices with their start and end apart: 19, of which 11 were waited for; matrix products, arithmetic and copies ran while one was open for 3% of the time, Pallas kernels for 27%

profile of v2, /device:TPU:0, one launch (start us, length us, event | category | flops | bytes accessed | tf_op | source)
XLA Modules:
  0.0 120.8 jit_solution(8841313747714175235)
XLA Ops:
  0.6 4.1 %collective-permute-start = (f32[6]{0:T(128)}, f32[6]{0:T(128)S(1)}, u32[]{:S(2)}, u32[]{:S(2)}) collective-permute-start(f32[6]{0:T(128)} %refs_1_.2), channel_id=1, source_target_pairs={{0,8},{4,12},{8,0},{12,4},{1,9},{5,13},{9,1},{13,5},{2,10},{6,14},... | collective-permute-start | bytes 80 | tf_op jit(solution)/shard_map/ppermute | solution.py:317
  4.7 1.0 constant_dynamic-slice_fusion.4
  5.9 0.8 fusion.14.rel_ref
  6.7 1.6 %copy-done.8 = bf16[1024,1024]{1,0:T(8,128)(2,1)S(1)} copy-done((bf16[1024,1024]{1,0:T(8,128)(2,1)S(1)}, bf16[1024,1024]{1,0:T(8,128)(2,1)}, u32[]{:S(2)}) %copy-start.8) | copy-done | bytes 2097176
  8.3 2.0 %shard_map.67 = (s32[1,1024]{1,0:T(1,128)S(1)}, s32[1,1024]{1,0:T(1,128)S(1)}, f32[64,128]{1,0:T(8,128)S(1)}, bf16[528,1024]{1,0:T(8,128)(2,1)S(1)}) custom-call(s32[1,1024]{1,0:T(1,128)S(1)} %fusion.14.rel_ref, bf16[1024,1024]{1,0:T(8,128)(2,1)S(1)} %copy-done.8), custom_call_target="tpu_custom_call" | custom-call | flops 20000000000 | bytes 1 | tf_op jit(solution)/shard_map/pallas_call | solution.py:359
  10.3 1.9 %collective-permute-start.6 = (bf16[528,1024]{1,0:T(8,128)(2,1)S(1)}, bf16[528,1024]{1,0:T(8,128)(2,1)}, u32[]{:S(2)}, u32[]{:S(2)}) collective-permute-start(bf16[528,1024]{1,0:T(8,128)(2,1)S(1)} %get-tuple-element.38), channel_id=1, source_target_pairs={{0,4},{4,0},{8,12},{12,8},{1,5},{5,1},{9,13},{13,9},{2,6},{6,2},{1... | collective-permute-start | bytes 3244040 | tf_op jit(solution)/shard_map/ppermute | solution.py:312
  12.2 13.6 %collective-permute-done.1.refs_2_ = bf16[3,64,1024]{2,1,0:T(8,128)(2,1)S(1)} collective-permute-done((bf16[3,64,1024]{2,1,0:T(8,128)(2,1)S(1)}, bf16[3,64,1024]{2,1,0:T(8,128)(2,1)S(1)}, u32[]{:S(2)}, u32[]{:S(2)}) %collective-permute-start.1) | collective-permute-done | bytes 393248 | tf_op jit(solution)/shard_map/ppermute | solution.py:317
  25.8 1.5 %collective-permute-start.2 = (bf16[3,64,1024]{2,1,0:T(8,128)(2,1)S(1)}, bf16[3,64,1024]{2,1,0:T(8,128)(2,1)S(1)}, u32[]{:S(2)}, u32[]{:S(2)}) collective-permute-start(bf16[3,64,1024]{2,1,0:T(8,128)(2,1)S(1)} %collective-permute-done.1.refs_2_), channel_id=1, source_target_pairs={{0,16},{16,0},{1,17},{17,1},{2,18},{18,2},{3,19},{19,3},{4,20},{20... | collective-permute-start | bytes 1179656 | tf_op jit(solution)/shard_map/ppermute | solution.py:320
  27.4 1.5 %collective-permute-start.3 = (bf16[3,64,1024]{2,1,0:T(8,128)(2,1)S(1)}, bf16[3,64,1024]{2,1,0:T(8,128)(2,1)}, u32[]{:S(2)}, u32[]{:S(2)}) collective-permute-start(bf16[3,64,1024]{2,1,0:T(8,128)(2,1)S(1)} %collective-permute-done.1.refs_2_), channel_id=1, source_target_pairs={{0,2},{1,3},{2,0},{3,1},{4,6},{5,7},{6,4},{7,5},{8,10},{9,11},{10,... | collective-permute-start | bytes 1179656 | tf_op jit(solution)/shard_map/ppermute | solution.py:305
  28.8 1.2 %shard_map.68 = bf16[528,1024]{1,0:T(8,128)(2,1)S(1)} custom-call(s32[1,1024]{1,0:T(1,128)S(1)} %get-tuple-element.37.flat_ref, f32[64,128]{1,0:T(8,128)S(1)} %get-tuple-element.36.meta_ref, bf16[1024,1024]{1,0:T(8,128)(2,1)S(1)} %copy-done.8), custom_call_target="tpu_custom_call" | custom-call | flops 20000000000 | bytes 1 | tf_op jit(solution)/shard_map/pallas_call | solution.py:372
  30.1 1.0 copy-done.9
  31.1 4.6 %collective-permute-done.2.refs_3_ = bf16[3,64,1024]{2,1,0:T(8,128)(2,1)S(1)} collective-permute-done((bf16[3,64,1024]{2,1,0:T(8,128)(2,1)S(1)}, bf16[3,64,1024]{2,1,0:T(8,128)(2,1)S(1)}, u32[]{:S(2)}, u32[]{:S(2)}) %collective-permute-start.2) | collective-permute-done | bytes 393248 | tf_op jit(solution)/shard_map/ppermute | solution.py:320
  37.1 3.7 %shard_map.69.refs_6_ = bf16[1056,1024]{1,0:T(8,128)(2,1)} custom-call(s32[1,1024]{1,0:T(1,128)S(1)} %get-tuple-element.37.flat_ref, f32[64,128]{1,0:T(8,128)S(1)} %get-tuple-element.36.meta_ref, bf16[1024,1024]{1,0:T(8,128)(2,1)S(1)} %copy-done.8), custom_call_target="tpu_custom_call" | custom-call | flops 20000000000 | bytes 1 | tf_op jit(solution)/shard_map/pallas_call | solution.py:379
  40.9 1.0 collective-permute-start.4
  41.8 1.3 %collective-permute-done.6.refs_8_ = bf16[528,1024]{1,0:T(8,128)(2,1)} collective-permute-done((bf16[528,1024]{1,0:T(8,128)(2,1)S(1)}, bf16[528,1024]{1,0:T(8,128)(2,1)}, u32[]{:S(2)}, u32[]{:S(2)}) %collective-permute-start.6) | collective-permute-done | bytes 1081376 | tf_op jit(solution)/shard_map/ppermute | solution.py:312
  43.8 1.1 copy-done.3
  44.9 7.8 %collective-permute-done.4.refs_5_ = bf16[3,64,1024]{2,1,0:T(8,128)(2,1)} collective-permute-done((bf16[3,64,1024]{2,1,0:T(8,128)(2,1)}, bf16[3,64,1024]{2,1,0:T(8,128)(2,1)}, u32[]{:S(2)}, u32[]{:S(2)}) %collective-permute-start.4) | collective-permute-done | bytes 393248 | tf_op jit(solution)/shard_map/ppermute | solution.py:320
  52.7 1.0 copy-done.2
  53.7 6.2 %shard_map.70 = (f32[1,128,1024]{2,1,0:T(8,128)S(1)}, f32[1,8,256]{2,1,0:T(8,128)S(1)}, f32[1,8,640]{2,1,0:T(8,128)S(1)}, bf16[128,1024]{1,0:T(8,128)(2,1)S(1)}) custom-call(s32[3]{0:T(128)S(1)} %pad_add_fusion.refs_0_.code_ref, f32[6]{0:T(128)S(1)} %collective-permute-done.refs_1_, bf16[3,64,1024]{2,1,0:T(8,128)(2,1)S(1)} %collective-permute-done.1.refs_2_, ...), custom_call_target="tpu_custom_call" | custom-call | flops 1 | bytes 1 | tf_op jit(solution)/shard_map/pallas_call | solution.py:246
  59.9 1.6 %collective-permute-start.9 = (bf16[128,1024]{1,0:T(8,128)(2,1)S(1)}, bf16[128,1024]{1,0:T(8,128)(2,1)S(1)}, u32[]{:S(2)}, u32[]{:S(2)}) collective-permute-start(bf16[128,1024]{1,0:T(8,128)(2,1)S(1)} %get-tuple-element.47), channel_id=1, source_target_pairs={{0,2},{1,3},{2,0},{3,1},{4,6},{5,7},{6,4},{7,5},{8,10},{9,11},{10,... | collective-permute-start | bytes 786440 | tf_op jit(solution)/shard_map/ppermute | solution.py:305
  61.5 8.1 %shard_map.72 = (f32[2,128,1024]{2,1,0:T(8,128)S(1)}, f32[2,8,256]{2,1,0:T(8,128)S(1)}, f32[2,8,640]{2,1,0:T(8,128)S(1)}, bf16[272,1024]{1,0:T(8,128)(2,1)S(1)}) custom-call(s32[3]{0:T(128)S(1)} %pad_add_fusion.refs_0_.code_ref, f32[6]{0:T(128)S(1)} %collective-permute-done.refs_1_, bf16[3,64,1024]{2,1,0:T(8,128)(2,1)S(1)} %collective-permute-done.1.refs_2_, ...), custom_call_target="tpu_custom_call" | custom-call | flops 1 | bytes 1 | tf_op jit(solution)/shard_map/pallas_call | solution.py:246
  70.4 1.0 collective-permute-done.10.refs_8_
  71.4 12.3 %collective-permute-done.8 = bf16[272,1024]{1,0:T(8,128)(2,1)S(1)} collective-permute-done((bf16[272,1024]{1,0:T(8,128)(2,1)S(1)}, bf16[272,1024]{1,0:T(8,128)(2,1)S(1)}, u32[]{:S(2)}, u32[]{:S(2)}) %collective-permute-start.8) | collective-permute-done | bytes 557088 | tf_op jit(solution)/shard_map/ppermute | solution.py:305
  83.9 0.8 pad_maximum_fusion.2
  84.8 9.6 %shard_map.74 = (f32[3,128,1024]{2,1,0:T(8,128)S(1)}, f32[3,8,256]{2,1,0:T(8,128)S(1)}, f32[3,8,640]{2,1,0:T(8,128)S(1)}, bf16[400,1024]{1,0:T(8,128)(2,1)}) custom-call(s32[3]{0:T(128)S(1)} %pad_add_fusion.refs_0_.code_ref, f32[6]{0:T(128)S(1)} %copy-done.7, bf16[6,256,1024]{2,1,0:T(8,128)(2,1)S(1)} %copy-done, bf16[6,256,1024]{2,1,0:T(8,128)(2,1)S(1)} %copy-done, ...), custom_call_target="tpu_custom_call" | custom-call | flops 1 | bytes 1 | tf_op jit(solution)/shard_map/pallas_call | solution.py:246
  95.7 2.9 %collective-permute-start.17 = (f32[6,160]{1,0:T(8,128)S(1)}, f32[6,160]{1,0:T(8,128)S(1)}, u32[]{:S(2)}, u32[]{:S(2)}) collective-permute-start(f32[6,160]{1,0:T(8,128)S(1)} %get-tuple-element.63), channel_id=1, source_target_pairs={{0,4},{1,5},{2,6},{3,7},{4,0},{5,1},{6,2},{7,3},{8,12},{9,13},{10,... | collective-permute-start | bytes 11528 | tf_op jit(solution)/shard_map/ppermute | solution.py:330
  98.8 11.9 %collective-permute-done.17 = f32[6,160]{1,0:T(8,128)S(1)} collective-permute-done((f32[6,160]{1,0:T(8,128)S(1)}, f32[6,160]{1,0:T(8,128)S(1)}, u32[]{:S(2)}, u32[]{:S(2)}) %collective-permute-start.17) | collective-permute-done | bytes 3872 | tf_op jit(solution)/shard_map/ppermute | solution.py:330
  111.4 2.0 %collective-permute-done.13 = bf16[400,1024]{1,0:T(8,128)(2,1)S(1)} collective-permute-done((bf16[400,1024]{1,0:T(8,128)(2,1)}, bf16[400,1024]{1,0:T(8,128)(2,1)S(1)}, u32[]{:S(2)}, u32[]{:S(2)}) %collective-permute-start.13) | collective-permute-done | bytes 819232 | tf_op jit(solution)/shard_map/ppermute | solution.py:305
  113.7 1.2 slice.98
  116.5 0.9 shard_map.77
  117.4 1.5 %collective-permute-done.15 = f32[3,72,1024]{2,1,0:T(8,128)S(1)} collective-permute-done((f32[3,72,1024]{2,1,0:T(8,128)S(1)}, f32[3,72,1024]{2,1,0:T(8,128)S(1)}, u32[]{:S(2)}, u32[]{:S(2)}) %collective-permute-start.15) | collective-permute-done | bytes 884768 | tf_op jit(solution)/shard_map/ppermute | solution.py:302
  119.0 1.3 %maximum_select_fusion = f32[6,64,1024]{2,1,0:T(8,128)} fusion(f32[3,64,1024]{2,1,0:T(8,128)S(1)} %slice.133, f32[3,64,1024]{2,1,0:T(8,128)S(1)} %get-tuple-element.69, pred[]{:T(512)S(6)} %eq.14), kind=kLoop, calls=%fused_computation | loop fusion | flops 1179648 | bytes 3145729 | tf_op jit(solution)/shard_map/jit(_where)/select_n | solution.py:538
  (80 shorter events, 7.8 us)
Async XLA Ops:
  0.6 30.5 %collective-permute-start = (f32[6]{0:T(128)}, f32[6]{0:T(128)S(1)}, u32[]{:S(2)}, u32[]{:S(2)}) collective-permute-start(f32[6]{0:T(128)} %refs_1_.2), channel_id=1, source_target_pairs={{0,8},{4,12},{8,0},{12,4},{1,9},{5,13},{9,1},{13,5},{2,10},{6,14},... | collective-permute-start | bytes 80 | tf_op jit(solution)/shard_map/ppermute | solution.py:317
  5.8 20.1 %collective-permute-start.1 = (bf16[3,64,1024]{2,1,0:T(8,128)(2,1)S(1)}, bf16[3,64,1024]{2,1,0:T(8,128)(2,1)S(1)}, u32[]{:S(2)}, u32[]{:S(2)}) collective-permute-start(bf16[3,64,1024]{2,1,0:T(8,128)(2,1)S(1)} %constant_dynamic-slice_fusion.4), channel_id=1, source_target_pairs={{0,8},{4,12},{8,0},{12,4},{1,9},{5,13},{9,1},{13,5},{2,10},{6,14},... | collective-permute-start | bytes 1179656 | tf_op jit(solution)/shard_map/ppermute | solution.py:317
  6.7 1.6 %copy-start.8 = (bf16[1024,1024]{1,0:T(8,128)(2,1)S(1)}, bf16[1024,1024]{1,0:T(8,128)(2,1)}, u32[]{:S(2)}) copy-start(bf16[1024,1024]{1,0:T(8,128)(2,1)} %frames_ref.5) | copy-start | bytes 6291460
  10.3 32.8 %collective-permute-start.6 = (bf16[528,1024]{1,0:T(8,128)(2,1)S(1)}, bf16[528,1024]{1,0:T(8,128)(2,1)}, u32[]{:S(2)}, u32[]{:S(2)}) collective-permute-start(bf16[528,1024]{1,0:T(8,128)(2,1)S(1)} %get-tuple-element.38), channel_id=1, source_target_pairs={{0,4},{4,0},{8,12},{12,8},{1,5},{5,1},{9,13},{13,9},{2,6},{6,2},{1... | collective-permute-start | bytes 3244040 | tf_op jit(solution)/shard_map/ppermute | solution.py:312
  25.8 9.9 %collective-permute-start.2 = (bf16[3,64,1024]{2,1,0:T(8,128)(2,1)S(1)}, bf16[3,64,1024]{2,1,0:T(8,128)(2,1)S(1)}, u32[]{:S(2)}, u32[]{:S(2)}) collective-permute-start(bf16[3,64,1024]{2,1,0:T(8,128)(2,1)S(1)} %collective-permute-done.1.refs_2_), channel_id=1, source_target_pairs={{0,16},{16,0},{1,17},{17,1},{2,18},{18,2},{3,19},{19,3},{4,20},{20... | collective-permute-start | bytes 1179656 | tf_op jit(solution)/shard_map/ppermute | solution.py:320
  27.4 9.7 %collective-permute-start.3 = (bf16[3,64,1024]{2,1,0:T(8,128)(2,1)S(1)}, bf16[3,64,1024]{2,1,0:T(8,128)(2,1)}, u32[]{:S(2)}, u32[]{:S(2)}) collective-permute-start(bf16[3,64,1024]{2,1,0:T(8,128)(2,1)S(1)} %collective-permute-done.1.refs_2_), channel_id=1, source_target_pairs={{0,2},{1,3},{2,0},{3,1},{4,6},{5,7},{6,4},{7,5},{8,10},{9,11},{10,... | collective-permute-start | bytes 1179656 | tf_op jit(solution)/shard_map/ppermute | solution.py:305
  30.1 1.0 copy-start.9
  31.1 12.0 %copy-start = (bf16[6,256,1024]{2,1,0:T(8,128)(2,1)S(1)}, bf16[6,256,1024]{2,1,0:T(8,128)(2,1)}, u32[]{:S(2)}) copy-start(bf16[6,256,1024]{2,1,0:T(8,128)(2,1)} %refs_1_.3) | copy-start | bytes 9437188
  35.7 0.8 copy-start.1
  40.8 11.9 %collective-permute-start.5 = (bf16[1056,1024]{1,0:T(8,128)(2,1)}, bf16[1056,1024]{1,0:T(8,128)(2,1)}, u32[]{:S(2)}, u32[]{:S(2)}) collective-permute-start(bf16[1056,1024]{1,0:T(8,128)(2,1)} %shard_map.69.refs_6_), channel_id=1, source_target_pairs={{0,1},{1,0},{2,3},{3,2},{4,5},{5,4},{6,7},{7,6},{8,9},{9,8},{10,11... | collective-permute-start | bytes 6488072 | tf_op jit(solution)/shard_map/ppermute | solution.py:302
  40.9 11.8 %collective-permute-start.4 = (bf16[3,64,1024]{2,1,0:T(8,128)(2,1)}, bf16[3,64,1024]{2,1,0:T(8,128)(2,1)}, u32[]{:S(2)}, u32[]{:S(2)}) collective-permute-start(bf16[3,64,1024]{2,1,0:T(8,128)(2,1)} %collective-permute-done.3.refs_4_), channel_id=1, source_target_pairs={{0,16},{16,0},{1,17},{17,1},{2,18},{18,2},{3,19},{19,3},{4,20},{20... | collective-permute-start | bytes 1179656 | tf_op jit(solution)/shard_map/ppermute | solution.py:320
  43.1 9.6 %collective-permute-start.7 = (bf16[528,1024]{1,0:T(8,128)(2,1)}, bf16[528,1024]{1,0:T(8,128)(2,1)}, u32[]{:S(2)}, u32[]{:S(2)}) collective-permute-start(bf16[528,1024]{1,0:T(8,128)(2,1)} %collective-permute-done.6.refs_8_), channel_id=1, source_target_pairs={{0,1},{1,0},{2,3},{3,2},{4,5},{5,4},{6,7},{7,6},{8,9},{9,8},{10,11... | collective-permute-start | bytes 3244040 | tf_op jit(solution)/shard_map/ppermute | solution.py:302
  43.7 1.1 copy-start.3
  44.9 26.5 %collective-permute-start.10 = (bf16[528,1024]{1,0:T(8,128)(2,1)}, bf16[528,1024]{1,0:T(8,128)(2,1)S(1)}, u32[]{:S(2)}, u32[]{:S(2)}) collective-permute-start(bf16[528,1024]{1,0:T(8,128)(2,1)} %copy-done.9), channel_id=1, source_target_pairs={{0,4},{4,0},{8,12},{12,8},{1,5},{5,1},{9,13},{13,9},{2,6},{6,2},{1... | collective-permute-start | bytes 3244040 | tf_op jit(solution)/shard_map/ppermute | solution.py:312
  52.7 1.0 copy-start.2
  59.9 10.3 %collective-permute-start.9 = (bf16[128,1024]{1,0:T(8,128)(2,1)S(1)}, bf16[128,1024]{1,0:T(8,128)(2,1)S(1)}, u32[]{:S(2)}, u32[]{:S(2)}) collective-permute-start(bf16[128,1024]{1,0:T(8,128)(2,1)S(1)} %get-tuple-element.47), channel_id=1, source_target_pairs={{0,2},{1,3},{2,0},{3,1},{4,6},{5,7},{6,4},{7,5},{8,10},{9,11},{10,... | collective-permute-start | bytes 786440 | tf_op jit(solution)/shard_map/ppermute | solution.py:305
  69.6 14.1 %collective-permute-start.8 = (bf16[272,1024]{1,0:T(8,128)(2,1)S(1)}, bf16[272,1024]{1,0:T(8,128)(2,1)S(1)}, u32[]{:S(2)}, u32[]{:S(2)}) collective-permute-start(bf16[272,1024]{1,0:T(8,128)(2,1)S(1)} %get-tuple-element.44), channel_id=1, source_target_pairs={{0,2},{1,3},{2,0},{3,1},{4,6},{5,7},{6,4},{7,5},{8,10},{9,11},{10,... | collective-permute-start | bytes 1671176 | tf_op jit(solution)/shard_map/ppermute | solution.py:305
  70.3 24.1 %collective-permute-start.12 = (bf16[128,1024]{1,0:T(8,128)(2,1)S(1)}, bf16[128,1024]{1,0:T(8,128)(2,1)S(1)}, u32[]{:S(2)}, u32[]{:S(2)}) collective-permute-start(bf16[128,1024]{1,0:T(8,128)(2,1)S(1)} %fusion.3), channel_id=1, source_target_pairs={{0,8},{4,12},{8,0},{12,4},{1,9},{5,13},{9,1},{13,5},{2,10},{6,14},... | collective-permute-start | bytes 786440 | tf_op jit(solution)/shard_map/ppermute | solution.py:317
  71.4 13.4 %collective-permute-start.11 = (bf16[528,1024]{1,0:T(8,128)(2,1)S(1)}, bf16[528,1024]{1,0:T(8,128)(2,1)S(1)}, u32[]{:S(2)}, u32[]{:S(2)}) collective-permute-start(bf16[528,1024]{1,0:T(8,128)(2,1)S(1)} %collective-permute-done.10.refs_8_), channel_id=1, source_target_pairs={{0,1},{1,0},{2,3},{3,2},{4,5},{5,4},{6,7},{7,6},{8,9},{9,8},{10,11... | collective-permute-start | bytes 3244040 | tf_op jit(solution)/shard_map/ppermute | solution.py:302
  83.7 1.1 copy-start.7
  84.8 28.9 %collective-permute-start.14 = (bf16[272,1024]{1,0:T(8,128)(2,1)}, bf16[272,1024]{1,0:T(8,128)(2,1)}, u32[]{:S(2)}, u32[]{:S(2)}) collective-permute-start(bf16[272,1024]{1,0:T(8,128)(2,1)} %pad_maximum_fusion.2), channel_id=1, source_target_pairs={{0,8},{4,12},{8,0},{12,4},{1,9},{5,13},{9,1},{13,5},{2,10},{6,14},... | collective-permute-start | bytes 1671176 | tf_op jit(solution)/shard_map/ppermute | solution.py:317
  94.4 1.2 copy-start.5
  94.4 1.2 %copy-start.10 = (bf16[128,1024]{1,0:T(8,128)(2,1)}, bf16[128,1024]{1,0:T(8,128)(2,1)S(1)}, u32[]{:S(2)}) copy-start(bf16[128,1024]{1,0:T(8,128)(2,1)S(1)} %collective-permute-done.12) | copy-start | bytes 786436
  94.4 19.0 %collective-permute-start.13 = (bf16[400,1024]{1,0:T(8,128)(2,1)}, bf16[400,1024]{1,0:T(8,128)(2,1)S(1)}, u32[]{:S(2)}, u32[]{:S(2)}) collective-permute-start(bf16[400,1024]{1,0:T(8,128)(2,1)} %get-tuple-element.55), channel_id=1, source_target_pairs={{0,2},{1,3},{2,0},{3,1},{4,6},{5,7},{6,4},{7,5},{8,10},{9,11},{10,... | collective-permute-start | bytes 2457608 | tf_op jit(solution)/shard_map/ppermute | solution.py:305
  95.6 17.8 %copy-start.6 = (f32[3,128,1024]{2,1,0:T(8,128)S(1)}, f32[3,128,1024]{2,1,0:T(8,128)}, u32[]{:S(2)}) copy-start(f32[3,128,1024]{2,1,0:T(8,128)} %copy-done.5) | copy-start | bytes 4718596
  95.6 3.2 %collective-permute-start.16 = (f32[6,160]{1,0:T(8,128)S(1)}, f32[6,160]{1,0:T(8,128)S(1)}, u32[]{:S(2)}, u32[]{:S(2)}) collective-permute-start(f32[6,160]{1,0:T(8,128)S(1)} %get-tuple-element.62), channel_id=1, source_target_pairs={{0,1},{1,0},{2,3},{3,2},{4,5},{5,4},{6,7},{7,6},{8,9},{9,8},{10,11... | collective-permute-start | bytes 11528 | tf_op jit(solution)/shard_map/ppermute | solution.py:330
  95.7 15.1 %collective-permute-start.17 = (f32[6,160]{1,0:T(8,128)S(1)}, f32[6,160]{1,0:T(8,128)S(1)}, u32[]{:S(2)}, u32[]{:S(2)}) collective-permute-start(f32[6,160]{1,0:T(8,128)S(1)} %get-tuple-element.63), channel_id=1, source_target_pairs={{0,4},{1,5},{2,6},{3,7},{4,0},{5,1},{6,2},{7,3},{8,12},{9,13},{10,... | collective-permute-start | bytes 11528 | tf_op jit(solution)/shard_map/ppermute | solution.py:330
  98.6 12.3 %collective-permute-start.18 = (f32[6,160]{1,0:T(8,128)S(1)}, f32[6,160]{1,0:T(8,128)S(1)}, u32[]{:S(2)}, u32[]{:S(2)}) collective-permute-start(f32[6,160]{1,0:T(8,128)S(1)} %get-tuple-element.64), channel_id=1, source_target_pairs={{0,5},{1,4},{2,7},{3,6},{4,1},{5,0},{6,3},{7,2},{8,13},{9,12},{10,... | collective-permute-start | bytes 11528 | tf_op jit(solution)/shard_map/ppermute | solution.py:330
  113.4 2.2 %copy-start.11 = (bf16[128,1024]{1,0:T(8,128)(2,1)S(1)}, bf16[128,1024]{1,0:T(8,128)(2,1)}, u32[]{:S(2)}) copy-start(bf16[128,1024]{1,0:T(8,128)(2,1)} %copy-done.10) | copy-start | bytes 786436
  113.7 2.1 %copy-start.4 = (f32[3,128,1024]{2,1,0:T(8,128)S(1)}, f32[3,128,1024]{2,1,0:T(8,128)}, u32[]{:S(2)}) copy-start(f32[3,128,1024]{2,1,0:T(8,128)} %copy-done.3) | copy-start | bytes 4718596
  116.4 2.5 %collective-permute-start.15 = (f32[3,72,1024]{2,1,0:T(8,128)S(1)}, f32[3,72,1024]{2,1,0:T(8,128)S(1)}, u32[]{:S(2)}, u32[]{:S(2)}) collective-permute-start(f32[3,72,1024]{2,1,0:T(8,128)S(1)} %pad_maximum_fusion), channel_id=1, source_target_pairs={{0,1},{1,0},{2,3},{3,2},{4,5},{5,4},{6,7},{7,6},{8,9},{9,8},{10,11... | collective-permute-start | bytes 2654216 | tf_op jit(solution)/shard_map/ppermute | solution.py:302

commit v3 on v2

--- a/solution.py
+++ b/solution.py
@@ -13,7 +13,8 @@
 vmem_limit = 16 * 1024 * 1024
 anywhere = pl.BlockSpec(memory_space=pl.ANY)
 cheap = pl.CostEstimate(flops=1, bytes_accessed=1, transcendentals=0)
-dear = pl.CostEstimate(flops=20_000_000_000, bytes_accessed=1, transcendentals=0)
+busy = pl.CostEstimate(flops=20_000_000_000, bytes_accessed=1, transcendentals=0)
+dear = pl.CostEstimate(flops=20_000_000_000, bytes_accessed=1_000_000_000, transcendentals=0)
 meta_extra = 16
 
 
@@ -36,7 +37,7 @@
 
 
 def _place_kernel(
-    cells_local, window, own_slots, segments, rel_ref, frames_ref, flat_ref, off_ref, meta_ref, *outs
+    per_core, reach, window, own_slots, segments, rel_ref, frames_ref, flat_ref, off_ref, meta_ref, *outs
 ):
     rows = rel_ref.shape[1]
     lines = meta_ref.shape[0]
@@ -52,8 +53,14 @@
         running += jnp.where(lane >= step, pltpu.roll(running, step, 1), 0)
         step *= 2
     count = jnp.sum(hits, axis=1, keepdims=True)
-    start = jnp.sum(jnp.where((rel < line) & (rel >= base), 1, 0), axis=1, keepdims=True)
-    first = jnp.minimum((start >> 4) << 4, own_slots - window)
+    ahead = jnp.sum(jnp.where((rel < line) & (rel >= base), 1, 0), axis=1, keepdims=True)
+    behind = jnp.sum(
+        jnp.where((rel >= line) & (rel < base + meta_extra), 1, 0), axis=1, keepdims=True
+    )
+    back = (line - base)[:, :1] >= per_core
+    start = jnp.where(back, own_slots - behind, ahead)
+    floor = jnp.where(back, own_slots - reach, 0)
+    first = jnp.minimum(((start - floor) >> 4) << 4, reach - window) + floor
     position = jnp.sum(hits * (running + (start - 1)), axis=0, keepdims=True)
     flat = segment * own_slots + position
     flat_ref[...] = flat
@@ -61,7 +68,7 @@
     column = lax.broadcasted_iota(jnp.int32, meta_ref.shape, 1)
     meta = jnp.where(
         column == 0,
-        first >> 4,
+        (first - floor) >> 4,
         jnp.where(column == 1, start - first, jnp.where(column == 2, count, 0)),
     ).astype(jnp.float32)
     meta_ref[...] = meta
@@ -92,39 +99,48 @@
     out_ref[...] = score_ref[:, 0]
 
 
+def _copy_kernel(in_ref, out_ref):
+    out_ref[...] = in_ref[...]
+
+
 def _prior_kernel(group_count, code_ref, *refs):
     for g in range(group_count):
         size = refs[g].shape[1]
         refs[-1][:, g * size : (g + 1) * size] = refs[g][...].astype(jnp.float32)
 
 
-def _cell_kernel(sources, window, pieces, share, steps, per_core, begin, span, bases, earlier, tail, *refs):
+def _cell_kernel(sources, window, reach, pieces, near, share, steps, per_core, begin, span, bases, earlier, tail, *refs):
     code_ref, sharp_ref = refs[:2]
     refs = refs[2:]
-    centre_refs, refs = refs[:pieces], refs[pieces:]
+    centre_refs, refs = (refs[:1], refs[1:]) if near else (refs[:pieces], refs[pieces:])
+    piece = share // 2
     row_refs, refs = refs[:sources], refs[sources:]
     earlier_refs, refs = refs[:earlier], refs[earlier:]
     keep_ref, mass_ref, score_ref = refs[:3]
-    send_refs, (held, sems, meta_low, meta_wide, meta_ref, meta_sems) = refs[3:-6], refs[-6:]
+    send_refs, (held, centres, sems, meta_low, meta_wide, meta_ref, meta_sems) = refs[3:-7], refs[-7:]
     step = pl.program_id(0)
-
-    def entry(n, at_step, field):
-        return meta_ref[n * meta_extra + (n % cores) * per_core + begin + at_step, field]
-
-    def copies(at_step, half):
-        found = []
-        for n in range(sources):
-            first = entry(n, at_step, 0) * 16 + bases[n]
-            found.append(
-                pltpu.make_async_copy(
-                    row_refs[n].at[pl.ds(pl.multiple_of(first, 16), window)],
-                    held.at[half, pl.ds(n * window, window)],
-                    sems.at[half, n],
-                )
+    cell = (code_ref[2] * per_core if near else 0) + begin
+    loads = []
+    for n in range(sources):
+        low = bases[n] + (0 if n % cores == 0 else span - meta_extra - reach)
+        loads.append(
+            pltpu.make_async_copy(
+                row_refs[n].at[pl.ds(low, reach)],
+                held.at[n, pl.ds(0, reach)],
+                sems.at[n],
             )
-        return found
-
-    now = lax.rem(step, 2)
+        )
+    for n in range(pieces):
+        s, g = n // 2, n % 2
+        if near:
+            chip = lax.rem(code_ref[0] + s, pieces // 2)
+            kid = (chip * 2 + lax.rem(code_ref[1] + g, 2)) * piece
+            source = centre_refs[0].at[pl.ds(cell, steps), pl.ds(pl.multiple_of(kid, piece), piece)]
+        else:
+            source = centre_refs[n].at[pl.ds(begin, steps)]
+        loads.append(
+            pltpu.make_async_copy(source, centres.at[:, pl.ds(n * piece, piece)], sems.at[sources + n])
+        )
 
     @pl.when(step == 0)
     def _():
@@ -136,7 +152,7 @@
             )
             for n in range(sources)
         ]
-        for copy in lines:
+        for copy in lines + loads:
             copy.start()
         for copy in lines:
             copy.wait()
@@ -144,27 +160,23 @@
         to_scalars = pltpu.make_async_copy(meta_wide, meta_ref, meta_sems.at[sources])
         to_scalars.start()
         to_scalars.wait()
-        for copy in copies(0, 0):
-            copy.start()
-
-    if steps > 1:
-
-        @pl.when(step + 1 < steps)
-        def _():
-            for copy in copies(step + 1, 1 - now):
-                copy.start()
-
-    centre = jnp.concatenate([c[0] for c in centre_refs], axis=0)
+        for copy in loads:
+            copy.wait()
+
+    def entry(n, field):
+        return meta_ref[n * meta_extra + (n % cores) * per_core + begin + step, field]
+
+    centre = centres[step]
     wide = centre.astype(jnp.float32)
     half_norm = 0.5 * jnp.sum(wide * wide, axis=1, keepdims=True)
     slot = lax.broadcasted_iota(jnp.int32, (1, sources * window), 1)
     valid = slot < 0
     for n in range(sources):
-        low = n * window + entry(n, step, 1)
-        valid = valid | ((slot >= low) & (slot < low + entry(n, step, 2)))
-    for copy in copies(step, now):
-        copy.wait()
-    chosen = held[now]
+        low = n * window + entry(n, 1)
+        valid = valid | ((slot >= low) & (slot < low + entry(n, 2)))
+    chosen = jnp.concatenate(
+        [held[n, pl.ds(pl.multiple_of(entry(n, 0) * 16, 16), window)] for n in range(sources)]
+    )
     products = lax.dot_general(
         centre, chosen, (((1,), (1,)), ((), ())), preferred_element_type=jnp.float32
     )
@@ -225,15 +237,65 @@
     return lax.optimization_barrier((value, *others))[0]
 
 
+def _update_kernel(per_core, chips, piece, tail, code_ref, keep_ref, mass_ref, *refs):
+    got_refs, refs = refs[: 2 * (chips - 1)], refs[2 * (chips - 1) :]
+    first_ref, others_ref, tail_ref, prior_ref, out_ref, swap_ref, lines_ref, weight = refs
+    step = pl.program_id(0)
+    lines = mass_ref[:, 0, :128]
+    for ref in [*got_refs[1::2], tail_ref]:
+        rows = ref[...].astype(jnp.float32)
+        for n in range(3):
+            lines = lines + rows[n * per_core : (n + 1) * per_core]
+    line = lax.broadcasted_iota(jnp.int32, lines.shape, 0)
+    mine = jnp.sum(jnp.where(line == step, lines, 0.0), axis=0, keepdims=True)
+    weight[...] = jnp.broadcast_to(1.0 / (mine + prior_mass), (128, 128)).T
+
+    @pl.when(step == 0)
+    def _():
+        lines_ref[...] = jnp.concatenate(
+            [lines, jnp.zeros((lines_ref.shape[0] - per_core, 128), jnp.float32)], axis=0
+        )
+
+    def updated(at_kid):
+        rows = pl.ds(pl.multiple_of(at_kid, piece), piece)
+        numer = keep_ref[0, rows] + prior_mass * prior_ref[0, rows]
+        for ref in got_refs[0::2]:
+            numer = numer + ref[rows].astype(jnp.float32)
+        far = jnp.where(step == 0, first_ref[rows], others_ref[rows])
+        return (numer + far.astype(jnp.float32)) * weight[rows, :1]
+
+    here = lax.rem(code_ref[2] + code_ref[1], 2) * piece
+    out_ref[0] = updated(here)
+    swap_ref[0, :piece] = updated(piece - here)
+    swap_ref[0, piece:] = jnp.zeros((8, swap_ref.shape[2]), jnp.float32)
+    swap_ref[0, piece:, :128] = jnp.broadcast_to(mine, (8, 128))
+
+
+def _finish_kernel(per_core, piece, code_ref, _, swap_ref, lines_ref, out_ref, mass_ref, sem):
+    other = 1 - code_ref[2]
+    copy = pltpu.make_async_copy(
+        swap_ref.at[:, pl.ds(0, piece)], out_ref.at[pl.ds(other * per_core, per_core)], sem
+    )
+    copy.start()
+    mine = lines_ref[:per_core]
+    theirs = swap_ref[:, piece, :128]
+    lines = jnp.where(
+        other == 1, jnp.concatenate([mine, theirs], axis=0), jnp.concatenate([theirs, mine], axis=0)
+    )
+    here = lax.rem(code_ref[2] + code_ref[1], 2)
+    mass_ref[...] = jnp.where(here == 0, lines[:, :piece], lines[:, piece : 2 * piece])
+    copy.wait()
+
+
 def _params():
     return pltpu.CompilerParams(vmem_limit_bytes=vmem_limit)
 
 
-def _cell_call(code, sharp, centre_in, row_blocks, window, per_core, begin, steps, kids, share, sends, earlier, tail):
+def _cell_call(code, sharp, arrays, near, row_blocks, window, reach, per_core, begin, steps, kids, share, sends, earlier, tail):
     sources = len(row_blocks)
     row_arrays, bases = zip(*row_blocks, strict=True)
     width = row_arrays[0].shape[1]
-    arrays, specs = zip(*centre_in, strict=True)
+    pieces = kids // (share // 2)
     span = row_arrays[0].shape[0] // 2
     rows = sources * window
     out_shape = [
@@ -245,18 +307,19 @@
     moving = lambda shape: pl.BlockSpec((1, *shape[1:]), lambda n, *_: (n, 0, 0))
     return pl.pallas_call(
         functools.partial(
-            _cell_kernel, sources, window, len(arrays), share, steps, per_core, begin, span, bases, len(earlier), tail
+            _cell_kernel, sources, window, reach, pieces, near, share, steps, per_core, begin, span, bases, len(earlier), tail
         ),
         grid_spec=pltpu.PrefetchScalarGridSpec(
             num_scalar_prefetch=2,
             grid=(steps,),
-            in_specs=list(specs) + [anywhere] * sources + [fixed(v.shape) for v in earlier],
+            in_specs=[anywhere] * (len(arrays) + sources) + [fixed(v.shape) for v in earlier],
             out_specs=[
                 (moving if n in (0, 2) else fixed)(o.shape) for n, o in enumerate(out_shape)
             ],
             scratch_shapes=[
-                pltpu.VMEM((min(steps, 2), rows, width), jnp.bfloat16),
-                pltpu.SemaphoreType.DMA((min(steps, 2), sources)),
+                pltpu.VMEM((sources, reach, width), jnp.bfloat16),
+                pltpu.VMEM((steps, kids, width), jnp.bfloat16),
+                pltpu.SemaphoreType.DMA((sources + pieces,)),
                 pltpu.VMEM((sources * meta_extra, 128), jnp.bfloat16),
                 pltpu.VMEM((sources * meta_extra, 128), jnp.int32),
                 pltpu.SMEM((sources * meta_extra, 128), jnp.int32),
@@ -264,8 +327,8 @@
             ],
         ),
         out_shape=out_shape,
-        compiler_params=_params(),
-        cost_estimate=cheap,
+        compiler_params=pltpu.CompilerParams(vmem_limit_bytes=44 * 1024 * 1024),
+        cost_estimate=busy,
     )(code, sharp, *arrays, *row_arrays, *earlier)
 
 
@@ -285,7 +348,8 @@
     window = -(-(cell_cap + 16) // 16) * 16
     while sources * window % 128:
         window += 16
-    window = min(window, own_slots)
+    reach = min(own_slots, -(-per_core * cell_cap // 16) * 16)
+    window = min(window, reach)
     share = kids // chips
     piece = share // group_count
 
@@ -357,7 +421,7 @@
     block = jax.ShapeDtypeStruct((span, width), jnp.bfloat16)
     lines = cell_count * meta_extra
     flat, off, meta, *blocks = pl.pallas_call(
-        functools.partial(_place_kernel, cells_local, window, own_slots, first_segs),
+        functools.partial(_place_kernel, per_core, reach, window, own_slots, first_segs),
         out_shape=[
             jax.ShapeDtypeStruct((1, rows), jnp.int32),
             jax.ShapeDtypeStruct((1, rows), jnp.int32),
@@ -413,29 +477,25 @@
                 mass = mass + masses_in(got[steps * share :])
         return keep, mass
 
-    results, totals, masses, theirs, notes = [], [], [], [], []
+    results, totals, theirs, notes = [], [], [], []
     for t, begin, size in [(1, *part) for part in parts] + [(0, 0, per_core)]:
-        code_here = _after(code, notes[-1] if t else totals[1]) if results else code
         if not t:
-            held[0] = held_of(0, totals[0])
-        centre_in = []
-        for s in range(chips):
-            for g in range(group_count):
-                if t:
-                    spec = pl.BlockSpec((1, piece, width), lambda n, *_, o=begin: (o + n, 0, 0))
-                    centre_in.append((foreign_pieces[s * group_count + g], spec))
-                else:
-
-                    def where_from(n, c, sharp_ref, s=s, g=g, o=begin):
-                        chip = lax.rem(c[0] + s, chips)
-                        return c[2] * per_core + o + n, chip * group_count + lax.rem(c[1] + g, group_count), 0
-
-                    centre_in.append((centroids, pl.BlockSpec((1, piece, width), where_from)))
+            held[0] = held_of(0, totals[1])
+            notes.append(
+                pl.pallas_call(
+                    _copy_kernel,
+                    out_shape=jax.ShapeDtypeStruct(notes[-1].shape, jnp.float32),
+                    compiler_params=_params(),
+                    cost_estimate=dear,
+                )(_after(notes.pop(), totals[1]))
+            )
+        code_here = _after(code, notes[-1]) if results else code
         earlier = [r[1] for r in results] if t else []
         extra = 0 if t and begin + size < per_core else tail
         results.append(
             _cell_call(
-                code_here, foreign_sharp if t else sharpness, centre_in, held[t], window, per_core,
+                code_here, foreign_sharp if t else sharpness, foreign_pieces if t else [centroids],
+                not t, held[t], window, reach, per_core,
                 begin, size, kids, share, chips - 1, earlier if extra else [], extra,
             )
         )
@@ -451,29 +511,21 @@
                     cost_estimate=dear,
                 )(scores)
             )
-        else:
-            results[-1] = [*results[-1][:3], *(_after(v, theirs[0]) for v in results[-1][3:])]
+        if not t:
+            arrived = [hop_chip(results[-1][3 + n], n + 1) for n in range(chips - 1)]
+            break
         total, mass = over_chips(results[-1], size, earlier, extra)
         if t and extra:
             total = _after(total, notes[-1])
-        masses.append(mass)
-        if t:
-            total = total.astype(wire).reshape(size * share, width)
-            if extra:
-                high = _round(mass)
-                middle = _round(mass - high)
-                terms = jnp.concatenate([high, middle, mass - high - middle])
-                behind = jnp.pad(
-                    terms.astype(wire), ((0, tail - terms.shape[0]), (0, width - share))
-                )
-                total = jnp.concatenate([total, behind])
-            theirs.append(hop_partner(total))
+        total = total.astype(wire).reshape(size * share, width)
+        if extra:
+            high = _round(mass)
+            middle = _round(mass - high)
+            terms = jnp.concatenate([high, middle, mass - high - middle])
+            behind = jnp.pad(terms.astype(wire), ((0, tail - terms.shape[0]), (0, width - share)))
+            total = jnp.concatenate([total, behind])
+        theirs.append(hop_partner(total))
         totals.append(total)
-    theirs = [_after(v, totals[-1]) for v in theirs]
-    got = jnp.concatenate([v[: size * share] for v, (_, size) in zip(theirs, parts, strict=True)])
-    numer = totals[-1] + got.reshape(totals[-1].shape).astype(jnp.float32)
-    mass = masses[-1] + masses_in(theirs[-1][-tail:])
-
     score_parts = pl.pallas_call(
         functools.partial(_pack_kernel, sources, window),
         out_shape=[jax.ShapeDtypeStruct((2 * per_core, window), jnp.float32)] * sources,
@@ -497,7 +549,7 @@
         functools.partial(_score_kernel, lines, window),
         out_shape=jax.ShapeDtypeStruct((1, rows), jnp.float32),
         compiler_params=_params(),
-        cost_estimate=dear,
+        cost_estimate=cheap,
     )(rel, off, jnp.concatenate(values, axis=0)).reshape(rows)
 
     def prior_from(n, c, g=0):
@@ -518,30 +570,59 @@
         compiler_params=_params(),
         cost_estimate=dear,
     )(code, *([centroids] * group_count))
-    updated = (numer + prior_mass * previous) / (mass[:, :, None] + prior_mass)
-    mine_at = ((k - y) % group_count) * piece
-    theirs_at = ((1 - k - y) % group_count) * piece
-
-    def both(at_kid):
-        lines = jnp.pad(
-            lax.dynamic_slice_in_dim(mass, at_kid, piece, 1), ((0, 0), (0, width - piece))
-        )
-        return lax.dynamic_slice_in_dim(updated, at_kid, piece, 1), lines
-
-    mine, mass_mine = both(mine_at)
-    theirs, mass_theirs = both(theirs_at)
-    swapped = hop_core(
-        jnp.concatenate([theirs, jnp.broadcast_to(mass_theirs[:, None], (per_core, 8, width))], 1)
-    )
-
-    def ordered(a, b):
-        return jnp.where(k == 0, jnp.concatenate([a, b], 0), jnp.concatenate([b, a], 0))
-
-    return (
-        ordered(mine, swapped[:, :piece]),
-        ordered(mass_mine[:, :piece], swapped[:, piece, :piece]),
-        frame_score,
-    )
+    theirs = [_after(v, *arrived) for v in theirs]
+    one_cell = lambda block, where: pl.BlockSpec(block, where)
+    whole = lambda v: pl.BlockSpec(v.shape, lambda n, c: (0,) * v.ndim)
+    behind = lambda steps: pl.BlockSpec((tail, 128), lambda n, c: (steps * share // tail, 0))
+    keep, mass = results[-1][:2]
+    got, got_specs = [], []
+    for v in arrived:
+        got += [v, v]
+        got_specs += [one_cell((share, width), lambda n, c: (n, 0)), behind(per_core)]
+    out, swap, lines_mine = pl.pallas_call(
+        functools.partial(_update_kernel, per_core, chips, piece, tail),
+        grid_spec=pltpu.PrefetchScalarGridSpec(
+            num_scalar_prefetch=1,
+            grid=(per_core,),
+            in_specs=[
+                one_cell((1, share, width), lambda n, c: (n, 0, 0)),
+                whole(mass),
+                *got_specs,
+                one_cell((share, width), lambda n, c: (0, 0)),
+                one_cell((share, width), lambda n, c: (jnp.maximum(n - 1, 0), 0)),
+                behind(per_core - 1),
+                one_cell((1, share, width), lambda n, c: (n, 0, 0)),
+            ],
+            out_specs=[
+                one_cell((1, piece, width), lambda n, c: (c[2] * per_core + n, 0, 0)),
+                one_cell((1, piece + 8, width), lambda n, c: (n, 0, 0)),
+                pl.BlockSpec((8, 128), lambda n, c: (0, 0)),
+            ],
+            scratch_shapes=[pltpu.VMEM((128, 128), jnp.float32)],
+        ),
+        out_shape=[
+            jax.ShapeDtypeStruct((cells_local, piece, width), jnp.float32),
+            jax.ShapeDtypeStruct((per_core, piece + 8, width), jnp.float32),
+            jax.ShapeDtypeStruct((8, 128), jnp.float32),
+        ],
+        compiler_params=_params(),
+        cost_estimate=dear,
+    )(code, keep, mass, *got, theirs[0], theirs[1], theirs[1], previous)
+    new_centroids, child_mass = pl.pallas_call(
+        functools.partial(_finish_kernel, per_core, piece),
+        in_specs=[pl.BlockSpec(memory_space=pltpu.SMEM), anywhere]
+        + [pl.BlockSpec(memory_space=pltpu.VMEM)] * 2,
+        out_specs=[anywhere, pl.BlockSpec(memory_space=pltpu.VMEM)],
+        out_shape=[
+            jax.ShapeDtypeStruct(out.shape, jnp.float32),
+            jax.ShapeDtypeStruct((cells_local, piece), jnp.float32),
+        ],
+        scratch_shapes=[pltpu.SemaphoreType.DMA(())],
+        input_output_aliases={1: 0},
+        compiler_params=_params(),
+        cost_estimate=dear,
+    )(code, out, hop_core(swap), lines_mine)
+    return new_centroids, child_mass, frame_score
 
 
 def solution(mesh):

time: 121 us -> 113 us (0.934)
  local copies, waits for them, and re-layouts: 9.17 us -> 3.25 us
  Pallas kernels: 32.5 us -> 27.9 us
  waiting for transfers between devices: 56.7 us -> 61 us
  other arithmetic: 5.32 us -> 1.18 us
  starting transfers between devices: 16.2 us -> 18.2 us
    ppermute x3, waiting for transfers between devices: 12.1 us -> 0.01 us  [hop_any(): return lax.ppermute(v, ('cell', 'frame'), pairs)]
    ppermute x4, waiting for transfers between devices: 13.6 us -> 24 us  [hop_partner(): lax.ppermute(v, 'cell', [(i, (i + half) % cell_count) for i in range(cell...]
    unnamed x25 -> x12, local copies, waits for them, and re-layouts: 6.02 us -> 1.61 us
    ppermute x2, waiting for transfers between devices: 2.25 us -> 5.88 us  [hop_member(): lax.ppermute(v, 'cell', [(b * half + i, b * half + (i + s) % half) for b...]
    pallas_call x4 -> x7, Pallas kernels: 25.9 us -> 22.6 us  [the longest x3 16.1 us: _cell_call(): pl.pallas_call(functools.partial(_cell_kernel, sources, window, reach, pi...]
    ppermute x4, waiting for transfers between devices: 1.5 us -> 3.61 us  [hop_core(): return lax.ppermute(v, 'frame', [(i, i ^ 1) for i in range(frame_count)])]
    select_n x2 -> x0, other arithmetic: 1.87 us -> none  [ordered(): jnp.where(k == 0, jnp.concatenate([a, b], 0), jnp.concatenate([b, a], 0))]
    ppermute x4, waiting for transfers between devices: 14.8 us -> 16.6 us  [hop_chip(): lax.ppermute(v, 'frame', [(a * cores + c, (a + s) % chips * cores + c) fo...]
  transfers between devices with their start and end apart: 19 -> 19, of which waited for: 11 -> 12; matrix products, arithmetic and copies ran while one was open for 3% -> 2% of each run, Pallas kernels for 27% -> 23%
where the time goes in v3:
time: 113 us; the launch traced here: 112 us
  waiting for transfers between devices  61 us (54%)
  Pallas kernels  27.9 us (25%)
  starting transfers between devices  18.2 us (16%)
  local copies, waits for them, and re-layouts  3.25 us (3%)
  other arithmetic  1.18 us (1%)
    ppermute x4, waiting for transfers between devices, hop_partner(): lax.ppermute(v, 'cell', [(i, (i + half) % cell_count) for i in range(cell...  24 us
    ppermute x4, waiting for transfers between devices, hop_chip(): lax.ppermute(v, 'frame', [(a * cores + c, (a + s) % chips * cores + c) fo...  16.6 us
    pallas_call x3, Pallas kernels, _cell_call(): pl.pallas_call(functools.partial(_cell_kernel, sources, window, reach, pi...  16.1 us
    ppermute x2, waiting for transfers between devices, hop_group(): return lax.ppermute(v, 'groups', [(i, 1 - i) for i in range(2)])  10.9 us
    ppermute x2, waiting for transfers between devices, hop_member(): lax.ppermute(v, 'cell', [(b * half + i, b * half + (i + s) % half) for b...  5.88 us
    ppermute x4, starting transfers between devices, hop_partner(): lax.ppermute(v, 'cell', [(i, (i + half) % cell_count) for i in range(cell...  5.76 us
    ppermute x4, starting transfers between devices, hop_chip(): lax.ppermute(v, 'frame', [(a * cores + c, (a + s) % chips * cores + c) fo...  5.27 us
    ppermute x4, waiting for transfers between devices, hop_core(): return lax.ppermute(v, 'frame', [(i, i ^ 1) for i in range(frame_count)])  3.61 us
  transfers between devices with their start and end apart: 19, of which 12 were waited for; matrix products, arithmetic and copies ran while one was open for 2% of the time, Pallas kernels for 23%

profile of v3, /device:TPU:0, one launch (start us, length us, event | category | flops | bytes accessed | tf_op | source)
XLA Modules:
  0.0 112.5 jit_solution(8763903478822270467)
XLA Ops:
  0.7 1.0 constant_dynamic-slice_fusion
  1.7 4.1 %collective-permute-start.1 = (bf16[3,64,1024]{2,1,0:T(8,128)(2,1)S(1)}, bf16[3,64,1024]{2,1,0:T(8,128)(2,1)S(1)}, u32[]{:S(2)}, u32[]{:S(2)}) collective-permute-start(bf16[3,64,1024]{2,1,0:T(8,128)(2,1)S(1)} %constant_dynamic-slice_fusion), channel_id=1, source_target_pairs={{0,8},{4,12},{8,0},{12,4},{1,9},{5,13},{9,1},{13,5},{2,10},{6,14},... | collective-permute-start | bytes 1179656 | tf_op jit(solution)/shard_map/ppermute | solution.py:381
  5.9 0.8 fusion.12.rel_ref
  6.7 1.6 %copy-done.3 = bf16[1024,1024]{1,0:T(8,128)(2,1)S(1)} copy-done((bf16[1024,1024]{1,0:T(8,128)(2,1)S(1)}, bf16[1024,1024]{1,0:T(8,128)(2,1)}, u32[]{:S(2)}) %copy-start.3) | copy-done | bytes 2097176
  8.3 2.0 %shard_map.67 = (s32[1,1024]{1,0:T(1,128)S(1)}, s32[1,1024]{1,0:T(1,128)S(1)}, f32[64,128]{1,0:T(8,128)S(1)}, bf16[528,1024]{1,0:T(8,128)(2,1)S(1)}) custom-call(s32[1,1024]{1,0:T(1,128)S(1)} %fusion.12.rel_ref, bf16[1024,1024]{1,0:T(8,128)(2,1)S(1)} %copy-done.3), custom_call_target="tpu_custom_call" | custom-call | flops 20000000000 | bytes 1000000000 | tf_op jit(solution)/shard_map/pallas_call | solution.py:423
  10.3 1.9 %collective-permute-start.6 = (bf16[528,1024]{1,0:T(8,128)(2,1)S(1)}, bf16[528,1024]{1,0:T(8,128)(2,1)S(1)}, u32[]{:S(2)}, u32[]{:S(2)}) collective-permute-start(bf16[528,1024]{1,0:T(8,128)(2,1)S(1)} %get-tuple-element.43), channel_id=1, source_target_pairs={{0,4},{4,0},{8,12},{12,8},{1,5},{5,1},{9,13},{13,9},{2,6},{6,2},{1... | collective-permute-start | bytes 3244040 | tf_op jit(solution)/shard_map/ppermute | solution.py:376
  12.2 11.2 %collective-permute-done.1.refs_2_ = bf16[3,64,1024]{2,1,0:T(8,128)(2,1)S(1)} collective-permute-done((bf16[3,64,1024]{2,1,0:T(8,128)(2,1)S(1)}, bf16[3,64,1024]{2,1,0:T(8,128)(2,1)S(1)}, u32[]{:S(2)}, u32[]{:S(2)}) %collective-permute-start.1) | collective-permute-done | bytes 393248 | tf_op jit(solution)/shard_map/ppermute | solution.py:381
  23.5 1.6 %collective-permute-start.2 = (bf16[3,64,1024]{2,1,0:T(8,128)(2,1)S(1)}, bf16[3,64,1024]{2,1,0:T(8,128)(2,1)S(1)}, u32[]{:S(2)}, u32[]{:S(2)}) collective-permute-start(bf16[3,64,1024]{2,1,0:T(8,128)(2,1)S(1)} %collective-permute-done.1.refs_2_), channel_id=1, source_target_pairs={{0,16},{16,0},{1,17},{17,1},{2,18},{18,2},{3,19},{19,3},{4,20},{20... | collective-permute-start | bytes 1179656 | tf_op jit(solution)/shard_map/ppermute | solution.py:384
  25.0 1.5 %collective-permute-start.3 = (bf16[3,64,1024]{2,1,0:T(8,128)(2,1)S(1)}, bf16[3,64,1024]{2,1,0:T(8,128)(2,1)S(1)}, u32[]{:S(2)}, u32[]{:S(2)}) collective-permute-start(bf16[3,64,1024]{2,1,0:T(8,128)(2,1)S(1)} %collective-permute-done.1.refs_2_), channel_id=1, source_target_pairs={{0,2},{1,3},{2,0},{3,1},{4,6},{5,7},{6,4},{7,5},{8,10},{9,11},{10,... | collective-permute-start | bytes 1179656 | tf_op jit(solution)/shard_map/ppermute | solution.py:369
  26.5 1.3 %shard_map.68 = bf16[528,1024]{1,0:T(8,128)(2,1)S(1)} custom-call(s32[1,1024]{1,0:T(1,128)S(1)} %get-tuple-element.42.flat_ref, f32[64,128]{1,0:T(8,128)S(1)} %get-tuple-element.41.meta_ref, bf16[1024,1024]{1,0:T(8,128)(2,1)S(1)} %copy-done.4), custom_call_target="tpu_custom_call" | custom-call | flops 20000000000 | bytes 1000000000 | tf_op jit(solution)/shard_map/pallas_call | solution.py:436
  27.8 5.9 %collective-permute-done.2.refs_3_ = bf16[3,64,1024]{2,1,0:T(8,128)(2,1)S(1)} collective-permute-done((bf16[3,64,1024]{2,1,0:T(8,128)(2,1)S(1)}, bf16[3,64,1024]{2,1,0:T(8,128)(2,1)S(1)}, u32[]{:S(2)}, u32[]{:S(2)}) %collective-permute-start.2) | collective-permute-done | bytes 393248 | tf_op jit(solution)/shard_map/ppermute | solution.py:384
  33.7 1.0 collective-permute-done.3.refs_4_
  34.7 2.4 %shard_map.69.refs_6_.refs_3_ = bf16[1056,1024]{1,0:T(8,128)(2,1)S(1)} custom-call(s32[1,1024]{1,0:T(1,128)S(1)} %get-tuple-element.42.flat_ref, f32[64,128]{1,0:T(8,128)S(1)} %get-tuple-element.41.meta_ref, bf16[1024,1024]{1,0:T(8,128)(2,1)S(1)} %copy-done.4), custom_call_target="tpu_custom_call" | custom-call | flops 20000000000 | bytes 1000000000 | tf_op jit(solution)/shard_map/pallas_call | solution.py:443
  38.0 5.0 %collective-permute-done.6.refs_8_ = bf16[528,1024]{1,0:T(8,128)(2,1)S(1)} collective-permute-done((bf16[528,1024]{1,0:T(8,128)(2,1)S(1)}, bf16[528,1024]{1,0:T(8,128)(2,1)S(1)}, u32[]{:S(2)}, u32[]{:S(2)}) %collective-permute-start.6) | collective-permute-done | bytes 1081376 | tf_op jit(solution)/shard_map/ppermute | solution.py:376
  43.7 5.0 %collective-permute-done.4.refs_5_ = bf16[3,64,1024]{2,1,0:T(8,128)(2,1)S(1)} collective-permute-done((bf16[3,64,1024]{2,1,0:T(8,128)(2,1)S(1)}, bf16[3,64,1024]{2,1,0:T(8,128)(2,1)S(1)}, u32[]{:S(2)}, u32[]{:S(2)}) %collective-permute-start.4) | collective-permute-done | bytes 393248 | tf_op jit(solution)/shard_map/ppermute | solution.py:384
  48.7 4.2 %shard_map.70 = (f32[1,128,1024]{2,1,0:T(8,128)S(1)}, f32[1,8,256]{2,1,0:T(8,128)S(1)}, f32[1,8,640]{2,1,0:T(8,128)S(1)}, bf16[128,1024]{1,0:T(8,128)(2,1)S(1)}) custom-call(s32[3]{0:T(128)S(1)} %pad_add_fusion.refs_0_.code_ref, f32[6]{0:T(128)S(1)} %collective-permute-done.refs_1_, bf16[3,64,1024]{2,1,0:T(8,128)(2,1)S(1)} %collective-permute-done.1.refs_2_, ...), custom_call_target="tpu_custom_call" | custom-call | flops 20000000000 | bytes 1 | tf_op jit(solution)/shard_map/pallas_call | solution.py:308
  52.9 1.6 %collective-permute-start.8 = (bf16[128,1024]{1,0:T(8,128)(2,1)S(1)}, bf16[128,1024]{1,0:T(8,128)(2,1)S(1)}, u32[]{:S(2)}, u32[]{:S(2)}) collective-permute-start(bf16[128,1024]{1,0:T(8,128)(2,1)S(1)} %get-tuple-element.50), channel_id=1, source_target_pairs={{0,2},{1,3},{2,0},{3,1},{4,6},{5,7},{6,4},{7,5},{8,10},{9,11},{10,... | collective-permute-start | bytes 786440 | tf_op jit(solution)/shard_map/ppermute | solution.py:369
  54.5 5.1 %shard_map.72 = (f32[2,128,1024]{2,1,0:T(8,128)S(1)}, f32[2,8,256]{2,1,0:T(8,128)S(1)}, f32[2,8,640]{2,1,0:T(8,128)S(1)}, bf16[272,1024]{1,0:T(8,128)(2,1)S(1)}) custom-call(s32[3]{0:T(128)S(1)} %pad_add_fusion.refs_0_.code_ref, f32[6]{0:T(128)S(1)} %collective-permute-done.refs_1_, bf16[3,64,1024]{2,1,0:T(8,128)(2,1)S(1)} %collective-permute-done.1.refs_2_, ...), custom_call_target="tpu_custom_call" | custom-call | flops 20000000000 | bytes 1 | tf_op jit(solution)/shard_map/pallas_call | solution.py:308
  61.0 0.8 collective-permute-start.13
  61.8 11.9 %collective-permute-done.9 = bf16[272,1024]{1,0:T(8,128)(2,1)S(1)} collective-permute-done((bf16[272,1024]{1,0:T(8,128)(2,1)S(1)}, bf16[272,1024]{1,0:T(8,128)(2,1)S(1)}, u32[]{:S(2)}, u32[]{:S(2)}) %collective-permute-start.9) | collective-permute-done | bytes 557088 | tf_op jit(solution)/shard_map/ppermute | solution.py:369
  74.0 0.8 collective-permute-start.14
  74.8 0.9 collective-permute-done.10.refs_5_
  75.6 2.7 %collective-permute-done.11.refs_6_ = bf16[528,1024]{1,0:T(8,128)(2,1)S(1)} collective-permute-done((bf16[528,1024]{1,0:T(8,128)(2,1)S(1)}, bf16[528,1024]{1,0:T(8,128)(2,1)S(1)}, u32[]{:S(2)}, u32[]{:S(2)}) %collective-permute-start.11) | collective-permute-done | bytes 1081376 | tf_op jit(solution)/shard_map/ppermute | solution.py:366
  78.3 6.8 %shard_map.75 = (f32[3,128,1024]{2,1,0:T(8,128)S(1)}, f32[3,8,256]{2,1,0:T(8,128)S(1)}, f32[3,8,640]{2,1,0:T(8,128)S(1)}, bf16[400,1024]{1,0:T(8,128)(2,1)S(1)}) custom-call(s32[3]{0:T(128)S(1)} %pad_add_fusion.refs_0_.code_ref, f32[6]{0:T(128)S(1)} %copy-done.5, bf16[6,256,1024]{2,1,0:T(8,128)(2,1)} %refs_1_.3, ...), custom_call_target="tpu_custom_call" | custom-call | flops 20000000000 | bytes 1 | tf_op jit(solution)/shard_map/pallas_call | solution.py:308
  85.2 1.6 %collective-permute-start.12 = (bf16[400,1024]{1,0:T(8,128)(2,1)S(1)}, bf16[400,1024]{1,0:T(8,128)(2,1)S(1)}, u32[]{:S(2)}, u32[]{:S(2)}) collective-permute-start(bf16[400,1024]{1,0:T(8,128)(2,1)S(1)} %get-tuple-element.61), channel_id=1, source_target_pairs={{0,2},{1,3},{2,0},{3,1},{4,6},{5,7},{6,4},{7,5},{8,10},{9,11},{10,... | collective-permute-start | bytes 2457608 | tf_op jit(solution)/shard_map/ppermute | solution.py:369
  86.9 2.2 %collective-permute-start.18 = (f32[6,160]{1,0:T(8,128)S(1)}, f32[6,160]{1,0:T(8,128)S(1)}, u32[]{:S(2)}, u32[]{:S(2)}) collective-permute-start(f32[6,160]{1,0:T(8,128)S(1)} %get-tuple-element.74), channel_id=1, source_target_pairs={{0,5},{1,4},{2,7},{3,6},{4,1},{5,0},{6,3},{7,2},{8,13},{9,12},{10,... | collective-permute-start | bytes 11528 | tf_op jit(solution)/shard_map/ppermute | solution.py:394
  89.7 12.8 %collective-permute-done.14.refs_3_.refs_4_ = bf16[272,1024]{1,0:T(8,128)(2,1)S(1)} collective-permute-done((bf16[272,1024]{1,0:T(8,128)(2,1)S(1)}, bf16[272,1024]{1,0:T(8,128)(2,1)S(1)}, u32[]{:S(2)}, u32[]{:S(2)}) %collective-permute-start.14) | collective-permute-done | bytes 557088 | tf_op jit(solution)/shard_map/ppermute | solution.py:381
  102.5 3.1 %collective-permute-done.12.refs_0_.refs_1_ = bf16[400,1024]{1,0:T(8,128)(2,1)S(1)} collective-permute-done((bf16[400,1024]{1,0:T(8,128)(2,1)S(1)}, bf16[400,1024]{1,0:T(8,128)(2,1)S(1)}, u32[]{:S(2)}, u32[]{:S(2)}) %collective-permute-start.12) | collective-permute-done | bytes 819232 | tf_op jit(solution)/shard_map/ppermute | solution.py:369
  105.6 2.4 %shard_map.77 = (f32[6,64,1024]{2,1,0:T(8,128)}, f32[3,72,1024]{2,1,0:T(8,128)S(1)}, f32[8,128]{1,0:T(8,128)S(1)}) custom-call(s32[3]{0:T(128)S(1)} %pad_add_fusion.refs_0_.code_ref, f32[3,128,1024]{2,1,0:T(8,128)S(1)} %get-tuple-element.59.keep_ref, f32[3,8,256]{2,1,0:T(8,128)S(1)} %get-tuple-element.60.mass_ref, ...), custom_call_target="tpu_custom_call" | custom-call | flops 20000000000 | bytes 1000000000 | tf_op jit(solution)/shard_map/pallas_call | solution.py:582
  108.6 0.9 shard_map.80
  109.5 0.9 collective-permute-done.15.swap_ref
  110.4 2.0 %shard_map.78 = (f32[6,64,1024]{2,1,0:T(8,128)}, f32[6,64]{1,0:T(8,128)}) custom-call(s32[3]{0:T(128)S(1)} %pad_add_fusion.refs_0_.code_ref, f32[6,64,1024]{2,1,0:T(8,128)} %get-tuple-element.64._, f32[3,72,1024]{2,1,0:T(8,128)S(1)} %collective-permute-done.15.swap_ref, f32[8,128]{1,0:T(8,128)S(1)} %get-tuple-element.66.lines_ref), custom_call_target="tpu_custom_call", output_to_operand_aliasing={{0}: (1, {})} | custom-call | flops 20000000000 | bytes 1000000000 | tf_op jit(solution)/shard_map/pallas_call | solution.py:611
  (53 shorter events, 4.6 us)
Async XLA Ops:
  1.7 21.8 %collective-permute-start.1 = (bf16[3,64,1024]{2,1,0:T(8,128)(2,1)S(1)}, bf16[3,64,1024]{2,1,0:T(8,128)(2,1)S(1)}, u32[]{:S(2)}, u32[]{:S(2)}) collective-permute-start(bf16[3,64,1024]{2,1,0:T(8,128)(2,1)S(1)} %constant_dynamic-slice_fusion), channel_id=1, source_target_pairs={{0,8},{4,12},{8,0},{12,4},{1,9},{5,13},{9,1},{13,5},{2,10},{6,14},... | collective-permute-start | bytes 1179656 | tf_op jit(solution)/shard_map/ppermute | solution.py:381
  5.8 22.0 %collective-permute-start = (f32[6]{0:T(128)}, f32[6]{0:T(128)S(1)}, u32[]{:S(2)}, u32[]{:S(2)}) collective-permute-start(f32[6]{0:T(128)} %refs_1_.2), channel_id=1, source_target_pairs={{0,8},{4,12},{8,0},{12,4},{1,9},{5,13},{9,1},{13,5},{2,10},{6,14},... | collective-permute-start | bytes 80 | tf_op jit(solution)/shard_map/ppermute | solution.py:381
  6.7 1.6 %copy-start.3 = (bf16[1024,1024]{1,0:T(8,128)(2,1)S(1)}, bf16[1024,1024]{1,0:T(8,128)(2,1)}, u32[]{:S(2)}) copy-start(bf16[1024,1024]{1,0:T(8,128)(2,1)} %frames_ref.5) | copy-start | bytes 6291460
  8.3 2.0 %copy-start.1 = (s32[1,1024]{1,0:T(1,128)}, s32[1,1024]{1,0:T(1,128)S(1)}, u32[]{:S(2)}) copy-start(s32[1,1024]{1,0:T(1,128)S(1)} %fusion.12.rel_ref) | copy-start | bytes 12292
  8.3 18.2 %copy-start.4 = (bf16[1024,1024]{1,0:T(8,128)(2,1)S(1)}, bf16[1024,1024]{1,0:T(8,128)(2,1)}, u32[]{:S(2)}) copy-start(bf16[1024,1024]{1,0:T(8,128)(2,1)} %frames_ref.5) | copy-start | bytes 6291460
  10.3 32.7 %collective-permute-start.6 = (bf16[528,1024]{1,0:T(8,128)(2,1)S(1)}, bf16[528,1024]{1,0:T(8,128)(2,1)S(1)}, u32[]{:S(2)}, u32[]{:S(2)}) collective-permute-start(bf16[528,1024]{1,0:T(8,128)(2,1)S(1)} %get-tuple-element.43), channel_id=1, source_target_pairs={{0,4},{4,0},{8,12},{12,8},{1,5},{5,1},{9,13},{13,9},{2,6},{6,2},{1... | collective-permute-start | bytes 3244040 | tf_op jit(solution)/shard_map/ppermute | solution.py:376
  23.5 10.2 %collective-permute-start.2 = (bf16[3,64,1024]{2,1,0:T(8,128)(2,1)S(1)}, bf16[3,64,1024]{2,1,0:T(8,128)(2,1)S(1)}, u32[]{:S(2)}, u32[]{:S(2)}) collective-permute-start(bf16[3,64,1024]{2,1,0:T(8,128)(2,1)S(1)} %collective-permute-done.1.refs_2_), channel_id=1, source_target_pairs={{0,16},{16,0},{1,17},{17,1},{2,18},{18,2},{3,19},{19,3},{4,20},{20... | collective-permute-start | bytes 1179656 | tf_op jit(solution)/shard_map/ppermute | solution.py:384
  25.0 9.7 %collective-permute-start.3 = (bf16[3,64,1024]{2,1,0:T(8,128)(2,1)S(1)}, bf16[3,64,1024]{2,1,0:T(8,128)(2,1)S(1)}, u32[]{:S(2)}, u32[]{:S(2)}) collective-permute-start(bf16[3,64,1024]{2,1,0:T(8,128)(2,1)S(1)} %collective-permute-done.1.refs_2_), channel_id=1, source_target_pairs={{0,2},{1,3},{2,0},{3,1},{4,6},{5,7},{6,4},{7,5},{8,10},{9,11},{10,... | collective-permute-start | bytes 1179656 | tf_op jit(solution)/shard_map/ppermute | solution.py:369
  27.8 15.2 %copy-start = (bf16[6,256,1024]{2,1,0:T(8,128)(2,1)S(1)}, bf16[6,256,1024]{2,1,0:T(8,128)(2,1)}, u32[]{:S(2)}) copy-start(bf16[6,256,1024]{2,1,0:T(8,128)(2,1)} %refs_1_.3) | copy-start | bytes 9437188
  37.1 11.7 %collective-permute-start.5 = (bf16[1056,1024]{1,0:T(8,128)(2,1)S(1)}, bf16[1056,1024]{1,0:T(8,128)(2,1)S(1)}, u32[]{:S(2)}, u32[]{:S(2)}) collective-permute-start(bf16[1056,1024]{1,0:T(8,128)(2,1)S(1)} %shard_map.69.refs_6_.refs_3_), channel_id=1, source_target_pairs={{0,1},{1,0},{2,3},{3,2},{4,5},{5,4},{6,7},{7,6},{8,9},{9,8},{10,11... | collective-permute-start | bytes 6488072 | tf_op jit(solution)/shard_map/ppermute | solution.py:366
  37.2 11.5 %collective-permute-start.4 = (bf16[3,64,1024]{2,1,0:T(8,128)(2,1)S(1)}, bf16[3,64,1024]{2,1,0:T(8,128)(2,1)S(1)}, u32[]{:S(2)}, u32[]{:S(2)}) collective-permute-start(bf16[3,64,1024]{2,1,0:T(8,128)(2,1)S(1)} %collective-permute-done.3.refs_4_), channel_id=1, source_target_pairs={{0,16},{16,0},{1,17},{17,1},{2,18},{18,2},{3,19},{19,3},{4,20},{20... | collective-permute-start | bytes 1179656 | tf_op jit(solution)/shard_map/ppermute | solution.py:384
  43.0 5.7 %collective-permute-start.7 = (bf16[528,1024]{1,0:T(8,128)(2,1)S(1)}, bf16[528,1024]{1,0:T(8,128)(2,1)S(1)}, u32[]{:S(2)}, u32[]{:S(2)}) collective-permute-start(bf16[528,1024]{1,0:T(8,128)(2,1)S(1)} %collective-permute-done.6.refs_8_), channel_id=1, source_target_pairs={{0,1},{1,0},{2,3},{3,2},{4,5},{5,4},{6,7},{7,6},{8,9},{9,8},{10,11... | collective-permute-start | bytes 3244040 | tf_op jit(solution)/shard_map/ppermute | solution.py:366
  43.7 32.0 %collective-permute-start.10 = (bf16[528,1024]{1,0:T(8,128)(2,1)S(1)}, bf16[528,1024]{1,0:T(8,128)(2,1)S(1)}, u32[]{:S(2)}, u32[]{:S(2)}) collective-permute-start(bf16[528,1024]{1,0:T(8,128)(2,1)S(1)} %shard_map.68), channel_id=1, source_target_pairs={{0,4},{4,0},{8,12},{12,8},{1,5},{5,1},{9,13},{13,9},{2,6},{6,2},{1... | collective-permute-start | bytes 3244040 | tf_op jit(solution)/shard_map/ppermute | solution.py:376
  52.9 8.0 %collective-permute-start.8 = (bf16[128,1024]{1,0:T(8,128)(2,1)S(1)}, bf16[128,1024]{1,0:T(8,128)(2,1)S(1)}, u32[]{:S(2)}, u32[]{:S(2)}) collective-permute-start(bf16[128,1024]{1,0:T(8,128)(2,1)S(1)} %get-tuple-element.50), channel_id=1, source_target_pairs={{0,2},{1,3},{2,0},{3,1},{4,6},{5,7},{6,4},{7,5},{8,10},{9,11},{10,... | collective-permute-start | bytes 786440 | tf_op jit(solution)/shard_map/ppermute | solution.py:369
  59.6 14.0 %collective-permute-start.9 = (bf16[272,1024]{1,0:T(8,128)(2,1)S(1)}, bf16[272,1024]{1,0:T(8,128)(2,1)S(1)}, u32[]{:S(2)}, u32[]{:S(2)}) collective-permute-start(bf16[272,1024]{1,0:T(8,128)(2,1)S(1)} %get-tuple-element.53), channel_id=1, source_target_pairs={{0,2},{1,3},{2,0},{3,1},{4,6},{5,7},{6,4},{7,5},{8,10},{9,11},{10,... | collective-permute-start | bytes 1671176 | tf_op jit(solution)/shard_map/ppermute | solution.py:369
  61.0 44.6 %collective-permute-start.13 = (bf16[128,1024]{1,0:T(8,128)(2,1)S(1)}, bf16[128,1024]{1,0:T(8,128)(2,1)S(1)}, u32[]{:S(2)}, u32[]{:S(2)}) collective-permute-start(bf16[128,1024]{1,0:T(8,128)(2,1)S(1)} %fusion.1), channel_id=1, source_target_pairs={{0,8},{4,12},{8,0},{12,4},{1,9},{5,13},{9,1},{13,5},{2,10},{6,14},... | collective-permute-start | bytes 786440 | tf_op jit(solution)/shard_map/ppermute | solution.py:381
  74.0 4.4 %copy-start.5 = (f32[6]{0:T(128)S(1)}, f32[6]{0:T(128)}, u32[]{:S(2)}) copy-start(f32[6]{0:T(128)} %refs_1_.2) | copy-start | bytes 76
  74.0 28.5 %collective-permute-start.14 = (bf16[272,1024]{1,0:T(8,128)(2,1)S(1)}, bf16[272,1024]{1,0:T(8,128)(2,1)S(1)}, u32[]{:S(2)}, u32[]{:S(2)}) collective-permute-start(bf16[272,1024]{1,0:T(8,128)(2,1)S(1)} %pad_maximum_fusion), channel_id=1, source_target_pairs={{0,8},{4,12},{8,0},{12,4},{1,9},{5,13},{9,1},{13,5},{2,10},{6,14},... | collective-permute-start | bytes 1671176 | tf_op jit(solution)/shard_map/ppermute | solution.py:381
  75.6 2.7 %collective-permute-start.11 = (bf16[528,1024]{1,0:T(8,128)(2,1)S(1)}, bf16[528,1024]{1,0:T(8,128)(2,1)S(1)}, u32[]{:S(2)}, u32[]{:S(2)}) collective-permute-start(bf16[528,1024]{1,0:T(8,128)(2,1)S(1)} %collective-permute-done.10.refs_5_), channel_id=1, source_target_pairs={{0,1},{1,0},{2,3},{3,2},{4,5},{5,4},{6,7},{7,6},{8,9},{9,8},{10,11... | collective-permute-start | bytes 3244040 | tf_op jit(solution)/shard_map/ppermute | solution.py:366
  85.2 20.4 %collective-permute-start.12 = (bf16[400,1024]{1,0:T(8,128)(2,1)S(1)}, bf16[400,1024]{1,0:T(8,128)(2,1)S(1)}, u32[]{:S(2)}, u32[]{:S(2)}) collective-permute-start(bf16[400,1024]{1,0:T(8,128)(2,1)S(1)} %get-tuple-element.61), channel_id=1, source_target_pairs={{0,2},{1,3},{2,0},{3,1},{4,6},{5,7},{6,4},{7,5},{8,10},{9,11},{10,... | collective-permute-start | bytes 2457608 | tf_op jit(solution)/shard_map/ppermute | solution.py:369
  86.9 21.1 %collective-permute-start.18 = (f32[6,160]{1,0:T(8,128)S(1)}, f32[6,160]{1,0:T(8,128)S(1)}, u32[]{:S(2)}, u32[]{:S(2)}) collective-permute-start(f32[6,160]{1,0:T(8,128)S(1)} %get-tuple-element.74), channel_id=1, source_target_pairs={{0,5},{1,4},{2,7},{3,6},{4,1},{5,0},{6,3},{7,2},{8,13},{9,12},{10,... | collective-permute-start | bytes 11528 | tf_op jit(solution)/shard_map/ppermute | solution.py:394
  89.1 18.9 %collective-permute-start.17 = (f32[6,160]{1,0:T(8,128)S(1)}, f32[6,160]{1,0:T(8,128)S(1)}, u32[]{:S(2)}, u32[]{:S(2)}) collective-permute-start(f32[6,160]{1,0:T(8,128)S(1)} %get-tuple-element.73), channel_id=1, source_target_pairs={{0,4},{1,5},{2,6},{3,7},{4,0},{5,1},{6,2},{7,3},{8,12},{9,13},{10,... | collective-permute-start | bytes 11528 | tf_op jit(solution)/shard_map/ppermute | solution.py:394
  102.5 5.6 %collective-permute-start.16 = (f32[6,160]{1,0:T(8,128)S(1)}, f32[6,160]{1,0:T(8,128)S(1)}, u32[]{:S(2)}, u32[]{:S(2)}) collective-permute-start(f32[6,160]{1,0:T(8,128)S(1)} %get-tuple-element.72), channel_id=1, source_target_pairs={{0,1},{1,0},{2,3},{3,2},{4,5},{5,4},{6,7},{7,6},{8,9},{9,8},{10,11... | collective-permute-start | bytes 11528 | tf_op jit(solution)/shard_map/ppermute | solution.py:394
  105.6 3.0 %copy-start.2 = (s32[1,1024]{1,0:T(1,128)S(1)}, s32[1,1024]{1,0:T(1,128)}, u32[]{:S(2)}) copy-start(s32[1,1024]{1,0:T(1,128)} %copy-done.1) | copy-start | bytes 12292
  108.0 2.4 %collective-permute-start.15 = (f32[3,72,1024]{2,1,0:T(8,128)S(1)}, f32[3,72,1024]{2,1,0:T(8,128)S(1)}, u32[]{:S(2)}, u32[]{:S(2)}) collective-permute-start(f32[3,72,1024]{2,1,0:T(8,128)S(1)} %get-tuple-element.65), channel_id=1, source_target_pairs={{0,1},{1,0},{2,3},{3,2},{4,5},{5,4},{6,7},{7,6},{8,9},{9,8},{10,11... | collective-permute-start | bytes 2654216 | tf_op jit(solution)/shard_map/ppermute | solution.py:366

commit v4 on v3

--- a/solution.py
+++ b/solution.py
@@ -76,12 +76,10 @@
         _pick(flat, meta, frames_ref, g, out_ref)
 
 
-def _pick_kernel(segments, separate, flat_ref, meta_ref, frames_ref, *outs):
+def _pick_kernel(segments, flat_ref, meta_ref, frames_ref, *outs):
     flat, meta = flat_ref[...], meta_ref[...]
-    size = outs[0].shape[0] // (1 if separate else len(segments))
-    for n, g in enumerate(segments):
-        target = outs[n] if separate else outs[0].at[pl.ds(n * size, size)]
-        _pick(flat, meta, frames_ref, g, target)
+    for g, out_ref in zip(segments, outs, strict=True):
+        _pick(flat, meta, frames_ref, g, out_ref)
 
 
 def _split(lines, rows):
@@ -103,13 +101,32 @@
     out_ref[...] = in_ref[...]
 
 
+def _split(lines, rows):
+    high = lines.astype(jnp.bfloat16).astype(jnp.float32)
+    middle = (lines - high).astype(jnp.bfloat16).astype(jnp.float32)
+    rest = jnp.zeros((rows - 3 * lines.shape[0], lines.shape[1]), jnp.float32)
+    return jnp.concatenate([high, middle, lines - high - middle, rest], axis=0)
+
+
+def _round(value):
+    return lax.reduce_precision(value, 8, 7)
+
+
+def _note_kernel(score_ref, out_ref):
+    out_ref[...] = score_ref[:, 0]
+
+
+def _copy_kernel(in_ref, out_ref):
+    out_ref[...] = in_ref[...]
+
+
 def _prior_kernel(group_count, code_ref, *refs):
     for g in range(group_count):
         size = refs[g].shape[1]
         refs[-1][:, g * size : (g + 1) * size] = refs[g][...].astype(jnp.float32)
 
 
-def _cell_kernel(sources, window, reach, pieces, near, share, steps, per_core, begin, span, bases, earlier, tail, *refs):
+def _cell_kernel(sources, window, reach, pieces, near, share, steps, per_core, begin, span, earlier, tail, *refs):
     code_ref, sharp_ref = refs[:2]
     refs = refs[2:]
     centre_refs, refs = (refs[:1], refs[1:]) if near else (refs[:pieces], refs[pieces:])
@@ -122,7 +139,7 @@
     cell = (code_ref[2] * per_core if near else 0) + begin
     loads = []
     for n in range(sources):
-        low = bases[n] + (0 if n % cores == 0 else span - meta_extra - reach)
+        low = 0 if n % cores == 0 else span - meta_extra - reach
         loads.append(
             pltpu.make_async_copy(
                 row_refs[n].at[pl.ds(low, reach)],
@@ -146,7 +163,7 @@
     def _():
         lines = [
             pltpu.make_async_copy(
-                row_refs[n].at[pl.ds(bases[n] + span - meta_extra, meta_extra), pl.ds(0, 128)],
+                row_refs[n].at[pl.ds(span - meta_extra, meta_extra), pl.ds(0, 128)],
                 meta_low.at[pl.ds(n * meta_extra, meta_extra)],
                 meta_sems.at[n],
             )
@@ -192,7 +209,7 @@
     mass_ref[step] = jnp.broadcast_to(mass, (mass.shape[0], 128)).T[: mass_ref.shape[1]]
     low = resp.astype(jnp.bfloat16)
     numer = jnp.dot(low, chosen, preferred_element_type=jnp.float32)
-    keep_ref[0] = numer[:share]
+    keep_ref[0] = numer[:share] + prior_mass * centre[:share].astype(jnp.float32) if near else numer[:share]
     for n, ref in enumerate(send_refs):
         at_row = pl.multiple_of(step * share, share)
         ref[pl.ds(at_row, share)] = numer[(n + 1) * share : (n + 2) * share].astype(ref.dtype)
@@ -239,7 +256,7 @@
 
 def _update_kernel(per_core, chips, piece, tail, code_ref, keep_ref, mass_ref, *refs):
     got_refs, refs = refs[: 2 * (chips - 1)], refs[2 * (chips - 1) :]
-    first_ref, others_ref, tail_ref, prior_ref, out_ref, swap_ref, lines_ref, weight = refs
+    first_ref, others_ref, tail_ref, out_ref, swap_ref, lines_ref, weight = refs
     step = pl.program_id(0)
     lines = mass_ref[:, 0, :128]
     for ref in [*got_refs[1::2], tail_ref]:
@@ -258,7 +275,7 @@
 
     def updated(at_kid):
         rows = pl.ds(pl.multiple_of(at_kid, piece), piece)
-        numer = keep_ref[0, rows] + prior_mass * prior_ref[0, rows]
+        numer = keep_ref[0, rows]
         for ref in got_refs[0::2]:
             numer = numer + ref[rows].astype(jnp.float32)
         far = jnp.where(step == 0, first_ref[rows], others_ref[rows])
@@ -271,14 +288,14 @@
     swap_ref[0, piece:, :128] = jnp.broadcast_to(mine, (8, 128))
 
 
-def _finish_kernel(per_core, piece, code_ref, _, swap_ref, lines_ref, out_ref, mass_ref, sem):
+def _finish_kernel(per_core, piece, code_ref, _, swap_ref, line_ref, lines_ref, out_ref, mass_ref, sem):
     other = 1 - code_ref[2]
     copy = pltpu.make_async_copy(
         swap_ref.at[:, pl.ds(0, piece)], out_ref.at[pl.ds(other * per_core, per_core)], sem
     )
     copy.start()
     mine = lines_ref[:per_core]
-    theirs = swap_ref[:, piece, :128]
+    theirs = line_ref[:, 0]
     lines = jnp.where(
         other == 1, jnp.concatenate([mine, theirs], axis=0), jnp.concatenate([theirs, mine], axis=0)
     )
@@ -293,10 +310,8 @@
 
 def _cell_call(code, sharp, arrays, near, row_blocks, window, reach, per_core, begin, steps, kids, share, sends, earlier, tail):
     sources = len(row_blocks)
-    row_arrays, bases = zip(*row_blocks, strict=True)
-    width = row_arrays[0].shape[1]
+    span, width = row_blocks[0].shape
     pieces = kids // (share // 2)
-    span = row_arrays[0].shape[0] // 2
     rows = sources * window
     out_shape = [
         jax.ShapeDtypeStruct((steps, share, width), jnp.float32),
@@ -307,7 +322,7 @@
     moving = lambda shape: pl.BlockSpec((1, *shape[1:]), lambda n, *_: (n, 0, 0))
     return pl.pallas_call(
         functools.partial(
-            _cell_kernel, sources, window, reach, pieces, near, share, steps, per_core, begin, span, bases, len(earlier), tail
+            _cell_kernel, sources, window, reach, pieces, near, share, steps, per_core, begin, span, len(earlier), tail
         ),
         grid_spec=pltpu.PrefetchScalarGridSpec(
             num_scalar_prefetch=2,
@@ -329,7 +344,7 @@
         out_shape=out_shape,
         compiler_params=pltpu.CompilerParams(vmem_limit_bytes=44 * 1024 * 1024),
         cost_estimate=busy,
-    )(code, sharp, *arrays, *row_arrays, *earlier)
+    )(code, sharp, *arrays, *row_blocks, *earlier)
 
 
 def on_device(frames, labels, centroids, sharpness):
@@ -416,7 +431,6 @@
     seg = lambda s, t: s * 2 + t
     first_segs = [seg(s, 1) for s in range(1, half)]
     next_segs = [seg(s, 0) for s in range(1, half)]
-    last_segs = [seg(0, 1), seg(0, 0)]
     span = own_slots + meta_extra
     block = jax.ShapeDtypeStruct((span, width), jnp.bfloat16)
     lines = cell_count * meta_extra
@@ -434,28 +448,29 @@
     segments = dict(zip(first_segs, blocks, strict=True))
 
     blocks = pl.pallas_call(
-        functools.partial(_pick_kernel, next_segs, len(next_segs)),
+        functools.partial(_pick_kernel, next_segs),
         out_shape=[block] * len(next_segs),
         compiler_params=_params(),
         cost_estimate=dear,
     )(_after(flat, first), meta, frames)
     segments.update(zip(next_segs, blocks, strict=True))
-    here = pl.pallas_call(
-        functools.partial(_pick_kernel, last_segs, 0),
-        out_shape=[jax.ShapeDtypeStruct((2 * span, width), jnp.bfloat16)],
-        compiler_params=_params(),
-        cost_estimate=dear,
-    )(_after(flat, *blocks, foreign_sharp, *around), meta, frames)[0]
-
-    here_other = hop_core(here)
-    received = {t: [hop_member(segments[seg(s, t)], s) for s in range(1, half)] for t in (1, 0)}
+    received = {1: [hop_member(segments[seg(s, 1)], s) for s in range(1, half)]}
+    here = {}
+    for t, gate in ((1, (*blocks, foreign_sharp, *around)), (0, received[1])):
+        here[t] = pl.pallas_call(
+            functools.partial(_pick_kernel, [seg(0, t)]),
+            out_shape=[block],
+            compiler_params=_params(),
+            cost_estimate=dear,
+        )(_after(flat, *gate), meta, frames)[0]
+
+    received[0] = [hop_member(segments[seg(s, 0)], s) for s in range(1, half)]
 
     def held_of(t, *gate):
-        base = 0 if t else span
-        held = [(here, base), (here_other, base)]
+        held = [here[t], hop_core(here[t])]
         for v in received[t]:
             v = _after(v, *gate)
-            held += [(v, 0), (hop_core(v), 0)]
+            held += [v, hop_core(v)]
         return held
 
     held = {1: held_of(1, *around)}
@@ -480,7 +495,7 @@
     results, totals, theirs, notes = [], [], [], []
     for t, begin, size in [(1, *part) for part in parts] + [(0, 0, per_core)]:
         if not t:
-            held[0] = held_of(0, totals[1])
+            held[0] = held_of(0, totals[0])
             notes.append(
                 pl.pallas_call(
                     _copy_kernel,
@@ -549,27 +564,9 @@
         functools.partial(_score_kernel, lines, window),
         out_shape=jax.ShapeDtypeStruct((1, rows), jnp.float32),
         compiler_params=_params(),
-        cost_estimate=cheap,
+        cost_estimate=dear,
     )(rel, off, jnp.concatenate(values, axis=0)).reshape(rows)
 
-    def prior_from(n, c, g=0):
-        return c[2], c[0] * group_count + lax.rem(c[1] + g, group_count), 0
-
-    previous = pl.pallas_call(
-        functools.partial(_prior_kernel, group_count),
-        grid_spec=pltpu.PrefetchScalarGridSpec(
-            num_scalar_prefetch=1,
-            grid=(1,),
-            in_specs=[
-                pl.BlockSpec((per_core, piece, width), functools.partial(prior_from, g=g))
-                for g in range(group_count)
-            ],
-            out_specs=pl.BlockSpec((per_core, share, width), lambda n, c: (0, 0, 0)),
-        ),
-        out_shape=jax.ShapeDtypeStruct((per_core, share, width), jnp.float32),
-        compiler_params=_params(),
-        cost_estimate=dear,
-    )(code, *([centroids] * group_count))
     theirs = [_after(v, *arrived) for v in theirs]
     one_cell = lambda block, where: pl.BlockSpec(block, where)
     whole = lambda v: pl.BlockSpec(v.shape, lambda n, c: (0,) * v.ndim)
@@ -591,7 +588,6 @@
                 one_cell((share, width), lambda n, c: (0, 0)),
                 one_cell((share, width), lambda n, c: (jnp.maximum(n - 1, 0), 0)),
                 behind(per_core - 1),
-                one_cell((1, share, width), lambda n, c: (n, 0, 0)),
             ],
             out_specs=[
                 one_cell((1, piece, width), lambda n, c: (c[2] * per_core + n, 0, 0)),
@@ -606,22 +602,31 @@
             jax.ShapeDtypeStruct((8, 128), jnp.float32),
         ],
         compiler_params=_params(),
-        cost_estimate=dear,
-    )(code, keep, mass, *got, theirs[0], theirs[1], theirs[1], previous)
+        cost_estimate=busy,
+    )(code, keep, mass, *got, theirs[0], theirs[1], theirs[1])
+    swapped = hop_core(swap)
     new_centroids, child_mass = pl.pallas_call(
         functools.partial(_finish_kernel, per_core, piece),
-        in_specs=[pl.BlockSpec(memory_space=pltpu.SMEM), anywhere]
-        + [pl.BlockSpec(memory_space=pltpu.VMEM)] * 2,
-        out_specs=[anywhere, pl.BlockSpec(memory_space=pltpu.VMEM)],
+        grid_spec=pltpu.PrefetchScalarGridSpec(
+            num_scalar_prefetch=1,
+            grid=(1,),
+            in_specs=[
+                anywhere,
+                anywhere,
+                pl.BlockSpec((per_core, 8, 128), lambda n, c: (0, piece // 8, 0)),
+                pl.BlockSpec((8, 128), lambda n, c: (0, 0)),
+            ],
+            out_specs=[anywhere, pl.BlockSpec((cells_local, piece), lambda n, c: (0, 0))],
+            scratch_shapes=[pltpu.SemaphoreType.DMA(())],
+        ),
         out_shape=[
             jax.ShapeDtypeStruct(out.shape, jnp.float32),
             jax.ShapeDtypeStruct((cells_local, piece), jnp.float32),
         ],
-        scratch_shapes=[pltpu.SemaphoreType.DMA(())],
         input_output_aliases={1: 0},
         compiler_params=_params(),
-        cost_estimate=dear,
-    )(code, out, hop_core(swap), lines_mine)
+        cost_estimate=busy,
+    )(code, out, swapped, swapped, lines_mine)
     return new_centroids, child_mass, frame_score
 
 

time: 113 us -> 111 us (0.982)
  local copies, waits for them, and re-layouts: 3.25 us -> 6.14 us
  waiting for transfers between devices: 61 us -> 58.3 us
  starting transfers between devices: 18.2 us -> 16.9 us
    ppermute x3, waiting for transfers between devices: 0.01 us -> 13.8 us  [hop_any(): return lax.ppermute(v, ('cell', 'frame'), pairs)]
    ppermute x4, waiting for transfers between devices: 24 us -> 13.5 us  [hop_partner(): lax.ppermute(v, 'cell', [(i, (i + half) % cell_count) for i in range(cell...]
    ppermute x4, waiting for transfers between devices: 16.6 us -> 10.9 us  [hop_chip(): lax.ppermute(v, 'frame', [(a * cores + c, (a + s) % chips * cores + c) fo...]
    ppermute x2, waiting for transfers between devices: 5.88 us -> 9.47 us  [hop_member(): lax.ppermute(v, 'cell', [(b * half + i, b * half + (i + s) % half) for b...]
    unnamed x12 -> x16, local copies, waits for them, and re-layouts: 1.61 us -> 4.53 us
    ppermute x4 -> x5, waiting for transfers between devices: 3.61 us -> 1.51 us  [hop_core(): return lax.ppermute(v, 'frame', [(i, i ^ 1) for i in range(frame_count)])]
    ppermute x2, waiting for transfers between devices: 10.9 us -> 9.05 us  [hop_group(): return lax.ppermute(v, 'groups', [(i, 1 - i) for i in range(2)])]
  transfers between devices with their start and end apart: 19 -> 20, of which waited for: 12 -> 12; matrix products, arithmetic and copies ran while one was open for 2% -> 3% of each run, Pallas kernels for 23% -> 21%
where the time goes in v4:
time: 111 us
  waiting for transfers between devices  58.3 us (53%)
  Pallas kernels  27.4 us (25%)
  starting transfers between devices  16.9 us (15%)
  local copies, waits for them, and re-layouts  6.14 us (6%)
  other arithmetic  1.19 us (1%)
    pallas_call x3, Pallas kernels, _cell_call(): pl.pallas_call(functools.partial(_cell_kernel, sources, window, reach, pi...  16.2 us
    ppermute x3, waiting for transfers between devices, hop_any(): return lax.ppermute(v, ('cell', 'frame'), pairs)  13.8 us
    ppermute x4, waiting for transfers between devices, hop_partner(): lax.ppermute(v, 'cell', [(i, (i + half) % cell_count) for i in range(cell...  13.5 us
    ppermute x4, waiting for transfers between devices, hop_chip(): lax.ppermute(v, 'frame', [(a * cores + c, (a + s) % chips * cores + c) fo...  10.9 us
    ppermute x2, waiting for transfers between devices, hop_member(): lax.ppermute(v, 'cell', [(b * half + i, b * half + (i + s) % half) for b...  9.47 us
    ppermute x2, waiting for transfers between devices, hop_group(): return lax.ppermute(v, 'groups', [(i, 1 - i) for i in range(2)])  9.05 us
    ppermute x4, starting transfers between devices, hop_partner(): lax.ppermute(v, 'cell', [(i, (i + half) % cell_count) for i in range(cell...  5.58 us
    unnamed x16, local copies, waits for them, and re-layouts  4.53 us
  transfers between devices with their start and end apart: 20, of which 12 were waited for; matrix products, arithmetic and copies ran while one was open for 3% of the time, Pallas kernels for 21%

profile of v4, /device:TPU:0, one launch (start us, length us, event | category | flops | bytes accessed | tf_op | source)
XLA Modules:
  0.0 110.8 jit_solution(14743416382472263300)
XLA Ops:
  0.6 4.1 %collective-permute-start = (f32[6]{0:T(128)}, f32[6]{0:T(128)S(1)}, u32[]{:S(2)}, u32[]{:S(2)}) collective-permute-start(f32[6]{0:T(128)} %refs_1_.1), channel_id=1, source_target_pairs={{0,8},{4,12},{8,0},{12,4},{1,9},{5,13},{9,1},{13,5},{2,10},{6,14},... | collective-permute-start | bytes 80 | tf_op jit(solution)/shard_map/ppermute | solution.py:396
  4.7 1.0 constant_dynamic-slice_fusion
  6.7 1.6 %copy-done.3 = bf16[1024,1024]{1,0:T(8,128)(2,1)S(1)} copy-done((bf16[1024,1024]{1,0:T(8,128)(2,1)S(1)}, bf16[1024,1024]{1,0:T(8,128)(2,1)}, u32[]{:S(2)}) %copy-start.3) | copy-done | bytes 2097176
  8.3 2.0 %shard_map.67 = (s32[1,1024]{1,0:T(1,128)S(1)}, s32[1,1024]{1,0:T(1,128)S(1)}, f32[64,128]{1,0:T(8,128)S(1)}, bf16[528,1024]{1,0:T(8,128)(2,1)S(1)}) custom-call(s32[1,1024]{1,0:T(1,128)S(1)} %fusion.12.rel_ref, bf16[1024,1024]{1,0:T(8,128)(2,1)S(1)} %copy-done.3), custom_call_target="tpu_custom_call" | custom-call | flops 20000000000 | bytes 1000000000 | tf_op jit(solution)/shard_map/pallas_call | solution.py:437
  10.3 1.9 %collective-permute-start.6 = (bf16[528,1024]{1,0:T(8,128)(2,1)S(1)}, bf16[528,1024]{1,0:T(8,128)(2,1)S(1)}, u32[]{:S(2)}, u32[]{:S(2)}) collective-permute-start(bf16[528,1024]{1,0:T(8,128)(2,1)S(1)} %get-tuple-element.44), channel_id=1, source_target_pairs={{0,4},{4,0},{8,12},{12,8},{1,5},{5,1},{9,13},{13,9},{2,6},{6,2},{1... | collective-permute-start | bytes 3244040 | tf_op jit(solution)/shard_map/ppermute | solution.py:391
  12.3 13.5 %collective-permute-done.1.refs_2_ = bf16[3,64,1024]{2,1,0:T(8,128)(2,1)S(1)} collective-permute-done((bf16[3,64,1024]{2,1,0:T(8,128)(2,1)S(1)}, bf16[3,64,1024]{2,1,0:T(8,128)(2,1)S(1)}, u32[]{:S(2)}, u32[]{:S(2)}) %collective-permute-start.1) | collective-permute-done | bytes 393248 | tf_op jit(solution)/shard_map/ppermute | solution.py:396
  25.8 1.5 %collective-permute-start.2 = (bf16[3,64,1024]{2,1,0:T(8,128)(2,1)S(1)}, bf16[3,64,1024]{2,1,0:T(8,128)(2,1)S(1)}, u32[]{:S(2)}, u32[]{:S(2)}) collective-permute-start(bf16[3,64,1024]{2,1,0:T(8,128)(2,1)S(1)} %collective-permute-done.1.refs_2_), channel_id=1, source_target_pairs={{0,16},{16,0},{1,17},{17,1},{2,18},{18,2},{3,19},{19,3},{4,20},{20... | collective-permute-start | bytes 1179656 | tf_op jit(solution)/shard_map/ppermute | solution.py:399
  27.3 1.5 %collective-permute-start.3 = (bf16[3,64,1024]{2,1,0:T(8,128)(2,1)S(1)}, bf16[3,64,1024]{2,1,0:T(8,128)(2,1)S(1)}, u32[]{:S(2)}, u32[]{:S(2)}) collective-permute-start(bf16[3,64,1024]{2,1,0:T(8,128)(2,1)S(1)} %collective-permute-done.1.refs_2_), channel_id=1, source_target_pairs={{0,2},{1,3},{2,0},{3,1},{4,6},{5,7},{6,4},{7,5},{8,10},{9,11},{10,... | collective-permute-start | bytes 1179656 | tf_op jit(solution)/shard_map/ppermute | solution.py:384
  28.8 1.2 %shard_map.68 = bf16[528,1024]{1,0:T(8,128)(2,1)S(1)} custom-call(s32[1,1024]{1,0:T(1,128)S(1)} %get-tuple-element.59.flat_ref, f32[64,128]{1,0:T(8,128)S(1)} %get-tuple-element.42.meta_ref, bf16[1024,1024]{1,0:T(8,128)(2,1)S(1)} %copy-done.4), custom_call_target="tpu_custom_call" | custom-call | flops 20000000000 | bytes 1000000000 | tf_op jit(solution)/shard_map/pallas_call | solution.py:450
  30.2 5.5 %collective-permute-done.2.refs_3_ = bf16[3,64,1024]{2,1,0:T(8,128)(2,1)S(1)} collective-permute-done((bf16[3,64,1024]{2,1,0:T(8,128)(2,1)S(1)}, bf16[3,64,1024]{2,1,0:T(8,128)(2,1)S(1)}, u32[]{:S(2)}, u32[]{:S(2)}) %collective-permute-start.2) | collective-permute-done | bytes 393248 | tf_op jit(solution)/shard_map/ppermute | solution.py:399
  35.7 1.2 %collective-permute-done.3.refs_4_ = bf16[3,64,1024]{2,1,0:T(8,128)(2,1)S(1)} collective-permute-done((bf16[3,64,1024]{2,1,0:T(8,128)(2,1)S(1)}, bf16[3,64,1024]{2,1,0:T(8,128)(2,1)S(1)}, u32[]{:S(2)}, u32[]{:S(2)}) %collective-permute-start.3) | collective-permute-done | bytes 393248 | tf_op jit(solution)/shard_map/ppermute | solution.py:384
  37.0 1.3 %shard_map.69.refs_6_ = bf16[528,1024]{1,0:T(8,128)(2,1)S(1)} custom-call(s32[1,1024]{1,0:T(1,128)S(1)} %get-tuple-element.59.flat_ref, f32[64,128]{1,0:T(8,128)S(1)} %get-tuple-element.42.meta_ref, bf16[1024,1024]{1,0:T(8,128)(2,1)S(1)} %copy-done.4), custom_call_target="tpu_custom_call" | custom-call | flops 20000000000 | bytes 1000000000 | tf_op jit(solution)/shard_map/pallas_call | solution.py:460
  38.9 5.6 %collective-permute-done.6.refs_8_ = bf16[528,1024]{1,0:T(8,128)(2,1)S(1)} collective-permute-done((bf16[528,1024]{1,0:T(8,128)(2,1)S(1)}, bf16[528,1024]{1,0:T(8,128)(2,1)S(1)}, u32[]{:S(2)}, u32[]{:S(2)}) %collective-permute-start.6) | collective-permute-done | bytes 1081376 | tf_op jit(solution)/shard_map/ppermute | solution.py:391
  44.5 1.3 %shard_map.75.refs_3_ = bf16[528,1024]{1,0:T(8,128)(2,1)S(1)} custom-call(s32[1,1024]{1,0:T(1,128)S(1)} %get-tuple-element.59.flat_ref, f32[64,128]{1,0:T(8,128)S(1)} %get-tuple-element.42.meta_ref, bf16[1024,1024]{1,0:T(8,128)(2,1)S(1)} %copy-done.4), custom_call_target="tpu_custom_call" | custom-call | flops 20000000000 | bytes 1000000000 | tf_op jit(solution)/shard_map/pallas_call | solution.py:460
  46.3 3.5 %collective-permute-done.4.refs_5_ = bf16[3,64,1024]{2,1,0:T(8,128)(2,1)S(1)} collective-permute-done((bf16[3,64,1024]{2,1,0:T(8,128)(2,1)S(1)}, bf16[3,64,1024]{2,1,0:T(8,128)(2,1)S(1)}, u32[]{:S(2)}, u32[]{:S(2)}) %collective-permute-start.4) | collective-permute-done | bytes 393248 | tf_op jit(solution)/shard_map/ppermute | solution.py:399
  49.8 4.2 %shard_map.70 = (f32[1,128,1024]{2,1,0:T(8,128)S(1)}, f32[1,8,256]{2,1,0:T(8,128)S(1)}, f32[1,8,640]{2,1,0:T(8,128)S(1)}, bf16[128,1024]{1,0:T(8,128)(2,1)S(1)}) custom-call(s32[3]{0:T(128)S(1)} %pad_add_fusion.refs_0_.code_ref, f32[6]{0:T(128)S(1)} %collective-permute-done.refs_1_, bf16[3,64,1024]{2,1,0:T(8,128)(2,1)S(1)} %collective-permute-done.1.refs_2_, ...), custom_call_target="tpu_custom_call" | custom-call | flops 20000000000 | bytes 1 | tf_op jit(solution)/shard_map/pallas_call | solution.py:323
  54.0 1.6 %collective-permute-start.8 = (bf16[128,1024]{1,0:T(8,128)(2,1)S(1)}, bf16[128,1024]{1,0:T(8,128)(2,1)S(1)}, u32[]{:S(2)}, u32[]{:S(2)}) collective-permute-start(bf16[128,1024]{1,0:T(8,128)(2,1)S(1)} %get-tuple-element.51), channel_id=1, source_target_pairs={{0,2},{1,3},{2,0},{3,1},{4,6},{5,7},{6,4},{7,5},{8,10},{9,11},{10,... | collective-permute-start | bytes 786440 | tf_op jit(solution)/shard_map/ppermute | solution.py:384
  55.6 5.1 %shard_map.72 = (f32[2,128,1024]{2,1,0:T(8,128)S(1)}, f32[2,8,256]{2,1,0:T(8,128)S(1)}, f32[2,8,640]{2,1,0:T(8,128)S(1)}, bf16[272,1024]{1,0:T(8,128)(2,1)S(1)}) custom-call(s32[3]{0:T(128)S(1)} %pad_add_fusion.refs_0_.code_ref, f32[6]{0:T(128)S(1)} %collective-permute-done.refs_1_, bf16[3,64,1024]{2,1,0:T(8,128)(2,1)S(1)} %collective-permute-done.1.refs_2_, ...), custom_call_target="tpu_custom_call" | custom-call | flops 20000000000 | bytes 1 | tf_op jit(solution)/shard_map/pallas_call | solution.py:323
  62.8 3.9 %collective-permute-done.11.refs_5_ = bf16[528,1024]{1,0:T(8,128)(2,1)S(1)} collective-permute-done((bf16[528,1024]{1,0:T(8,128)(2,1)S(1)}, bf16[528,1024]{1,0:T(8,128)(2,1)S(1)}, u32[]{:S(2)}, u32[]{:S(2)}) %collective-permute-start.11) | collective-permute-done | bytes 1081376 | tf_op jit(solution)/shard_map/ppermute | solution.py:391
  66.7 8.0 %collective-permute-done.9 = bf16[272,1024]{1,0:T(8,128)(2,1)S(1)} collective-permute-done((bf16[272,1024]{1,0:T(8,128)(2,1)S(1)}, bf16[272,1024]{1,0:T(8,128)(2,1)S(1)}, u32[]{:S(2)}, u32[]{:S(2)}) %collective-permute-start.9) | collective-permute-done | bytes 557088 | tf_op jit(solution)/shard_map/ppermute | solution.py:384
  75.6 1.3 %copy-done = bf16[6,256,1024]{2,1,0:T(8,128)(2,1)S(1)} copy-done((bf16[6,256,1024]{2,1,0:T(8,128)(2,1)S(1)}, bf16[6,256,1024]{2,1,0:T(8,128)(2,1)}, u32[]{:S(2)}) %copy-start) | copy-done | bytes 3145752
  76.9 6.9 %shard_map.76 = (f32[3,128,1024]{2,1,0:T(8,128)S(1)}, f32[3,8,256]{2,1,0:T(8,128)S(1)}, f32[3,8,640]{2,1,0:T(8,128)S(1)}, bf16[400,1024]{1,0:T(8,128)(2,1)S(1)}) custom-call(s32[3]{0:T(128)S(1)} %pad_add_fusion.refs_0_.code_ref, f32[6]{0:T(128)S(1)} %copy-done.5, bf16[6,256,1024]{2,1,0:T(8,128)(2,1)S(1)} %copy-done, ...), custom_call_target="tpu_custom_call" | custom-call | flops 20000000000 | bytes 1 | tf_op jit(solution)/shard_map/pallas_call | solution.py:323
  85.0 1.2 %collective-permute-start.18 = (f32[6,160]{1,0:T(8,128)S(1)}, f32[6,160]{1,0:T(8,128)S(1)}, u32[]{:S(2)}, u32[]{:S(2)}) collective-permute-start(f32[6,160]{1,0:T(8,128)S(1)} %get-tuple-element.75), channel_id=1, source_target_pairs={{0,4},{1,5},{2,6},{3,7},{4,0},{5,1},{6,2},{7,3},{8,12},{9,13},{10,... | collective-permute-start | bytes 11528 | tf_op jit(solution)/shard_map/ppermute | solution.py:409
  86.2 0.9 collective-permute-start.19
  87.2 1.5 %collective-permute-done.18 = f32[6,160]{1,0:T(8,128)S(1)} collective-permute-done((f32[6,160]{1,0:T(8,128)S(1)}, f32[6,160]{1,0:T(8,128)S(1)}, u32[]{:S(2)}, u32[]{:S(2)}) %collective-permute-start.18) | collective-permute-done | bytes 3872 | tf_op jit(solution)/shard_map/ppermute | solution.py:409
  88.6 12.3 %collective-permute-done.19 = f32[6,160]{1,0:T(8,128)S(1)} collective-permute-done((f32[6,160]{1,0:T(8,128)S(1)}, f32[6,160]{1,0:T(8,128)S(1)}, u32[]{:S(2)}, u32[]{:S(2)}) %collective-permute-start.19) | collective-permute-done | bytes 3872 | tf_op jit(solution)/shard_map/ppermute | solution.py:409
  101.5 1.0 collective-permute-done.13.refs_0_.refs_1_
  102.5 1.4 %copy-done.7 = f32[3,128,1024]{2,1,0:T(8,128)S(1)} copy-done((f32[3,128,1024]{2,1,0:T(8,128)S(1)}, f32[3,128,1024]{2,1,0:T(8,128)}, u32[]{:S(2)}) %copy-start.7) | copy-done | bytes 1572888
  103.9 2.4 %shard_map.77 = (f32[6,64,1024]{2,1,0:T(8,128)}, f32[3,72,1024]{2,1,0:T(8,128)S(1)}, f32[8,128]{1,0:T(8,128)S(1)}) custom-call(s32[3]{0:T(128)S(1)} %pad_add_fusion.refs_0_.code_ref, f32[3,128,1024]{2,1,0:T(8,128)S(1)} %copy-done.7, f32[3,8,256]{2,1,0:T(8,128)S(1)} %get-tuple-element.62.mass_ref, ...), custom_call_target="tpu_custom_call" | custom-call | flops 20000000000 | bytes 1 | tf_op jit(solution)/shard_map/pallas_call | solution.py:579
  106.4 0.9 shard_map.80
  107.3 1.5 %collective-permute-done.16.swap_ref.line_ref = f32[3,72,1024]{2,1,0:T(8,128)S(1)} collective-permute-done((f32[3,72,1024]{2,1,0:T(8,128)S(1)}, f32[3,72,1024]{2,1,0:T(8,128)S(1)}, u32[]{:S(2)}, u32[]{:S(2)}) %collective-permute-start.16) | collective-permute-done | bytes 884768 | tf_op jit(solution)/shard_map/ppermute | solution.py:381
  108.8 2.0 %shard_map.78 = (f32[6,64,1024]{2,1,0:T(8,128)}, f32[6,64]{1,0:T(8,128)}) custom-call(s32[3]{0:T(128)S(1)} %pad_add_fusion.refs_0_.code_ref, f32[6,64,1024]{2,1,0:T(8,128)} %get-tuple-element.66._, f32[3,72,1024]{2,1,0:T(8,128)S(1)} %collective-permute-done.16.swap_ref.line_ref, ...), custom_call_target="tpu_custom_call", output_to_operand_aliasing={{0}: (1, {})} | custom-call | flops 20000000000 | bytes 1 | tf_op jit(solution)/shard_map/pallas_call | solution.py:608
  (59 shorter events, 7.0 us)
Async XLA Ops:
  0.6 29.5 %collective-permute-start = (f32[6]{0:T(128)}, f32[6]{0:T(128)S(1)}, u32[]{:S(2)}, u32[]{:S(2)}) collective-permute-start(f32[6]{0:T(128)} %refs_1_.1), channel_id=1, source_target_pairs={{0,8},{4,12},{8,0},{12,4},{1,9},{5,13},{9,1},{13,5},{2,10},{6,14},... | collective-permute-start | bytes 80 | tf_op jit(solution)/shard_map/ppermute | solution.py:396
  5.8 20.1 %collective-permute-start.1 = (bf16[3,64,1024]{2,1,0:T(8,128)(2,1)S(1)}, bf16[3,64,1024]{2,1,0:T(8,128)(2,1)S(1)}, u32[]{:S(2)}, u32[]{:S(2)}) collective-permute-start(bf16[3,64,1024]{2,1,0:T(8,128)(2,1)S(1)} %constant_dynamic-slice_fusion), channel_id=1, source_target_pairs={{0,8},{4,12},{8,0},{12,4},{1,9},{5,13},{9,1},{13,5},{2,10},{6,14},... | collective-permute-start | bytes 1179656 | tf_op jit(solution)/shard_map/ppermute | solution.py:396
  6.7 1.6 %copy-start.3 = (bf16[1024,1024]{1,0:T(8,128)(2,1)S(1)}, bf16[1024,1024]{1,0:T(8,128)(2,1)}, u32[]{:S(2)}) copy-start(bf16[1024,1024]{1,0:T(8,128)(2,1)} %frames_ref.7) | copy-start | bytes 6291460
  8.3 2.0 %copy-start.1 = (s32[1,1024]{1,0:T(1,128)}, s32[1,1024]{1,0:T(1,128)S(1)}, u32[]{:S(2)}) copy-start(s32[1,1024]{1,0:T(1,128)S(1)} %fusion.12.rel_ref) | copy-start | bytes 12292
  8.3 20.6 %copy-start.4 = (bf16[1024,1024]{1,0:T(8,128)(2,1)S(1)}, bf16[1024,1024]{1,0:T(8,128)(2,1)}, u32[]{:S(2)}) copy-start(bf16[1024,1024]{1,0:T(8,128)(2,1)} %frames_ref.7) | copy-start | bytes 6291460
  10.3 34.2 %collective-permute-start.6 = (bf16[528,1024]{1,0:T(8,128)(2,1)S(1)}, bf16[528,1024]{1,0:T(8,128)(2,1)S(1)}, u32[]{:S(2)}, u32[]{:S(2)}) collective-permute-start(bf16[528,1024]{1,0:T(8,128)(2,1)S(1)} %get-tuple-element.44), channel_id=1, source_target_pairs={{0,4},{4,0},{8,12},{12,8},{1,5},{5,1},{9,13},{13,9},{2,6},{6,2},{1... | collective-permute-start | bytes 3244040 | tf_op jit(solution)/shard_map/ppermute | solution.py:391
  25.8 9.9 %collective-permute-start.2 = (bf16[3,64,1024]{2,1,0:T(8,128)(2,1)S(1)}, bf16[3,64,1024]{2,1,0:T(8,128)(2,1)S(1)}, u32[]{:S(2)}, u32[]{:S(2)}) collective-permute-start(bf16[3,64,1024]{2,1,0:T(8,128)(2,1)S(1)} %collective-permute-done.1.refs_2_), channel_id=1, source_target_pairs={{0,16},{16,0},{1,17},{17,1},{2,18},{18,2},{3,19},{19,3},{4,20},{20... | collective-permute-start | bytes 1179656 | tf_op jit(solution)/shard_map/ppermute | solution.py:399
  27.3 9.6 %collective-permute-start.3 = (bf16[3,64,1024]{2,1,0:T(8,128)(2,1)S(1)}, bf16[3,64,1024]{2,1,0:T(8,128)(2,1)S(1)}, u32[]{:S(2)}, u32[]{:S(2)}) collective-permute-start(bf16[3,64,1024]{2,1,0:T(8,128)(2,1)S(1)} %collective-permute-done.1.refs_2_), channel_id=1, source_target_pairs={{0,2},{1,3},{2,0},{3,1},{4,6},{5,7},{6,4},{7,5},{8,10},{9,11},{10,... | collective-permute-start | bytes 1179656 | tf_op jit(solution)/shard_map/ppermute | solution.py:384
  30.1 36.6 %collective-permute-start.11 = (bf16[528,1024]{1,0:T(8,128)(2,1)S(1)}, bf16[528,1024]{1,0:T(8,128)(2,1)S(1)}, u32[]{:S(2)}, u32[]{:S(2)}) collective-permute-start(bf16[528,1024]{1,0:T(8,128)(2,1)S(1)} %shard_map.68), channel_id=1, source_target_pairs={{0,4},{4,0},{8,12},{12,8},{1,5},{5,1},{9,13},{13,9},{2,6},{6,2},{1... | collective-permute-start | bytes 3244040 | tf_op jit(solution)/shard_map/ppermute | solution.py:391
  38.2 11.6 %collective-permute-start.5 = (bf16[528,1024]{1,0:T(8,128)(2,1)S(1)}, bf16[528,1024]{1,0:T(8,128)(2,1)S(1)}, u32[]{:S(2)}, u32[]{:S(2)}) collective-permute-start(bf16[528,1024]{1,0:T(8,128)(2,1)S(1)} %shard_map.69.refs_6_), channel_id=1, source_target_pairs={{0,1},{1,0},{2,3},{3,2},{4,5},{5,4},{6,7},{7,6},{8,9},{9,8},{10,11... | collective-permute-start | bytes 3244040 | tf_op jit(solution)/shard_map/ppermute | solution.py:381
  38.3 11.5 %collective-permute-start.4 = (bf16[3,64,1024]{2,1,0:T(8,128)(2,1)S(1)}, bf16[3,64,1024]{2,1,0:T(8,128)(2,1)S(1)}, u32[]{:S(2)}, u32[]{:S(2)}) collective-permute-start(bf16[3,64,1024]{2,1,0:T(8,128)(2,1)S(1)} %collective-permute-done.3.refs_4_), channel_id=1, source_target_pairs={{0,16},{16,0},{1,17},{17,1},{2,18},{18,2},{3,19},{19,3},{4,20},{20... | collective-permute-start | bytes 1179656 | tf_op jit(solution)/shard_map/ppermute | solution.py:399
  44.5 5.3 %collective-permute-start.7 = (bf16[528,1024]{1,0:T(8,128)(2,1)S(1)}, bf16[528,1024]{1,0:T(8,128)(2,1)S(1)}, u32[]{:S(2)}, u32[]{:S(2)}) collective-permute-start(bf16[528,1024]{1,0:T(8,128)(2,1)S(1)} %collective-permute-done.6.refs_8_), channel_id=1, source_target_pairs={{0,1},{1,0},{2,3},{3,2},{4,5},{5,4},{6,7},{7,6},{8,9},{9,8},{10,11... | collective-permute-start | bytes 3244040 | tf_op jit(solution)/shard_map/ppermute | solution.py:381
  45.8 29.9 %collective-permute-start.10 = (bf16[528,1024]{1,0:T(8,128)(2,1)S(1)}, bf16[528,1024]{1,0:T(8,128)(2,1)S(1)}, u32[]{:S(2)}, u32[]{:S(2)}) collective-permute-start(bf16[528,1024]{1,0:T(8,128)(2,1)S(1)} %shard_map.75.refs_3_), channel_id=1, source_target_pairs={{0,1},{1,0},{2,3},{3,2},{4,5},{5,4},{6,7},{7,6},{8,9},{9,8},{10,11... | collective-permute-start | bytes 3244040 | tf_op jit(solution)/shard_map/ppermute | solution.py:381
  54.0 7.9 %collective-permute-start.8 = (bf16[128,1024]{1,0:T(8,128)(2,1)S(1)}, bf16[128,1024]{1,0:T(8,128)(2,1)S(1)}, u32[]{:S(2)}, u32[]{:S(2)}) collective-permute-start(bf16[128,1024]{1,0:T(8,128)(2,1)S(1)} %get-tuple-element.51), channel_id=1, source_target_pairs={{0,2},{1,3},{2,0},{3,1},{4,6},{5,7},{6,4},{7,5},{8,10},{9,11},{10,... | collective-permute-start | bytes 786440 | tf_op jit(solution)/shard_map/ppermute | solution.py:384
  60.7 14.0 %collective-permute-start.9 = (bf16[272,1024]{1,0:T(8,128)(2,1)S(1)}, bf16[272,1024]{1,0:T(8,128)(2,1)S(1)}, u32[]{:S(2)}, u32[]{:S(2)}) collective-permute-start(bf16[272,1024]{1,0:T(8,128)(2,1)S(1)} %get-tuple-element.54), channel_id=1, source_target_pairs={{0,2},{1,3},{2,0},{3,1},{4,6},{5,7},{6,4},{7,5},{8,10},{9,11},{10,... | collective-permute-start | bytes 1671176 | tf_op jit(solution)/shard_map/ppermute | solution.py:384
  62.0 39.4 %collective-permute-start.14 = (bf16[128,1024]{1,0:T(8,128)(2,1)S(1)}, bf16[128,1024]{1,0:T(8,128)(2,1)S(1)}, u32[]{:S(2)}, u32[]{:S(2)}) collective-permute-start(bf16[128,1024]{1,0:T(8,128)(2,1)S(1)} %fusion.1), channel_id=1, source_target_pairs={{0,8},{4,12},{8,0},{12,4},{1,9},{5,13},{9,1},{13,5},{2,10},{6,14},... | collective-permute-start | bytes 786440 | tf_op jit(solution)/shard_map/ppermute | solution.py:396
  66.7 9.0 %collective-permute-start.12 = (bf16[528,1024]{1,0:T(8,128)(2,1)S(1)}, bf16[528,1024]{1,0:T(8,128)(2,1)S(1)}, u32[]{:S(2)}, u32[]{:S(2)}) collective-permute-start(bf16[528,1024]{1,0:T(8,128)(2,1)S(1)} %collective-permute-done.11.refs_5_), channel_id=1, source_target_pairs={{0,1},{1,0},{2,3},{3,2},{4,5},{5,4},{6,7},{7,6},{8,9},{9,8},{10,11... | collective-permute-start | bytes 3244040 | tf_op jit(solution)/shard_map/ppermute | solution.py:381
  75.0 1.9 %copy-start = (bf16[6,256,1024]{2,1,0:T(8,128)(2,1)S(1)}, bf16[6,256,1024]{2,1,0:T(8,128)(2,1)}, u32[]{:S(2)}) copy-start(bf16[6,256,1024]{2,1,0:T(8,128)(2,1)} %refs_2_.1) | copy-start | bytes 9437188
  75.0 1.9 %copy-start.5 = (f32[6]{0:T(128)S(1)}, f32[6]{0:T(128)}, u32[]{:S(2)}) copy-start(f32[6]{0:T(128)} %refs_1_.1) | copy-start | bytes 76
  75.0 27.5 %collective-permute-start.15 = (bf16[272,1024]{1,0:T(8,128)(2,1)S(1)}, bf16[272,1024]{1,0:T(8,128)(2,1)S(1)}, u32[]{:S(2)}, u32[]{:S(2)}) collective-permute-start(bf16[272,1024]{1,0:T(8,128)(2,1)S(1)} %pad_maximum_fusion), channel_id=1, source_target_pairs={{0,8},{4,12},{8,0},{12,4},{1,9},{5,13},{9,1},{13,5},{2,10},{6,14},... | collective-permute-start | bytes 1671176 | tf_op jit(solution)/shard_map/ppermute | solution.py:396
  83.8 1.1 %copy-start.6 = (f32[3,128,1024]{2,1,0:T(8,128)}, f32[3,128,1024]{2,1,0:T(8,128)S(1)}, u32[]{:S(2)}) copy-start(f32[3,128,1024]{2,1,0:T(8,128)S(1)} %get-tuple-element.61.keep_ref) | copy-start | bytes 4718596
  83.8 18.7 %collective-permute-start.13 = (bf16[400,1024]{1,0:T(8,128)(2,1)S(1)}, bf16[400,1024]{1,0:T(8,128)(2,1)S(1)}, u32[]{:S(2)}, u32[]{:S(2)}) collective-permute-start(bf16[400,1024]{1,0:T(8,128)(2,1)S(1)} %get-tuple-element.63), channel_id=1, source_target_pairs={{0,2},{1,3},{2,0},{3,1},{4,6},{5,7},{6,4},{7,5},{8,10},{9,11},{10,... | collective-permute-start | bytes 2457608 | tf_op jit(solution)/shard_map/ppermute | solution.py:384
  85.0 1.3 %collective-permute-start.17 = (f32[6,160]{1,0:T(8,128)S(1)}, f32[6,160]{1,0:T(8,128)S(1)}, u32[]{:S(2)}, u32[]{:S(2)}) collective-permute-start(f32[6,160]{1,0:T(8,128)S(1)} %get-tuple-element.74), channel_id=1, source_target_pairs={{0,1},{1,0},{2,3},{3,2},{4,5},{5,4},{6,7},{7,6},{8,9},{9,8},{10,11... | collective-permute-start | bytes 11528 | tf_op jit(solution)/shard_map/ppermute | solution.py:409
  85.0 3.7 %collective-permute-start.18 = (f32[6,160]{1,0:T(8,128)S(1)}, f32[6,160]{1,0:T(8,128)S(1)}, u32[]{:S(2)}, u32[]{:S(2)}) collective-permute-start(f32[6,160]{1,0:T(8,128)S(1)} %get-tuple-element.75), channel_id=1, source_target_pairs={{0,4},{1,5},{2,6},{3,7},{4,0},{5,1},{6,2},{7,3},{8,12},{9,13},{10,... | collective-permute-start | bytes 11528 | tf_op jit(solution)/shard_map/ppermute | solution.py:409
  86.2 14.7 %collective-permute-start.19 = (f32[6,160]{1,0:T(8,128)S(1)}, f32[6,160]{1,0:T(8,128)S(1)}, u32[]{:S(2)}, u32[]{:S(2)}) collective-permute-start(f32[6,160]{1,0:T(8,128)S(1)} %get-tuple-element.76), channel_id=1, source_target_pairs={{0,5},{1,4},{2,7},{3,6},{4,1},{5,0},{6,3},{7,2},{8,13},{9,12},{10,... | collective-permute-start | bytes 11528 | tf_op jit(solution)/shard_map/ppermute | solution.py:409
  102.5 1.4 %copy-start.7 = (f32[3,128,1024]{2,1,0:T(8,128)S(1)}, f32[3,128,1024]{2,1,0:T(8,128)}, u32[]{:S(2)}) copy-start(f32[3,128,1024]{2,1,0:T(8,128)} %copy-done.6) | copy-start | bytes 4718596
  103.9 2.4 %copy-start.2 = (s32[1,1024]{1,0:T(1,128)S(1)}, s32[1,1024]{1,0:T(1,128)}, u32[]{:S(2)}) copy-start(s32[1,1024]{1,0:T(1,128)} %copy-done.1) | copy-start | bytes 12292
  106.4 2.4 %collective-permute-start.16 = (f32[3,72,1024]{2,1,0:T(8,128)S(1)}, f32[3,72,1024]{2,1,0:T(8,128)S(1)}, u32[]{:S(2)}, u32[]{:S(2)}) collective-permute-start(f32[3,72,1024]{2,1,0:T(8,128)S(1)} %get-tuple-element.67), channel_id=1, source_target_pairs={{0,1},{1,0},{2,3},{3,2},{4,5},{5,4},{6,7},{7,6},{8,9},{9,8},{10,11... | collective-permute-start | bytes 2654216 | tf_op jit(solution)/shard_map/ppermute | solution.py:381

commit v5 on v4

--- a/solution.py
+++ b/solution.py
@@ -126,17 +126,16 @@
         refs[-1][:, g * size : (g + 1) * size] = refs[g][...].astype(jnp.float32)
 
 
-def _cell_kernel(sources, window, reach, pieces, near, share, steps, per_core, begin, span, earlier, tail, *refs):
+def _cell_kernel(sources, window, reach, pieces, places, near, share, steps, per_core, begin, span, earlier, tail, *refs):
     code_ref, sharp_ref = refs[:2]
     refs = refs[2:]
-    centre_refs, refs = (refs[:1], refs[1:]) if near else (refs[:pieces], refs[pieces:])
+    centre_refs, refs = refs[: len(places)], refs[len(places) :]
     piece = share // 2
     row_refs, refs = refs[:sources], refs[sources:]
     earlier_refs, refs = refs[:earlier], refs[earlier:]
     keep_ref, mass_ref, score_ref = refs[:3]
     send_refs, (held, centres, sems, meta_low, meta_wide, meta_ref, meta_sems) = refs[3:-7], refs[-7:]
     step = pl.program_id(0)
-    cell = (code_ref[2] * per_core if near else 0) + begin
     loads = []
     for n in range(sources):
         low = 0 if n % cores == 0 else span - meta_extra - reach
@@ -147,17 +146,15 @@
                 sems.at[n],
             )
         )
-    for n in range(pieces):
-        s, g = n // 2, n % 2
-        if near:
-            chip = lax.rem(code_ref[0] + s, pieces // 2)
-            kid = (chip * 2 + lax.rem(code_ref[1] + g, 2)) * piece
-            source = centre_refs[0].at[pl.ds(cell, steps), pl.ds(pl.multiple_of(kid, piece), piece)]
-        else:
-            source = centre_refs[n].at[pl.ds(begin, steps)]
-        loads.append(
-            pltpu.make_async_copy(source, centres.at[:, pl.ds(n * piece, piece)], sems.at[sources + n])
-        )
+    if not near:
+        for n, low in enumerate(places):
+            loads.append(
+                pltpu.make_async_copy(
+                    centre_refs[n].at[pl.ds(begin, steps)],
+                    centres.at[:, pl.ds(low, centre_refs[n].shape[1])],
+                    sems.at[sources + n],
+                )
+            )
 
     @pl.when(step == 0)
     def _():
@@ -183,7 +180,15 @@
     def entry(n, field):
         return meta_ref[n * meta_extra + (n % cores) * per_core + begin + step, field]
 
-    centre = centres[step]
+    if near:
+        found = []
+        for n in range(pieces):
+            chip = lax.rem(code_ref[0] + n // 2, pieces // 2)
+            kid = (chip * 2 + lax.rem(code_ref[1] + n % 2, 2)) * piece
+            found.append(centre_refs[0][0, pl.ds(pl.multiple_of(kid, piece), piece)])
+        centre = jnp.concatenate(found, axis=0)
+    else:
+        centre = centres[step]
     wide = centre.astype(jnp.float32)
     half_norm = 0.5 * jnp.sum(wide * wide, axis=1, keepdims=True)
     slot = lax.broadcasted_iota(jnp.int32, (1, sources * window), 1)
@@ -254,9 +259,9 @@
     return lax.optimization_barrier((value, *others))[0]
 
 
-def _update_kernel(per_core, chips, piece, tail, code_ref, keep_ref, mass_ref, *refs):
+def _update_kernel(per_core, chips, piece, mine, code_ref, keep_ref, mass_ref, *refs):
     got_refs, refs = refs[: 2 * (chips - 1)], refs[2 * (chips - 1) :]
-    first_ref, others_ref, tail_ref, out_ref, swap_ref, lines_ref, weight = refs
+    (first_ref, others_ref, tail_ref), out_ref, weight = refs[:3], refs[3], refs[-1]
     step = pl.program_id(0)
     lines = mass_ref[:, 0, :128]
     for ref in [*got_refs[1::2], tail_ref]:
@@ -264,28 +269,25 @@
         for n in range(3):
             lines = lines + rows[n * per_core : (n + 1) * per_core]
     line = lax.broadcasted_iota(jnp.int32, lines.shape, 0)
-    mine = jnp.sum(jnp.where(line == step, lines, 0.0), axis=0, keepdims=True)
-    weight[...] = jnp.broadcast_to(1.0 / (mine + prior_mass), (128, 128)).T
-
-    @pl.when(step == 0)
-    def _():
-        lines_ref[...] = jnp.concatenate(
-            [lines, jnp.zeros((lines_ref.shape[0] - per_core, 128), jnp.float32)], axis=0
-        )
-
-    def updated(at_kid):
-        rows = pl.ds(pl.multiple_of(at_kid, piece), piece)
-        numer = keep_ref[0, rows]
-        for ref in got_refs[0::2]:
-            numer = numer + ref[rows].astype(jnp.float32)
-        far = jnp.where(step == 0, first_ref[rows], others_ref[rows])
-        return (numer + far.astype(jnp.float32)) * weight[rows, :1]
-
-    here = lax.rem(code_ref[2] + code_ref[1], 2) * piece
-    out_ref[0] = updated(here)
-    swap_ref[0, :piece] = updated(piece - here)
-    swap_ref[0, piece:] = jnp.zeros((8, swap_ref.shape[2]), jnp.float32)
-    swap_ref[0, piece:, :128] = jnp.broadcast_to(mine, (8, 128))
+    mass = jnp.sum(jnp.where(line == step, lines, 0.0), axis=0, keepdims=True)
+    weight[...] = jnp.broadcast_to(1.0 / (mass + prior_mass), (128, 128)).T
+    numer = keep_ref[0]
+    for ref in got_refs[0::2]:
+        numer = numer + ref[...].astype(jnp.float32)
+    far = jnp.where(step == 0, first_ref[...], others_ref[...])
+    low = lax.rem((code_ref[2] if mine else 1 - code_ref[2]) + code_ref[1], 2) * piece
+    numer = numer + far.astype(jnp.float32)
+    out_ref[0, :piece] = numer * weight[pl.ds(pl.multiple_of(low, piece), piece), :1]
+    if not mine:
+        out_ref[0, piece:] = jnp.zeros((8, out_ref.shape[2]), jnp.float32)
+        out_ref[0, piece:, :128] = jnp.broadcast_to(mass, (8, 128))
+        lines_ref = refs[4]
+
+        @pl.when(step == 0)
+        def _():
+            lines_ref[...] = jnp.concatenate(
+                [lines, jnp.zeros((lines_ref.shape[0] - per_core, 128), jnp.float32)], axis=0
+            )
 
 
 def _finish_kernel(per_core, piece, code_ref, _, swap_ref, line_ref, lines_ref, out_ref, mass_ref, sem):
@@ -312,6 +314,7 @@
     sources = len(row_blocks)
     span, width = row_blocks[0].shape
     pieces = kids // (share // 2)
+    arrays, places = zip(*arrays, strict=True)
     rows = sources * window
     out_shape = [
         jax.ShapeDtypeStruct((steps, share, width), jnp.float32),
@@ -322,19 +325,25 @@
     moving = lambda shape: pl.BlockSpec((1, *shape[1:]), lambda n, *_: (n, 0, 0))
     return pl.pallas_call(
         functools.partial(
-            _cell_kernel, sources, window, reach, pieces, near, share, steps, per_core, begin, span, len(earlier), tail
+            _cell_kernel, sources, window, reach, pieces, places, near, share, steps, per_core, begin, span, len(earlier), tail
         ),
         grid_spec=pltpu.PrefetchScalarGridSpec(
             num_scalar_prefetch=2,
             grid=(steps,),
-            in_specs=[anywhere] * (len(arrays) + sources) + [fixed(v.shape) for v in earlier],
+            in_specs=(
+                [pl.BlockSpec((1, kids, width), lambda n, c, _: (c[2] * per_core + begin + n, 0, 0))]
+                if near
+                else [anywhere] * len(arrays)
+            )
+            + [anywhere] * sources
+            + [fixed(v.shape) for v in earlier],
             out_specs=[
                 (moving if n in (0, 2) else fixed)(o.shape) for n, o in enumerate(out_shape)
             ],
             scratch_shapes=[
                 pltpu.VMEM((sources, reach, width), jnp.bfloat16),
-                pltpu.VMEM((steps, kids, width), jnp.bfloat16),
-                pltpu.SemaphoreType.DMA((sources + pieces,)),
+                pltpu.VMEM((1 if near else steps, kids, width), jnp.bfloat16),
+                pltpu.SemaphoreType.DMA((sources + len(places),)),
                 pltpu.VMEM((sources * meta_extra, 128), jnp.bfloat16),
                 pltpu.VMEM((sources * meta_extra, 128), jnp.int32),
                 pltpu.SMEM((sources * meta_extra, 128), jnp.int32),
@@ -418,8 +427,16 @@
         )
     )
     by_chip = [first] + [hop_chip(first, -s) for s in range(1, chips)]
-    foreign_pieces = [v for c in by_chip for v in (c, hop_group(c))]
-    around = by_chip[1:] + foreign_pieces[1:2]
+    by_group = hop_group(first)
+    around = [*by_chip[1:], by_group]
+    part = piece // 2
+    foreign_pieces = [(first, 0), (by_group, piece)]
+    for s in range(1, chips):
+        foreign_pieces += [
+            (by_chip[s], s * share),
+            (hop_group(by_chip[s][:, :part]), s * share + piece),
+            (hop_chip(by_group[:, part:], -s), s * share + piece + part),
+        ]
 
     label = labels.reshape(1, rows)
     owner, local = label // cells_local, label % cells_local
@@ -509,7 +526,7 @@
         extra = 0 if t and begin + size < per_core else tail
         results.append(
             _cell_call(
-                code_here, foreign_sharp if t else sharpness, foreign_pieces if t else [centroids],
+                code_here, foreign_sharp if t else sharpness, foreign_pieces if t else [(centroids, 0)],
                 not t, held[t], window, reach, per_core,
                 begin, size, kids, share, chips - 1, earlier if extra else [], extra,
             )
@@ -572,38 +589,53 @@
     whole = lambda v: pl.BlockSpec(v.shape, lambda n, c: (0,) * v.ndim)
     behind = lambda steps: pl.BlockSpec((tail, 128), lambda n, c: (steps * share // tail, 0))
     keep, mass = results[-1][:2]
-    got, got_specs = [], []
-    for v in arrived:
-        got += [v, v]
-        got_specs += [one_cell((share, width), lambda n, c: (n, 0)), behind(per_core)]
-    out, swap, lines_mine = pl.pallas_call(
-        functools.partial(_update_kernel, per_core, chips, piece, tail),
-        grid_spec=pltpu.PrefetchScalarGridSpec(
-            num_scalar_prefetch=1,
-            grid=(per_core,),
-            in_specs=[
-                one_cell((1, share, width), lambda n, c: (n, 0, 0)),
-                whole(mass),
-                *got_specs,
-                one_cell((share, width), lambda n, c: (0, 0)),
-                one_cell((share, width), lambda n, c: (jnp.maximum(n - 1, 0), 0)),
-                behind(per_core - 1),
-            ],
-            out_specs=[
-                one_cell((1, piece, width), lambda n, c: (c[2] * per_core + n, 0, 0)),
+
+    def update(mine):
+        def part(c):
+            return lax.rem((c[2] if mine else 1 - c[2]) + c[1], 2)
+
+        got, got_specs = [], []
+        for v in arrived:
+            got += [v, v]
+            got_specs += [
+                one_cell((piece, width), lambda n, c: (2 * n + part(c), 0)),
+                behind(per_core),
+            ]
+        if mine:
+            out_specs = [one_cell((1, piece, width), lambda n, c: (c[2] * per_core + n, 0, 0))]
+            out_shape = [jax.ShapeDtypeStruct((cells_local, piece, width), jnp.float32)]
+        else:
+            out_specs = [
                 one_cell((1, piece + 8, width), lambda n, c: (n, 0, 0)),
                 pl.BlockSpec((8, 128), lambda n, c: (0, 0)),
-            ],
-            scratch_shapes=[pltpu.VMEM((128, 128), jnp.float32)],
-        ),
-        out_shape=[
-            jax.ShapeDtypeStruct((cells_local, piece, width), jnp.float32),
-            jax.ShapeDtypeStruct((per_core, piece + 8, width), jnp.float32),
-            jax.ShapeDtypeStruct((8, 128), jnp.float32),
-        ],
-        compiler_params=_params(),
-        cost_estimate=busy,
-    )(code, keep, mass, *got, theirs[0], theirs[1], theirs[1])
+            ]
+            out_shape = [
+                jax.ShapeDtypeStruct((per_core, piece + 8, width), jnp.float32),
+                jax.ShapeDtypeStruct((8, 128), jnp.float32),
+            ]
+        return pl.pallas_call(
+            functools.partial(_update_kernel, per_core, chips, piece, mine),
+            grid_spec=pltpu.PrefetchScalarGridSpec(
+                num_scalar_prefetch=1,
+                grid=(per_core,),
+                in_specs=[
+                    one_cell((1, piece, width), lambda n, c: (n, part(c), 0)),
+                    whole(mass),
+                    *got_specs,
+                    one_cell((piece, width), lambda n, c: (part(c), 0)),
+                    one_cell((piece, width), lambda n, c: (2 * jnp.maximum(n - 1, 0) + part(c), 0)),
+                    behind(per_core - 1),
+                ],
+                out_specs=out_specs,
+                scratch_shapes=[pltpu.VMEM((128, 128), jnp.float32)],
+            ),
+            out_shape=out_shape,
+            compiler_params=_params(),
+            cost_estimate=busy,
+        )(code, keep, mass, *got, theirs[0], theirs[1], theirs[1])
+
+    swap, lines_mine = update(False)
+    (out,) = update(True)
     swapped = hop_core(swap)
     new_centroids, child_mass = pl.pallas_call(
         functools.partial(_finish_kernel, per_core, piece),

time: 111 us -> 107 us (0.964)
  waiting for transfers between devices: 58.3 us -> 49.3 us
  starting transfers between devices: 16.9 us -> 23.7 us
  local copies, waits for them, and re-layouts: 6.14 us -> 3.51 us
    ppermute x4 -> x5, waiting for transfers between devices: 10.9 us -> 23.3 us  [hop_chip(): lax.ppermute(v, 'frame', [(a * cores + c, (a + s) % chips * cores + c) fo...]
    ppermute x3, waiting for transfers between devices: 13.8 us -> 2.14 us  [hop_any(): return lax.ppermute(v, ('cell', 'frame'), pairs)]
    ppermute x2, waiting for transfers between devices: 9.05 us -> 0.01 us  [hop_group(): return lax.ppermute(v, 'groups', [(i, 1 - i) for i in range(2)])]
    ppermute x4, starting transfers between devices: 5.58 us -> 9.57 us  [hop_partner(): lax.ppermute(v, 'cell', [(i, (i + half) % cell_count) for i in range(cell...]
    unnamed x16, local copies, waits for them, and re-layouts: 4.53 us -> 1.86 us
    ppermute x4 -> x5, starting transfers between devices: 4.41 us -> 5.96 us  [hop_chip(): lax.ppermute(v, 'frame', [(a * cores + c, (a + s) % chips * cores + c) fo...]
    pallas_call x1 -> x2, Pallas kernels: 2.42 us -> 3.66 us  [update(): pl.pallas_call(functools.partial(_update_kernel, per_core, chips, piece,...]
    ppermute x3, starting transfers between devices: 2.18 us -> 3.41 us  [hop_any(): return lax.ppermute(v, ('cell', 'frame'), pairs)]
  transfers between devices with their start and end apart: 20 -> 21, of which waited for: 12 -> 10; matrix products, arithmetic and copies ran while one was open for 3% -> 3% of each run, Pallas kernels for 21% -> 24%
where the time goes in v5:
time: 107 us
  waiting for transfers between devices  49.3 us (46%)
  Pallas kernels  28.5 us (27%)
  starting transfers between devices  23.7 us (22%)
  local copies, waits for them, and re-layouts  3.51 us (3%)
  other arithmetic  1.18 us (1%)
    ppermute x5, waiting for transfers between devices, hop_chip(): lax.ppermute(v, 'frame', [(a * cores + c, (a + s) % chips * cores + c) fo...  23.3 us
    pallas_call x3, Pallas kernels, _cell_call(): pl.pallas_call(functools.partial(_cell_kernel, sources, window, reach, pi...  16 us
    ppermute x4, waiting for transfers between devices, hop_partner(): lax.ppermute(v, 'cell', [(i, (i + half) % cell_count) for i in range(cell...  13.5 us
    ppermute x4, starting transfers between devices, hop_partner(): lax.ppermute(v, 'cell', [(i, (i + half) % cell_count) for i in range(cell...  9.57 us
    ppermute x2, waiting for transfers between devices, hop_member(): lax.ppermute(v, 'cell', [(b * half + i, b * half + (i + s) % half) for b...  9.42 us
    ppermute x5, starting transfers between devices, hop_chip(): lax.ppermute(v, 'frame', [(a * cores + c, (a + s) % chips * cores + c) fo...  5.96 us
    pallas_call x2, Pallas kernels, update(): pl.pallas_call(functools.partial(_update_kernel, per_core, chips, piece,...  3.66 us
    ppermute x3, starting transfers between devices, hop_any(): return lax.ppermute(v, ('cell', 'frame'), pairs)  3.41 us
  transfers between devices with their start and end apart: 21, of which 10 were waited for; matrix products, arithmetic and copies ran while one was open for 3% of the time, Pallas kernels for 24%

profile of v5, /device:TPU:0, one launch (start us, length us, event | category | flops | bytes accessed | tf_op | source)
XLA Modules:
  0.0 107.1 jit_solution(4682064654587293169)
XLA Ops:
  0.6 4.1 %collective-permute-start = (f32[6]{0:T(128)}, f32[6]{0:T(128)S(1)}, u32[]{:S(2)}, u32[]{:S(2)}) collective-permute-start(f32[6]{0:T(128)} %refs_1_.1), channel_id=1, source_target_pairs={{0,8},{4,12},{8,0},{12,4},{1,9},{5,13},{9,1},{13,5},{2,10},{6,14},... | collective-permute-start | bytes 80 | tf_op jit(solution)/shard_map/ppermute | solution.py:405
  4.7 1.0 constant_dynamic-slice_fusion
  6.7 1.6 %copy-done.3 = bf16[1024,1024]{1,0:T(8,128)(2,1)S(1)} copy-done((bf16[1024,1024]{1,0:T(8,128)(2,1)S(1)}, bf16[1024,1024]{1,0:T(8,128)(2,1)}, u32[]{:S(2)}) %copy-start.3) | copy-done | bytes 2097176
  8.3 2.0 %shard_map.67 = (s32[1,1024]{1,0:T(1,128)S(1)}, s32[1,1024]{1,0:T(1,128)S(1)}, f32[64,128]{1,0:T(8,128)S(1)}, bf16[528,1024]{1,0:T(8,128)(2,1)S(1)}) custom-call(s32[1,1024]{1,0:T(1,128)S(1)} %fusion.12.rel_ref, bf16[1024,1024]{1,0:T(8,128)(2,1)S(1)} %copy-done.3), custom_call_target="tpu_custom_call" | custom-call | flops 20000000000 | bytes 1000000000 | tf_op jit(solution)/shard_map/pallas_call | solution.py:454
  10.3 1.9 %collective-permute-start.7 = (bf16[528,1024]{1,0:T(8,128)(2,1)S(1)}, bf16[528,1024]{1,0:T(8,128)(2,1)S(1)}, u32[]{:S(2)}, u32[]{:S(2)}) collective-permute-start(bf16[528,1024]{1,0:T(8,128)(2,1)S(1)} %get-tuple-element.43), channel_id=1, source_target_pairs={{0,4},{4,0},{8,12},{12,8},{1,5},{5,1},{9,13},{13,9},{2,6},{6,2},{1... | collective-permute-start | bytes 3244040 | tf_op jit(solution)/shard_map/ppermute | solution.py:400
  12.3 13.5 %collective-permute-done.1.refs_2_ = bf16[3,64,1024]{2,1,0:T(8,128)(2,1)S(1)} collective-permute-done((bf16[3,64,1024]{2,1,0:T(8,128)(2,1)S(1)}, bf16[3,64,1024]{2,1,0:T(8,128)(2,1)S(1)}, u32[]{:S(2)}, u32[]{:S(2)}) %collective-permute-start.1) | collective-permute-done | bytes 393248 | tf_op jit(solution)/shard_map/ppermute | solution.py:405
  25.8 1.5 %collective-permute-start.2 = (bf16[3,64,1024]{2,1,0:T(8,128)(2,1)S(1)}, bf16[3,64,1024]{2,1,0:T(8,128)(2,1)S(1)}, u32[]{:S(2)}, u32[]{:S(2)}) collective-permute-start(bf16[3,64,1024]{2,1,0:T(8,128)(2,1)S(1)} %collective-permute-done.1.refs_2_), channel_id=1, source_target_pairs={{0,16},{16,0},{1,17},{17,1},{2,18},{18,2},{3,19},{19,3},{4,20},{20... | collective-permute-start | bytes 1179656 | tf_op jit(solution)/shard_map/ppermute | solution.py:408
  27.3 1.5 %collective-permute-start.3 = (bf16[3,64,1024]{2,1,0:T(8,128)(2,1)S(1)}, bf16[3,64,1024]{2,1,0:T(8,128)(2,1)S(1)}, u32[]{:S(2)}, u32[]{:S(2)}) collective-permute-start(bf16[3,64,1024]{2,1,0:T(8,128)(2,1)S(1)} %collective-permute-done.1.refs_2_), channel_id=1, source_target_pairs={{0,2},{1,3},{2,0},{3,1},{4,6},{5,7},{6,4},{7,5},{8,10},{9,11},{10,... | collective-permute-start | bytes 1179656 | tf_op jit(solution)/shard_map/ppermute | solution.py:393
  28.8 1.2 %shard_map.68 = bf16[528,1024]{1,0:T(8,128)(2,1)S(1)} custom-call(s32[1,1024]{1,0:T(1,128)S(1)} %get-tuple-element.58.flat_ref, f32[64,128]{1,0:T(8,128)S(1)} %get-tuple-element.41.meta_ref, bf16[1024,1024]{1,0:T(8,128)(2,1)S(1)} %copy-done.4), custom_call_target="tpu_custom_call" | custom-call | flops 20000000000 | bytes 1000000000 | tf_op jit(solution)/shard_map/pallas_call | solution.py:467
  30.2 6.8 %collective-permute-done.3.refs_4_ = bf16[3,64,1024]{2,1,0:T(8,128)(2,1)S(1)} collective-permute-done((bf16[3,64,1024]{2,1,0:T(8,128)(2,1)S(1)}, bf16[3,64,1024]{2,1,0:T(8,128)(2,1)S(1)}, u32[]{:S(2)}, u32[]{:S(2)}) %collective-permute-start.3) | collective-permute-done | bytes 393248 | tf_op jit(solution)/shard_map/ppermute | solution.py:393
  37.6 1.6 %collective-permute-start.5 = (bf16[3,32,1024]{2,1,0:T(8,128)(2,1)S(1)}, bf16[3,32,1024]{2,1,0:T(8,128)(2,1)S(1)}, u32[]{:S(2)}, u32[]{:S(2)}) collective-permute-start(bf16[3,32,1024]{2,1,0:T(8,128)(2,1)S(1)} %slice.71), channel_id=1, source_target_pairs={{0,2},{1,3},{2,0},{3,1},{4,6},{5,7},{6,4},{7,5},{8,10},{9,11},{10,... | collective-permute-start | bytes 589832 | tf_op jit(solution)/shard_map/ppermute | solution.py:393
  39.1 1.3 %shard_map.69.refs_7_ = bf16[528,1024]{1,0:T(8,128)(2,1)S(1)} custom-call(s32[1,1024]{1,0:T(1,128)S(1)} %get-tuple-element.58.flat_ref, f32[64,128]{1,0:T(8,128)S(1)} %get-tuple-element.41.meta_ref, bf16[1024,1024]{1,0:T(8,128)(2,1)S(1)} %copy-done.4), custom_call_target="tpu_custom_call" | custom-call | flops 20000000000 | bytes 1000000000 | tf_op jit(solution)/shard_map/pallas_call | solution.py:477
  40.5 4.0 %collective-permute-done.7.refs_9_ = bf16[528,1024]{1,0:T(8,128)(2,1)S(1)} collective-permute-done((bf16[528,1024]{1,0:T(8,128)(2,1)S(1)}, bf16[528,1024]{1,0:T(8,128)(2,1)S(1)}, u32[]{:S(2)}, u32[]{:S(2)}) %collective-permute-start.7) | collective-permute-done | bytes 1081376 | tf_op jit(solution)/shard_map/ppermute | solution.py:400
  44.5 1.3 %shard_map.75.refs_3_ = bf16[528,1024]{1,0:T(8,128)(2,1)S(1)} custom-call(s32[1,1024]{1,0:T(1,128)S(1)} %get-tuple-element.58.flat_ref, f32[64,128]{1,0:T(8,128)S(1)} %get-tuple-element.41.meta_ref, bf16[1024,1024]{1,0:T(8,128)(2,1)S(1)} %copy-done.4), custom_call_target="tpu_custom_call" | custom-call | flops 20000000000 | bytes 1000000000 | tf_op jit(solution)/shard_map/pallas_call | solution.py:477
  46.4 0.9 collective-permute-done.8.refs_10_
  47.2 4.2 %shard_map.70 = (f32[1,128,1024]{2,1,0:T(8,128)S(1)}, f32[1,8,256]{2,1,0:T(8,128)S(1)}, f32[1,8,640]{2,1,0:T(8,128)S(1)}, bf16[128,1024]{1,0:T(8,128)(2,1)S(1)}) custom-call(s32[3]{0:T(128)S(1)} %pad_add_fusion.refs_0_.code_ref, f32[6]{0:T(128)S(1)} %collective-permute-done.refs_1_, bf16[3,64,1024]{2,1,0:T(8,128)(2,1)S(1)} %collective-permute-done.1.refs_2_, ...), custom_call_target="tpu_custom_call" | custom-call | flops 20000000000 | bytes 1 | tf_op jit(solution)/shard_map/pallas_call | solution.py:326
  51.4 1.8 %collective-permute-start.9 = (bf16[128,1024]{1,0:T(8,128)(2,1)S(1)}, bf16[128,1024]{1,0:T(8,128)(2,1)S(1)}, u32[]{:S(2)}, u32[]{:S(2)}) collective-permute-start(bf16[128,1024]{1,0:T(8,128)(2,1)S(1)} %get-tuple-element.50), channel_id=1, source_target_pairs={{0,2},{1,3},{2,0},{3,1},{4,6},{5,7},{6,4},{7,5},{8,10},{9,11},{10,... | collective-permute-start | bytes 786440 | tf_op jit(solution)/shard_map/ppermute | solution.py:393
  53.2 5.3 %shard_map.72 = (f32[2,128,1024]{2,1,0:T(8,128)S(1)}, f32[2,8,256]{2,1,0:T(8,128)S(1)}, f32[2,8,640]{2,1,0:T(8,128)S(1)}, bf16[272,1024]{1,0:T(8,128)(2,1)S(1)}) custom-call(s32[3]{0:T(128)S(1)} %pad_add_fusion.refs_0_.code_ref, f32[6]{0:T(128)S(1)} %collective-permute-done.refs_1_, bf16[3,64,1024]{2,1,0:T(8,128)(2,1)S(1)} %collective-permute-done.1.refs_2_, ...), custom_call_target="tpu_custom_call" | custom-call | flops 20000000000 | bytes 1 | tf_op jit(solution)/shard_map/pallas_call | solution.py:326
  58.9 1.0 collective-permute-done.9
  59.9 2.9 %collective-permute-start.15 = (bf16[128,1024]{1,0:T(8,128)(2,1)S(1)}, bf16[128,1024]{1,0:T(8,128)(2,1)S(1)}, u32[]{:S(2)}, u32[]{:S(2)}) collective-permute-start(bf16[128,1024]{1,0:T(8,128)(2,1)S(1)} %fusion.1), channel_id=1, source_target_pairs={{0,8},{4,12},{8,0},{12,4},{1,9},{5,13},{9,1},{13,5},{2,10},{6,14},... | collective-permute-start | bytes 786440 | tf_op jit(solution)/shard_map/ppermute | solution.py:405
  62.8 5.4 %collective-permute-done.12.refs_5_ = bf16[528,1024]{1,0:T(8,128)(2,1)S(1)} collective-permute-done((bf16[528,1024]{1,0:T(8,128)(2,1)S(1)}, bf16[528,1024]{1,0:T(8,128)(2,1)S(1)}, u32[]{:S(2)}, u32[]{:S(2)}) %collective-permute-start.12) | collective-permute-done | bytes 1081376 | tf_op jit(solution)/shard_map/ppermute | solution.py:400
  68.2 4.8 %collective-permute-done.10 = bf16[272,1024]{1,0:T(8,128)(2,1)S(1)} collective-permute-done((bf16[272,1024]{1,0:T(8,128)(2,1)S(1)}, bf16[272,1024]{1,0:T(8,128)(2,1)S(1)}, u32[]{:S(2)}, u32[]{:S(2)}) %collective-permute-start.10) | collective-permute-done | bytes 557088 | tf_op jit(solution)/shard_map/ppermute | solution.py:393
  73.3 2.5 %collective-permute-start.16 = (bf16[272,1024]{1,0:T(8,128)(2,1)S(1)}, bf16[272,1024]{1,0:T(8,128)(2,1)S(1)}, u32[]{:S(2)}, u32[]{:S(2)}) collective-permute-start(bf16[272,1024]{1,0:T(8,128)(2,1)S(1)} %pad_maximum_fusion), channel_id=1, source_target_pairs={{0,8},{4,12},{8,0},{12,4},{1,9},{5,13},{9,1},{13,5},{2,10},{6,14},... | collective-permute-start | bytes 1671176 | tf_op jit(solution)/shard_map/ppermute | solution.py:405
  75.8 6.5 %shard_map.76 = (f32[3,128,1024]{2,1,0:T(8,128)S(1)}, f32[3,8,256]{2,1,0:T(8,128)S(1)}, f32[3,8,640]{2,1,0:T(8,128)S(1)}, bf16[400,1024]{1,0:T(8,128)(2,1)S(1)}) custom-call(s32[3]{0:T(128)S(1)} %pad_add_fusion.refs_0_.code_ref, f32[6]{0:T(128)S(1)} %copy-done.5, bf16[6,256,1024]{2,1,0:T(8,128)(2,1)S(1)} %copy-done, ...), custom_call_target="tpu_custom_call" | custom-call | flops 20000000000 | bytes 1 | tf_op jit(solution)/shard_map/pallas_call | solution.py:326
  83.5 2.5 %collective-permute-start.19 = (f32[6,160]{1,0:T(8,128)S(1)}, f32[6,160]{1,0:T(8,128)S(1)}, u32[]{:S(2)}, u32[]{:S(2)}) collective-permute-start(f32[6,160]{1,0:T(8,128)S(1)} %get-tuple-element.73), channel_id=1, source_target_pairs={{0,4},{1,5},{2,6},{3,7},{4,0},{5,1},{6,2},{7,3},{8,12},{9,13},{10,... | collective-permute-start | bytes 11528 | tf_op jit(solution)/shard_map/ppermute | solution.py:418
  86.0 0.9 collective-permute-start.20
  87.6 1.4 %collective-permute-done.20 = f32[6,160]{1,0:T(8,128)S(1)} collective-permute-done((f32[6,160]{1,0:T(8,128)S(1)}, f32[6,160]{1,0:T(8,128)S(1)}, u32[]{:S(2)}, u32[]{:S(2)}) %collective-permute-start.20) | collective-permute-done | bytes 3872 | tf_op jit(solution)/shard_map/ppermute | solution.py:418
  89.6 0.9 shard_map.81
  90.5 10.8 %collective-permute-done.14.refs_0_.refs_1_ = bf16[400,1024]{1,0:T(8,128)(2,1)S(1)} collective-permute-done((bf16[400,1024]{1,0:T(8,128)(2,1)S(1)}, bf16[400,1024]{1,0:T(8,128)(2,1)S(1)}, u32[]{:S(2)}, u32[]{:S(2)}) %collective-permute-start.14) | collective-permute-done | bytes 819232 | tf_op jit(solution)/shard_map/ppermute | solution.py:393
  101.3 1.2 %shard_map.78 = (f32[3,72,1024]{2,1,0:T(8,128)S(1)}, f32[8,128]{1,0:T(8,128)S(1)}) custom-call(s32[3]{0:T(128)S(1)} %pad_add_fusion.refs_0_.code_ref, f32[3,128,1024]{2,1,0:T(8,128)S(1)} %copy-done.7, f32[3,8,256]{2,1,0:T(8,128)S(1)} %get-tuple-element.61.mass_ref, bf16[400,1024]{1,0:T(8,128)(2,1)S(1)} %collective-permute-done.14.refs_0_.refs_1_, ...), custom_call_target="tpu_custom_call" | custom-call | flops 20000000000 | bytes 1 | tf_op jit(solution)/shard_map/pallas_call | solution.py:616
  102.6 2.4 %shard_map.77._ = f32[6,64,1024]{2,1,0:T(8,128)} custom-call(s32[3]{0:T(128)S(1)} %pad_add_fusion.refs_0_.code_ref, f32[3,128,1024]{2,1,0:T(8,128)S(1)} %copy-done.7, f32[3,8,256]{2,1,0:T(8,128)S(1)} %get-tuple-element.61.mass_ref, bf16[400,1024]{1,0:T(8,128)(2,1)S(1)} %collective-permute-done.14.refs_0_.refs_1_, ...), custom_call_target="tpu_custom_call" | custom-call | flops 20000000000 | bytes 1 | tf_op jit(solution)/shard_map/pallas_call | solution.py:616
  105.1 2.0 %shard_map.79 = (f32[6,64,1024]{2,1,0:T(8,128)}, f32[6,64]{1,0:T(8,128)}) custom-call(s32[3]{0:T(128)S(1)} %pad_add_fusion.refs_0_.code_ref, f32[6,64,1024]{2,1,0:T(8,128)} %shard_map.77._, f32[3,72,1024]{2,1,0:T(8,128)S(1)} %collective-permute-done.17.swap_ref.line_ref, ...), custom_call_target="tpu_custom_call", output_to_operand_aliasing={{0}: (1, {})} | custom-call | flops 20000000000 | bytes 1 | tf_op jit(solution)/shard_map/pallas_call | solution.py:640
  (64 shorter events, 5.5 us)
Async XLA Ops:
  0.6 38.5 %collective-permute-start = (f32[6]{0:T(128)}, f32[6]{0:T(128)S(1)}, u32[]{:S(2)}, u32[]{:S(2)}) collective-permute-start(f32[6]{0:T(128)} %refs_1_.1), channel_id=1, source_target_pairs={{0,8},{4,12},{8,0},{12,4},{1,9},{5,13},{9,1},{13,5},{2,10},{6,14},... | collective-permute-start | bytes 80 | tf_op jit(solution)/shard_map/ppermute | solution.py:405
  5.8 20.1 %collective-permute-start.1 = (bf16[3,64,1024]{2,1,0:T(8,128)(2,1)S(1)}, bf16[3,64,1024]{2,1,0:T(8,128)(2,1)S(1)}, u32[]{:S(2)}, u32[]{:S(2)}) collective-permute-start(bf16[3,64,1024]{2,1,0:T(8,128)(2,1)S(1)} %constant_dynamic-slice_fusion), channel_id=1, source_target_pairs={{0,8},{4,12},{8,0},{12,4},{1,9},{5,13},{9,1},{13,5},{2,10},{6,14},... | collective-permute-start | bytes 1179656 | tf_op jit(solution)/shard_map/ppermute | solution.py:405
  6.7 1.6 %copy-start.3 = (bf16[1024,1024]{1,0:T(8,128)(2,1)S(1)}, bf16[1024,1024]{1,0:T(8,128)(2,1)}, u32[]{:S(2)}) copy-start(bf16[1024,1024]{1,0:T(8,128)(2,1)} %frames_ref.7) | copy-start | bytes 6291460
  8.3 2.0 %copy-start.1 = (s32[1,1024]{1,0:T(1,128)}, s32[1,1024]{1,0:T(1,128)S(1)}, u32[]{:S(2)}) copy-start(s32[1,1024]{1,0:T(1,128)S(1)} %fusion.12.rel_ref) | copy-start | bytes 12292
  8.3 20.6 %copy-start.4 = (bf16[1024,1024]{1,0:T(8,128)(2,1)S(1)}, bf16[1024,1024]{1,0:T(8,128)(2,1)}, u32[]{:S(2)}) copy-start(bf16[1024,1024]{1,0:T(8,128)(2,1)} %frames_ref.7) | copy-start | bytes 6291460
  10.3 34.2 %collective-permute-start.7 = (bf16[528,1024]{1,0:T(8,128)(2,1)S(1)}, bf16[528,1024]{1,0:T(8,128)(2,1)S(1)}, u32[]{:S(2)}, u32[]{:S(2)}) collective-permute-start(bf16[528,1024]{1,0:T(8,128)(2,1)S(1)} %get-tuple-element.43), channel_id=1, source_target_pairs={{0,4},{4,0},{8,12},{12,8},{1,5},{5,1},{9,13},{13,9},{2,6},{6,2},{1... | collective-permute-start | bytes 3244040 | tf_op jit(solution)/shard_map/ppermute | solution.py:400
  25.8 11.7 %collective-permute-start.2 = (bf16[3,64,1024]{2,1,0:T(8,128)(2,1)S(1)}, bf16[3,64,1024]{2,1,0:T(8,128)(2,1)S(1)}, u32[]{:S(2)}, u32[]{:S(2)}) collective-permute-start(bf16[3,64,1024]{2,1,0:T(8,128)(2,1)S(1)} %collective-permute-done.1.refs_2_), channel_id=1, source_target_pairs={{0,16},{16,0},{1,17},{17,1},{2,18},{18,2},{3,19},{19,3},{4,20},{20... | collective-permute-start | bytes 1179656 | tf_op jit(solution)/shard_map/ppermute | solution.py:408
  27.3 9.6 %collective-permute-start.3 = (bf16[3,64,1024]{2,1,0:T(8,128)(2,1)S(1)}, bf16[3,64,1024]{2,1,0:T(8,128)(2,1)S(1)}, u32[]{:S(2)}, u32[]{:S(2)}) collective-permute-start(bf16[3,64,1024]{2,1,0:T(8,128)(2,1)S(1)} %collective-permute-done.1.refs_2_), channel_id=1, source_target_pairs={{0,2},{1,3},{2,0},{3,1},{4,6},{5,7},{6,4},{7,5},{8,10},{9,11},{10,... | collective-permute-start | bytes 1179656 | tf_op jit(solution)/shard_map/ppermute | solution.py:393
  30.1 38.1 %collective-permute-start.12 = (bf16[528,1024]{1,0:T(8,128)(2,1)S(1)}, bf16[528,1024]{1,0:T(8,128)(2,1)S(1)}, u32[]{:S(2)}, u32[]{:S(2)}) collective-permute-start(bf16[528,1024]{1,0:T(8,128)(2,1)S(1)} %shard_map.68), channel_id=1, source_target_pairs={{0,4},{4,0},{8,12},{12,8},{1,5},{5,1},{9,13},{13,9},{2,6},{6,2},{1... | collective-permute-start | bytes 3244040 | tf_op jit(solution)/shard_map/ppermute | solution.py:400
  37.0 8.8 %collective-permute-start.4 = (bf16[3,32,1024]{2,1,0:T(8,128)(2,1)S(1)}, bf16[3,32,1024]{2,1,0:T(8,128)(2,1)S(1)}, u32[]{:S(2)}, u32[]{:S(2)}) collective-permute-start(bf16[3,32,1024]{2,1,0:T(8,128)(2,1)S(1)} %slice.70), channel_id=1, source_target_pairs={{0,16},{16,0},{1,17},{17,1},{2,18},{18,2},{3,19},{19,3},{4,20},{20... | collective-permute-start | bytes 589832 | tf_op jit(solution)/shard_map/ppermute | solution.py:408
  37.6 8.8 %collective-permute-start.5 = (bf16[3,32,1024]{2,1,0:T(8,128)(2,1)S(1)}, bf16[3,32,1024]{2,1,0:T(8,128)(2,1)S(1)}, u32[]{:S(2)}, u32[]{:S(2)}) collective-permute-start(bf16[3,32,1024]{2,1,0:T(8,128)(2,1)S(1)} %slice.71), channel_id=1, source_target_pairs={{0,2},{1,3},{2,0},{3,1},{4,6},{5,7},{6,4},{7,5},{8,10},{9,11},{10,... | collective-permute-start | bytes 589832 | tf_op jit(solution)/shard_map/ppermute | solution.py:393
  40.4 5.9 %collective-permute-start.6 = (bf16[528,1024]{1,0:T(8,128)(2,1)S(1)}, bf16[528,1024]{1,0:T(8,128)(2,1)S(1)}, u32[]{:S(2)}, u32[]{:S(2)}) collective-permute-start(bf16[528,1024]{1,0:T(8,128)(2,1)S(1)} %shard_map.69.refs_7_), channel_id=1, source_target_pairs={{0,1},{1,0},{2,3},{3,2},{4,5},{5,4},{6,7},{7,6},{8,9},{9,8},{10,11... | collective-permute-start | bytes 3244040 | tf_op jit(solution)/shard_map/ppermute | solution.py:390
  44.5 2.7 %collective-permute-start.8 = (bf16[528,1024]{1,0:T(8,128)(2,1)S(1)}, bf16[528,1024]{1,0:T(8,128)(2,1)S(1)}, u32[]{:S(2)}, u32[]{:S(2)}) collective-permute-start(bf16[528,1024]{1,0:T(8,128)(2,1)S(1)} %collective-permute-done.7.refs_9_), channel_id=1, source_target_pairs={{0,1},{1,0},{2,3},{3,2},{4,5},{5,4},{6,7},{7,6},{8,9},{9,8},{10,11... | collective-permute-start | bytes 3244040 | tf_op jit(solution)/shard_map/ppermute | solution.py:390
  45.8 30.0 %collective-permute-start.11 = (bf16[528,1024]{1,0:T(8,128)(2,1)S(1)}, bf16[528,1024]{1,0:T(8,128)(2,1)S(1)}, u32[]{:S(2)}, u32[]{:S(2)}) collective-permute-start(bf16[528,1024]{1,0:T(8,128)(2,1)S(1)} %shard_map.75.refs_3_), channel_id=1, source_target_pairs={{0,1},{1,0},{2,3},{3,2},{4,5},{5,4},{6,7},{7,6},{8,9},{9,8},{10,11... | collective-permute-start | bytes 3244040 | tf_op jit(solution)/shard_map/ppermute | solution.py:390
  51.4 8.4 %collective-permute-start.9 = (bf16[128,1024]{1,0:T(8,128)(2,1)S(1)}, bf16[128,1024]{1,0:T(8,128)(2,1)S(1)}, u32[]{:S(2)}, u32[]{:S(2)}) collective-permute-start(bf16[128,1024]{1,0:T(8,128)(2,1)S(1)} %get-tuple-element.50), channel_id=1, source_target_pairs={{0,2},{1,3},{2,0},{3,1},{4,6},{5,7},{6,4},{7,5},{8,10},{9,11},{10,... | collective-permute-start | bytes 786440 | tf_op jit(solution)/shard_map/ppermute | solution.py:393
  58.5 14.4 %collective-permute-start.10 = (bf16[272,1024]{1,0:T(8,128)(2,1)S(1)}, bf16[272,1024]{1,0:T(8,128)(2,1)S(1)}, u32[]{:S(2)}, u32[]{:S(2)}) collective-permute-start(bf16[272,1024]{1,0:T(8,128)(2,1)S(1)} %get-tuple-element.53), channel_id=1, source_target_pairs={{0,2},{1,3},{2,0},{3,1},{4,6},{5,7},{6,4},{7,5},{8,10},{9,11},{10,... | collective-permute-start | bytes 1671176 | tf_op jit(solution)/shard_map/ppermute | solution.py:393
  59.9 30.6 %collective-permute-start.15 = (bf16[128,1024]{1,0:T(8,128)(2,1)S(1)}, bf16[128,1024]{1,0:T(8,128)(2,1)S(1)}, u32[]{:S(2)}, u32[]{:S(2)}) collective-permute-start(bf16[128,1024]{1,0:T(8,128)(2,1)S(1)} %fusion.1), channel_id=1, source_target_pairs={{0,8},{4,12},{8,0},{12,4},{1,9},{5,13},{9,1},{13,5},{2,10},{6,14},... | collective-permute-start | bytes 786440 | tf_op jit(solution)/shard_map/ppermute | solution.py:405
  68.2 7.6 %collective-permute-start.13 = (bf16[528,1024]{1,0:T(8,128)(2,1)S(1)}, bf16[528,1024]{1,0:T(8,128)(2,1)S(1)}, u32[]{:S(2)}, u32[]{:S(2)}) collective-permute-start(bf16[528,1024]{1,0:T(8,128)(2,1)S(1)} %collective-permute-done.12.refs_5_), channel_id=1, source_target_pairs={{0,1},{1,0},{2,3},{3,2},{4,5},{5,4},{6,7},{7,6},{8,9},{9,8},{10,11... | collective-permute-start | bytes 3244040 | tf_op jit(solution)/shard_map/ppermute | solution.py:390
  73.3 2.5 %copy-start = (bf16[6,256,1024]{2,1,0:T(8,128)(2,1)S(1)}, bf16[6,256,1024]{2,1,0:T(8,128)(2,1)}, u32[]{:S(2)}) copy-start(bf16[6,256,1024]{2,1,0:T(8,128)(2,1)} %refs_2_.1) | copy-start | bytes 9437188
  73.3 2.5 %copy-start.5 = (f32[6]{0:T(128)S(1)}, f32[6]{0:T(128)}, u32[]{:S(2)}) copy-start(f32[6]{0:T(128)} %refs_1_.1) | copy-start | bytes 76
  73.3 28.0 %collective-permute-start.16 = (bf16[272,1024]{1,0:T(8,128)(2,1)S(1)}, bf16[272,1024]{1,0:T(8,128)(2,1)S(1)}, u32[]{:S(2)}, u32[]{:S(2)}) collective-permute-start(bf16[272,1024]{1,0:T(8,128)(2,1)S(1)} %pad_maximum_fusion), channel_id=1, source_target_pairs={{0,8},{4,12},{8,0},{12,4},{1,9},{5,13},{9,1},{13,5},{2,10},{6,14},... | collective-permute-start | bytes 1671176 | tf_op jit(solution)/shard_map/ppermute | solution.py:405
  82.4 1.1 %copy-start.6 = (f32[3,128,1024]{2,1,0:T(8,128)}, f32[3,128,1024]{2,1,0:T(8,128)S(1)}, u32[]{:S(2)}) copy-start(f32[3,128,1024]{2,1,0:T(8,128)S(1)} %get-tuple-element.60.keep_ref) | copy-start | bytes 4718596
  82.4 18.9 %collective-permute-start.14 = (bf16[400,1024]{1,0:T(8,128)(2,1)S(1)}, bf16[400,1024]{1,0:T(8,128)(2,1)S(1)}, u32[]{:S(2)}, u32[]{:S(2)}) collective-permute-start(bf16[400,1024]{1,0:T(8,128)(2,1)S(1)} %get-tuple-element.62), channel_id=1, source_target_pairs={{0,2},{1,3},{2,0},{3,1},{4,6},{5,7},{6,4},{7,5},{8,10},{9,11},{10,... | collective-permute-start | bytes 2457608 | tf_op jit(solution)/shard_map/ppermute | solution.py:393
  83.2 6.4 %copy-start.2 = (s32[1,1024]{1,0:T(1,128)S(1)}, s32[1,1024]{1,0:T(1,128)}, u32[]{:S(2)}) copy-start(s32[1,1024]{1,0:T(1,128)} %copy-done.1) | copy-start | bytes 12292
  83.5 2.5 %collective-permute-start.18 = (f32[6,160]{1,0:T(8,128)S(1)}, f32[6,160]{1,0:T(8,128)S(1)}, u32[]{:S(2)}, u32[]{:S(2)}) collective-permute-start(f32[6,160]{1,0:T(8,128)S(1)} %get-tuple-element.72), channel_id=1, source_target_pairs={{0,1},{1,0},{2,3},{3,2},{4,5},{5,4},{6,7},{7,6},{8,9},{9,8},{10,11... | collective-permute-start | bytes 11528 | tf_op jit(solution)/shard_map/ppermute | solution.py:418
  83.5 4.1 %collective-permute-start.19 = (f32[6,160]{1,0:T(8,128)S(1)}, f32[6,160]{1,0:T(8,128)S(1)}, u32[]{:S(2)}, u32[]{:S(2)}) collective-permute-start(f32[6,160]{1,0:T(8,128)S(1)} %get-tuple-element.73), channel_id=1, source_target_pairs={{0,4},{1,5},{2,6},{3,7},{4,0},{5,1},{6,2},{7,3},{8,12},{9,13},{10,... | collective-permute-start | bytes 11528 | tf_op jit(solution)/shard_map/ppermute | solution.py:418
  86.0 3.1 %collective-permute-start.20 = (f32[6,160]{1,0:T(8,128)S(1)}, f32[6,160]{1,0:T(8,128)S(1)}, u32[]{:S(2)}, u32[]{:S(2)}) collective-permute-start(f32[6,160]{1,0:T(8,128)S(1)} %get-tuple-element.74), channel_id=1, source_target_pairs={{0,5},{1,4},{2,7},{3,6},{4,1},{5,0},{6,3},{7,2},{8,13},{9,12},{10,... | collective-permute-start | bytes 11528 | tf_op jit(solution)/shard_map/ppermute | solution.py:418
  89.6 11.7 %copy-start.7 = (f32[3,128,1024]{2,1,0:T(8,128)S(1)}, f32[3,128,1024]{2,1,0:T(8,128)}, u32[]{:S(2)}) copy-start(f32[3,128,1024]{2,1,0:T(8,128)} %copy-done.6) | copy-start | bytes 4718596
  102.6 2.5 %collective-permute-start.17 = (f32[3,72,1024]{2,1,0:T(8,128)S(1)}, f32[3,72,1024]{2,1,0:T(8,128)S(1)}, u32[]{:S(2)}, u32[]{:S(2)}) collective-permute-start(f32[3,72,1024]{2,1,0:T(8,128)S(1)} %get-tuple-element.65), channel_id=1, source_target_pairs={{0,1},{1,0},{2,3},{3,2},{4,5},{5,4},{6,7},{7,6},{8,9},{9,8},{10,11... | collective-permute-start | bytes 2654216 | tf_op jit(solution)/shard_map/ppermute | solution.py:390

commit v6 on v5

--- a/solution.py
+++ b/solution.py
@@ -55,7 +55,7 @@
     count = jnp.sum(hits, axis=1, keepdims=True)
     ahead = jnp.sum(jnp.where((rel < line) & (rel >= base), 1, 0), axis=1, keepdims=True)
     behind = jnp.sum(
-        jnp.where((rel >= line) & (rel < base + meta_extra), 1, 0), axis=1, keepdims=True
+        jnp.where((rel <= line) & (rel >= base + per_core), 1, 0), axis=1, keepdims=True
     )
     back = (line - base)[:, :1] >= per_core
     start = jnp.where(back, own_slots - behind, ahead)
@@ -108,10 +108,6 @@
     return jnp.concatenate([high, middle, lines - high - middle, rest], axis=0)
 
 
-def _round(value):
-    return lax.reduce_precision(value, 8, 7)
-
-
 def _note_kernel(score_ref, out_ref):
     out_ref[...] = score_ref[:, 0]
 
@@ -134,9 +130,11 @@
     row_refs, refs = refs[:sources], refs[sources:]
     earlier_refs, refs = refs[:earlier], refs[earlier:]
     keep_ref, mass_ref, score_ref = refs[:3]
-    send_refs, (held, centres, sems, meta_low, meta_wide, meta_ref, meta_sems) = refs[3:-7], refs[-7:]
+    send_refs, (held, centres, sems, meta_low, meta_sems) = refs[3:-5], refs[-5:]
     step = pl.program_id(0)
     loads = []
+    first_only = begin + steps == 1
+    reach = window if first_only else reach
     for n in range(sources):
         low = 0 if n % cores == 0 else span - meta_extra - reach
         loads.append(
@@ -170,15 +168,8 @@
             copy.start()
         for copy in lines:
             copy.wait()
-        meta_wide[...] = meta_low[...].astype(jnp.float32).astype(jnp.int32)
-        to_scalars = pltpu.make_async_copy(meta_wide, meta_ref, meta_sems.at[sources])
-        to_scalars.start()
-        to_scalars.wait()
         for copy in loads:
             copy.wait()
-
-    def entry(n, field):
-        return meta_ref[n * meta_extra + (n % cores) * per_core + begin + step, field]
 
     if near:
         found = []
@@ -193,12 +184,23 @@
     half_norm = 0.5 * jnp.sum(wide * wide, axis=1, keepdims=True)
     slot = lax.broadcasted_iota(jnp.int32, (1, sources * window), 1)
     valid = slot < 0
+    lines = meta_low[...].astype(jnp.float32).astype(jnp.int32)
+    line = lax.broadcasted_iota(jnp.int32, lines.shape, 0)
+    firsts = []
     for n in range(sources):
-        low = n * window + entry(n, 1)
-        valid = valid | ((slot >= low) & (slot < low + entry(n, 2)))
-    chosen = jnp.concatenate(
-        [held[n, pl.ds(pl.multiple_of(entry(n, 0) * 16, 16), window)] for n in range(sources)]
-    )
+        at_line = n * meta_extra + (n % cores) * per_core + begin
+        found = lines[at_line : at_line + 1]
+        if steps > 1:
+            found = jnp.sum(jnp.where(line == at_line + step, lines, 0), axis=0, keepdims=True)
+        firsts.append(None if first_only else found[0, 0] * 16)
+        low = found[:, 1:2] + n * window
+        valid = valid | ((slot >= low) & (slot < low + found[:, 2:3]))
+    if first_only:
+        chosen = held[...].reshape(sources * window, held.shape[2])
+    else:
+        chosen = jnp.concatenate(
+            [held[n, pl.ds(pl.multiple_of(firsts[n], 16), window)] for n in range(sources)]
+        )
     products = lax.dot_general(
         centre, chosen, (((1,), (1,)), ((), ())), preferred_element_type=jnp.float32
     )
@@ -341,13 +343,11 @@
                 (moving if n in (0, 2) else fixed)(o.shape) for n, o in enumerate(out_shape)
             ],
             scratch_shapes=[
-                pltpu.VMEM((sources, reach, width), jnp.bfloat16),
+                pltpu.VMEM((sources, window if begin + steps == 1 else reach, width), jnp.bfloat16),
                 pltpu.VMEM((1 if near else steps, kids, width), jnp.bfloat16),
                 pltpu.SemaphoreType.DMA((sources + len(places),)),
                 pltpu.VMEM((sources * meta_extra, 128), jnp.bfloat16),
-                pltpu.VMEM((sources * meta_extra, 128), jnp.int32),
-                pltpu.SMEM((sources * meta_extra, 128), jnp.int32),
-                pltpu.SemaphoreType.DMA((sources + 1,)),
+                pltpu.SemaphoreType.DMA((sources,)),
             ],
         ),
         out_shape=out_shape,

time: 107 us -> 105 us (0.981)
  Pallas kernels: 28.5 us -> 25.7 us
    pallas_call x3, Pallas kernels: 16 us -> 13.3 us  [_cell_call(): pl.pallas_call(functools.partial(_cell_kernel, sources, window, reach, pi...]
    ppermute x5, waiting for transfers between devices: 23.3 us -> 21.4 us  [hop_chip(): lax.ppermute(v, 'frame', [(a * cores + c, (a + s) % chips * cores + c) fo...]
    ppermute x2, waiting for transfers between devices: 9.42 us -> 10.9 us  [hop_member(): lax.ppermute(v, 'cell', [(b * half + i, b * half + (i + s) % half) for b...]
  transfers between devices with their start and end apart: 21 -> 21, of which waited for: 10 -> 10; matrix products, arithmetic and copies ran while one was open for 3% -> 3% of each run, Pallas kernels for 24% -> 21%
where the time goes in v6:
time: 105 us
  waiting for transfers between devices  48.9 us (47%)
  Pallas kernels  25.7 us (24%)
  starting transfers between devices  24.6 us (23%)
  local copies, waits for them, and re-layouts  3.27 us (3%)
  other arithmetic  1.18 us (1%)
    ppermute x5, waiting for transfers between devices, hop_chip(): lax.ppermute(v, 'frame', [(a * cores + c, (a + s) % chips * cores + c) fo...  21.4 us
    ppermute x4, waiting for transfers between devices, hop_partner(): lax.ppermute(v, 'cell', [(i, (i + half) % cell_count) for i in range(cell...  13.5 us
    pallas_call x3, Pallas kernels, _cell_call(): pl.pallas_call(functools.partial(_cell_kernel, sources, window, reach, pi...  13.3 us
    ppermute x2, waiting for transfers between devices, hop_member(): lax.ppermute(v, 'cell', [(b * half + i, b * half + (i + s) % half) for b...  10.9 us
    ppermute x4, starting transfers between devices, hop_partner(): lax.ppermute(v, 'cell', [(i, (i + half) % cell_count) for i in range(cell...  9.72 us
    ppermute x5, starting transfers between devices, hop_chip(): lax.ppermute(v, 'frame', [(a * cores + c, (a + s) % chips * cores + c) fo...  6.6 us
    pallas_call x2, Pallas kernels, update(): pl.pallas_call(functools.partial(_update_kernel, per_core, chips, piece,...  3.66 us
    ppermute x3, starting transfers between devices, hop_any(): return lax.ppermute(v, ('cell', 'frame'), pairs)  3.46 us
  transfers between devices with their start and end apart: 21, of which 10 were waited for; matrix products, arithmetic and copies ran while one was open for 3% of the time, Pallas kernels for 21%

profile of v6, /device:TPU:0, one launch (start us, length us, event | category | flops | bytes accessed | tf_op | source)
XLA Modules:
  0.0 104.7 jit_solution(6414371267073894760)
XLA Ops:
  0.6 4.1 %collective-permute-start = (f32[6]{0:T(128)}, f32[6]{0:T(128)S(1)}, u32[]{:S(2)}, u32[]{:S(2)}) collective-permute-start(f32[6]{0:T(128)} %refs_1_.1), channel_id=1, source_target_pairs={{0,8},{4,12},{8,0},{12,4},{1,9},{5,13},{9,1},{13,5},{2,10},{6,14},... | collective-permute-start | bytes 80 | tf_op jit(solution)/shard_map/ppermute | solution.py:405
  4.7 1.0 constant_dynamic-slice_fusion
  6.7 1.6 %copy-done.3 = bf16[1024,1024]{1,0:T(8,128)(2,1)S(1)} copy-done((bf16[1024,1024]{1,0:T(8,128)(2,1)S(1)}, bf16[1024,1024]{1,0:T(8,128)(2,1)}, u32[]{:S(2)}) %copy-start.3) | copy-done | bytes 2097176
  8.3 2.0 %shard_map.67 = (s32[1,1024]{1,0:T(1,128)S(1)}, s32[1,1024]{1,0:T(1,128)S(1)}, f32[64,128]{1,0:T(8,128)S(1)}, bf16[528,1024]{1,0:T(8,128)(2,1)S(1)}) custom-call(s32[1,1024]{1,0:T(1,128)S(1)} %fusion.12.rel_ref, bf16[1024,1024]{1,0:T(8,128)(2,1)S(1)} %copy-done.3), custom_call_target="tpu_custom_call" | custom-call | flops 20000000000 | bytes 1000000000 | tf_op jit(solution)/shard_map/pallas_call | solution.py:454
  10.3 1.9 %collective-permute-start.7 = (bf16[528,1024]{1,0:T(8,128)(2,1)S(1)}, bf16[528,1024]{1,0:T(8,128)(2,1)S(1)}, u32[]{:S(2)}, u32[]{:S(2)}) collective-permute-start(bf16[528,1024]{1,0:T(8,128)(2,1)S(1)} %get-tuple-element.43), channel_id=1, source_target_pairs={{0,4},{4,0},{8,12},{12,8},{1,5},{5,1},{9,13},{13,9},{2,6},{6,2},{1... | collective-permute-start | bytes 3244040 | tf_op jit(solution)/shard_map/ppermute | solution.py:400
  12.3 13.5 %collective-permute-done.1.refs_2_ = bf16[3,64,1024]{2,1,0:T(8,128)(2,1)S(1)} collective-permute-done((bf16[3,64,1024]{2,1,0:T(8,128)(2,1)S(1)}, bf16[3,64,1024]{2,1,0:T(8,128)(2,1)S(1)}, u32[]{:S(2)}, u32[]{:S(2)}) %collective-permute-start.1) | collective-permute-done | bytes 393248 | tf_op jit(solution)/shard_map/ppermute | solution.py:405
  25.8 1.5 %collective-permute-start.2 = (bf16[3,64,1024]{2,1,0:T(8,128)(2,1)S(1)}, bf16[3,64,1024]{2,1,0:T(8,128)(2,1)S(1)}, u32[]{:S(2)}, u32[]{:S(2)}) collective-permute-start(bf16[3,64,1024]{2,1,0:T(8,128)(2,1)S(1)} %collective-permute-done.1.refs_2_), channel_id=1, source_target_pairs={{0,16},{16,0},{1,17},{17,1},{2,18},{18,2},{3,19},{19,3},{4,20},{20... | collective-permute-start | bytes 1179656 | tf_op jit(solution)/shard_map/ppermute | solution.py:408
  27.3 1.5 %collective-permute-start.3 = (bf16[3,64,1024]{2,1,0:T(8,128)(2,1)S(1)}, bf16[3,64,1024]{2,1,0:T(8,128)(2,1)S(1)}, u32[]{:S(2)}, u32[]{:S(2)}) collective-permute-start(bf16[3,64,1024]{2,1,0:T(8,128)(2,1)S(1)} %collective-permute-done.1.refs_2_), channel_id=1, source_target_pairs={{0,2},{1,3},{2,0},{3,1},{4,6},{5,7},{6,4},{7,5},{8,10},{9,11},{10,... | collective-permute-start | bytes 1179656 | tf_op jit(solution)/shard_map/ppermute | solution.py:393
  28.8 1.2 %shard_map.68 = bf16[528,1024]{1,0:T(8,128)(2,1)S(1)} custom-call(s32[1,1024]{1,0:T(1,128)S(1)} %get-tuple-element.58.flat_ref, f32[64,128]{1,0:T(8,128)S(1)} %get-tuple-element.41.meta_ref, bf16[1024,1024]{1,0:T(8,128)(2,1)S(1)} %copy-done.4), custom_call_target="tpu_custom_call" | custom-call | flops 20000000000 | bytes 1000000000 | tf_op jit(solution)/shard_map/pallas_call | solution.py:467
  30.2 6.8 %collective-permute-done.3.refs_4_ = bf16[3,64,1024]{2,1,0:T(8,128)(2,1)S(1)} collective-permute-done((bf16[3,64,1024]{2,1,0:T(8,128)(2,1)S(1)}, bf16[3,64,1024]{2,1,0:T(8,128)(2,1)S(1)}, u32[]{:S(2)}, u32[]{:S(2)}) %collective-permute-start.3) | collective-permute-done | bytes 393248 | tf_op jit(solution)/shard_map/ppermute | solution.py:393
  37.6 1.6 %collective-permute-start.5 = (bf16[3,32,1024]{2,1,0:T(8,128)(2,1)S(1)}, bf16[3,32,1024]{2,1,0:T(8,128)(2,1)S(1)}, u32[]{:S(2)}, u32[]{:S(2)}) collective-permute-start(bf16[3,32,1024]{2,1,0:T(8,128)(2,1)S(1)} %slice.71), channel_id=1, source_target_pairs={{0,2},{1,3},{2,0},{3,1},{4,6},{5,7},{6,4},{7,5},{8,10},{9,11},{10,... | collective-permute-start | bytes 589832 | tf_op jit(solution)/shard_map/ppermute | solution.py:393
  39.1 1.3 %shard_map.69.refs_7_ = bf16[528,1024]{1,0:T(8,128)(2,1)S(1)} custom-call(s32[1,1024]{1,0:T(1,128)S(1)} %get-tuple-element.58.flat_ref, f32[64,128]{1,0:T(8,128)S(1)} %get-tuple-element.41.meta_ref, bf16[1024,1024]{1,0:T(8,128)(2,1)S(1)} %copy-done.4), custom_call_target="tpu_custom_call" | custom-call | flops 20000000000 | bytes 1000000000 | tf_op jit(solution)/shard_map/pallas_call | solution.py:477
  40.5 4.0 %collective-permute-done.7.refs_9_ = bf16[528,1024]{1,0:T(8,128)(2,1)S(1)} collective-permute-done((bf16[528,1024]{1,0:T(8,128)(2,1)S(1)}, bf16[528,1024]{1,0:T(8,128)(2,1)S(1)}, u32[]{:S(2)}, u32[]{:S(2)}) %collective-permute-start.7) | collective-permute-done | bytes 1081376 | tf_op jit(solution)/shard_map/ppermute | solution.py:400
  44.5 1.3 %shard_map.75.refs_3_ = bf16[528,1024]{1,0:T(8,128)(2,1)S(1)} custom-call(s32[1,1024]{1,0:T(1,128)S(1)} %get-tuple-element.58.flat_ref, f32[64,128]{1,0:T(8,128)S(1)} %get-tuple-element.41.meta_ref, bf16[1024,1024]{1,0:T(8,128)(2,1)S(1)} %copy-done.4), custom_call_target="tpu_custom_call" | custom-call | flops 20000000000 | bytes 1000000000 | tf_op jit(solution)/shard_map/pallas_call | solution.py:477
  46.4 0.9 collective-permute-done.8.refs_10_
  47.2 3.3 %shard_map.70 = (f32[1,128,1024]{2,1,0:T(8,128)S(1)}, f32[1,8,256]{2,1,0:T(8,128)S(1)}, f32[1,8,640]{2,1,0:T(8,128)S(1)}, bf16[128,1024]{1,0:T(8,128)(2,1)S(1)}) custom-call(s32[3]{0:T(128)S(1)} %pad_add_fusion.refs_0_.code_ref, f32[6]{0:T(128)S(1)} %collective-permute-done.refs_1_, bf16[3,64,1024]{2,1,0:T(8,128)(2,1)S(1)} %collective-permute-done.1.refs_2_, ...), custom_call_target="tpu_custom_call" | custom-call | flops 20000000000 | bytes 1 | tf_op jit(solution)/shard_map/pallas_call | solution.py:328
  50.5 1.8 %collective-permute-start.9 = (bf16[128,1024]{1,0:T(8,128)(2,1)S(1)}, bf16[128,1024]{1,0:T(8,128)(2,1)S(1)}, u32[]{:S(2)}, u32[]{:S(2)}) collective-permute-start(bf16[128,1024]{1,0:T(8,128)(2,1)S(1)} %get-tuple-element.50), channel_id=1, source_target_pairs={{0,2},{1,3},{2,0},{3,1},{4,6},{5,7},{6,4},{7,5},{8,10},{9,11},{10,... | collective-permute-start | bytes 786440 | tf_op jit(solution)/shard_map/ppermute | solution.py:393
  52.4 4.3 %shard_map.72 = (f32[2,128,1024]{2,1,0:T(8,128)S(1)}, f32[2,8,256]{2,1,0:T(8,128)S(1)}, f32[2,8,640]{2,1,0:T(8,128)S(1)}, bf16[272,1024]{1,0:T(8,128)(2,1)S(1)}) custom-call(s32[3]{0:T(128)S(1)} %pad_add_fusion.refs_0_.code_ref, f32[6]{0:T(128)S(1)} %collective-permute-done.refs_1_, bf16[3,64,1024]{2,1,0:T(8,128)(2,1)S(1)} %collective-permute-done.1.refs_2_, ...), custom_call_target="tpu_custom_call" | custom-call | flops 20000000000 | bytes 1 | tf_op jit(solution)/shard_map/pallas_call | solution.py:328
  57.0 2.0 %collective-permute-done.9 = bf16[128,1024]{1,0:T(8,128)(2,1)S(1)} collective-permute-done((bf16[128,1024]{1,0:T(8,128)(2,1)S(1)}, bf16[128,1024]{1,0:T(8,128)(2,1)S(1)}, u32[]{:S(2)}, u32[]{:S(2)}) %collective-permute-start.9) | collective-permute-done | bytes 262176 | tf_op jit(solution)/shard_map/ppermute | solution.py:393
  59.1 2.9 %collective-permute-start.15 = (bf16[128,1024]{1,0:T(8,128)(2,1)S(1)}, bf16[128,1024]{1,0:T(8,128)(2,1)S(1)}, u32[]{:S(2)}, u32[]{:S(2)}) collective-permute-start(bf16[128,1024]{1,0:T(8,128)(2,1)S(1)} %fusion.1), channel_id=1, source_target_pairs={{0,8},{4,12},{8,0},{12,4},{1,9},{5,13},{9,1},{13,5},{2,10},{6,14},... | collective-permute-start | bytes 786440 | tf_op jit(solution)/shard_map/ppermute | solution.py:405
  62.0 6.9 %collective-permute-done.12.refs_5_ = bf16[528,1024]{1,0:T(8,128)(2,1)S(1)} collective-permute-done((bf16[528,1024]{1,0:T(8,128)(2,1)S(1)}, bf16[528,1024]{1,0:T(8,128)(2,1)S(1)}, u32[]{:S(2)}, u32[]{:S(2)}) %collective-permute-start.12) | collective-permute-done | bytes 1081376 | tf_op jit(solution)/shard_map/ppermute | solution.py:400
  68.9 2.3 %collective-permute-done.10 = bf16[272,1024]{1,0:T(8,128)(2,1)S(1)} collective-permute-done((bf16[272,1024]{1,0:T(8,128)(2,1)S(1)}, bf16[272,1024]{1,0:T(8,128)(2,1)S(1)}, u32[]{:S(2)}, u32[]{:S(2)}) %collective-permute-start.10) | collective-permute-done | bytes 557088 | tf_op jit(solution)/shard_map/ppermute | solution.py:393
  71.5 2.6 %collective-permute-start.16 = (bf16[272,1024]{1,0:T(8,128)(2,1)S(1)}, bf16[272,1024]{1,0:T(8,128)(2,1)S(1)}, u32[]{:S(2)}, u32[]{:S(2)}) collective-permute-start(bf16[272,1024]{1,0:T(8,128)(2,1)S(1)} %pad_maximum_fusion), channel_id=1, source_target_pairs={{0,8},{4,12},{8,0},{12,4},{1,9},{5,13},{9,1},{13,5},{2,10},{6,14},... | collective-permute-start | bytes 1671176 | tf_op jit(solution)/shard_map/ppermute | solution.py:405
  74.1 5.7 %shard_map.76 = (f32[3,128,1024]{2,1,0:T(8,128)S(1)}, f32[3,8,256]{2,1,0:T(8,128)S(1)}, f32[3,8,640]{2,1,0:T(8,128)S(1)}, bf16[400,1024]{1,0:T(8,128)(2,1)S(1)}) custom-call(s32[3]{0:T(128)S(1)} %pad_add_fusion.refs_0_.code_ref, f32[6]{0:T(128)S(1)} %copy-done.5, bf16[6,256,1024]{2,1,0:T(8,128)(2,1)S(1)} %copy-done, ...), custom_call_target="tpu_custom_call" | custom-call | flops 20000000000 | bytes 1 | tf_op jit(solution)/shard_map/pallas_call | solution.py:328
  79.8 1.4 %collective-permute-start.14 = (bf16[400,1024]{1,0:T(8,128)(2,1)S(1)}, bf16[400,1024]{1,0:T(8,128)(2,1)S(1)}, u32[]{:S(2)}, u32[]{:S(2)}) collective-permute-start(bf16[400,1024]{1,0:T(8,128)(2,1)S(1)} %get-tuple-element.62), channel_id=1, source_target_pairs={{0,2},{1,3},{2,0},{3,1},{4,6},{5,7},{6,4},{7,5},{8,10},{9,11},{10,... | collective-permute-start | bytes 2457608 | tf_op jit(solution)/shard_map/ppermute | solution.py:393
  81.5 2.5 %collective-permute-start.19 = (f32[6,160]{1,0:T(8,128)S(1)}, f32[6,160]{1,0:T(8,128)S(1)}, u32[]{:S(2)}, u32[]{:S(2)}) collective-permute-start(f32[6,160]{1,0:T(8,128)S(1)} %get-tuple-element.73), channel_id=1, source_target_pairs={{0,4},{1,5},{2,6},{3,7},{4,0},{5,1},{6,2},{7,3},{8,12},{9,13},{10,... | collective-permute-start | bytes 11528 | tf_op jit(solution)/shard_map/ppermute | solution.py:418
  85.6 1.4 %collective-permute-done.20 = f32[6,160]{1,0:T(8,128)S(1)} collective-permute-done((f32[6,160]{1,0:T(8,128)S(1)}, f32[6,160]{1,0:T(8,128)S(1)}, u32[]{:S(2)}, u32[]{:S(2)}) %collective-permute-start.20) | collective-permute-done | bytes 3872 | tf_op jit(solution)/shard_map/ppermute | solution.py:418
  87.6 0.9 shard_map.81
  88.5 10.3 %collective-permute-done.14.refs_0_.refs_1_ = bf16[400,1024]{1,0:T(8,128)(2,1)S(1)} collective-permute-done((bf16[400,1024]{1,0:T(8,128)(2,1)S(1)}, bf16[400,1024]{1,0:T(8,128)(2,1)S(1)}, u32[]{:S(2)}, u32[]{:S(2)}) %collective-permute-start.14) | collective-permute-done | bytes 819232 | tf_op jit(solution)/shard_map/ppermute | solution.py:393
  98.9 1.2 %shard_map.78 = (f32[3,72,1024]{2,1,0:T(8,128)S(1)}, f32[8,128]{1,0:T(8,128)S(1)}) custom-call(s32[3]{0:T(128)S(1)} %pad_add_fusion.refs_0_.code_ref, f32[3,128,1024]{2,1,0:T(8,128)S(1)} %copy-done.7, f32[3,8,256]{2,1,0:T(8,128)S(1)} %get-tuple-element.61.mass_ref, bf16[400,1024]{1,0:T(8,128)(2,1)S(1)} %collective-permute-done.14.refs_0_.refs_1_, ...), custom_call_target="tpu_custom_call" | custom-call | flops 20000000000 | bytes 1 | tf_op jit(solution)/shard_map/pallas_call | solution.py:616
  100.2 2.4 %shard_map.77._ = f32[6,64,1024]{2,1,0:T(8,128)} custom-call(s32[3]{0:T(128)S(1)} %pad_add_fusion.refs_0_.code_ref, f32[3,128,1024]{2,1,0:T(8,128)S(1)} %copy-done.7, f32[3,8,256]{2,1,0:T(8,128)S(1)} %get-tuple-element.61.mass_ref, bf16[400,1024]{1,0:T(8,128)(2,1)S(1)} %collective-permute-done.14.refs_0_.refs_1_, ...), custom_call_target="tpu_custom_call" | custom-call | flops 20000000000 | bytes 1 | tf_op jit(solution)/shard_map/pallas_call | solution.py:616
  102.6 2.0 %shard_map.79 = (f32[6,64,1024]{2,1,0:T(8,128)}, f32[6,64]{1,0:T(8,128)}) custom-call(s32[3]{0:T(128)S(1)} %pad_add_fusion.refs_0_.code_ref, f32[6,64,1024]{2,1,0:T(8,128)} %shard_map.77._, f32[3,72,1024]{2,1,0:T(8,128)S(1)} %collective-permute-done.17.swap_ref.line_ref, ...), custom_call_target="tpu_custom_call", output_to_operand_aliasing={{0}: (1, {})} | custom-call | flops 20000000000 | bytes 1 | tf_op jit(solution)/shard_map/pallas_call | solution.py:640
  (64 shorter events, 5.5 us)
Async XLA Ops:
  0.6 38.5 %collective-permute-start = (f32[6]{0:T(128)}, f32[6]{0:T(128)S(1)}, u32[]{:S(2)}, u32[]{:S(2)}) collective-permute-start(f32[6]{0:T(128)} %refs_1_.1), channel_id=1, source_target_pairs={{0,8},{4,12},{8,0},{12,4},{1,9},{5,13},{9,1},{13,5},{2,10},{6,14},... | collective-permute-start | bytes 80 | tf_op jit(solution)/shard_map/ppermute | solution.py:405
  5.8 20.1 %collective-permute-start.1 = (bf16[3,64,1024]{2,1,0:T(8,128)(2,1)S(1)}, bf16[3,64,1024]{2,1,0:T(8,128)(2,1)S(1)}, u32[]{:S(2)}, u32[]{:S(2)}) collective-permute-start(bf16[3,64,1024]{2,1,0:T(8,128)(2,1)S(1)} %constant_dynamic-slice_fusion), channel_id=1, source_target_pairs={{0,8},{4,12},{8,0},{12,4},{1,9},{5,13},{9,1},{13,5},{2,10},{6,14},... | collective-permute-start | bytes 1179656 | tf_op jit(solution)/shard_map/ppermute | solution.py:405
  6.7 1.6 %copy-start.3 = (bf16[1024,1024]{1,0:T(8,128)(2,1)S(1)}, bf16[1024,1024]{1,0:T(8,128)(2,1)}, u32[]{:S(2)}) copy-start(bf16[1024,1024]{1,0:T(8,128)(2,1)} %frames_ref.7) | copy-start | bytes 6291460
  8.3 2.0 %copy-start.1 = (s32[1,1024]{1,0:T(1,128)}, s32[1,1024]{1,0:T(1,128)S(1)}, u32[]{:S(2)}) copy-start(s32[1,1024]{1,0:T(1,128)S(1)} %fusion.12.rel_ref) | copy-start | bytes 12292
  8.3 20.6 %copy-start.4 = (bf16[1024,1024]{1,0:T(8,128)(2,1)S(1)}, bf16[1024,1024]{1,0:T(8,128)(2,1)}, u32[]{:S(2)}) copy-start(bf16[1024,1024]{1,0:T(8,128)(2,1)} %frames_ref.7) | copy-start | bytes 6291460
  10.3 34.2 %collective-permute-start.7 = (bf16[528,1024]{1,0:T(8,128)(2,1)S(1)}, bf16[528,1024]{1,0:T(8,128)(2,1)S(1)}, u32[]{:S(2)}, u32[]{:S(2)}) collective-permute-start(bf16[528,1024]{1,0:T(8,128)(2,1)S(1)} %get-tuple-element.43), channel_id=1, source_target_pairs={{0,4},{4,0},{8,12},{12,8},{1,5},{5,1},{9,13},{13,9},{2,6},{6,2},{1... | collective-permute-start | bytes 3244040 | tf_op jit(solution)/shard_map/ppermute | solution.py:400
  25.8 11.7 %collective-permute-start.2 = (bf16[3,64,1024]{2,1,0:T(8,128)(2,1)S(1)}, bf16[3,64,1024]{2,1,0:T(8,128)(2,1)S(1)}, u32[]{:S(2)}, u32[]{:S(2)}) collective-permute-start(bf16[3,64,1024]{2,1,0:T(8,128)(2,1)S(1)} %collective-permute-done.1.refs_2_), channel_id=1, source_target_pairs={{0,16},{16,0},{1,17},{17,1},{2,18},{18,2},{3,19},{19,3},{4,20},{20... | collective-permute-start | bytes 1179656 | tf_op jit(solution)/shard_map/ppermute | solution.py:408
  27.3 9.6 %collective-permute-start.3 = (bf16[3,64,1024]{2,1,0:T(8,128)(2,1)S(1)}, bf16[3,64,1024]{2,1,0:T(8,128)(2,1)S(1)}, u32[]{:S(2)}, u32[]{:S(2)}) collective-permute-start(bf16[3,64,1024]{2,1,0:T(8,128)(2,1)S(1)} %collective-permute-done.1.refs_2_), channel_id=1, source_target_pairs={{0,2},{1,3},{2,0},{3,1},{4,6},{5,7},{6,4},{7,5},{8,10},{9,11},{10,... | collective-permute-start | bytes 1179656 | tf_op jit(solution)/shard_map/ppermute | solution.py:393
  30.1 38.8 %collective-permute-start.12 = (bf16[528,1024]{1,0:T(8,128)(2,1)S(1)}, bf16[528,1024]{1,0:T(8,128)(2,1)S(1)}, u32[]{:S(2)}, u32[]{:S(2)}) collective-permute-start(bf16[528,1024]{1,0:T(8,128)(2,1)S(1)} %shard_map.68), channel_id=1, source_target_pairs={{0,4},{4,0},{8,12},{12,8},{1,5},{5,1},{9,13},{13,9},{2,6},{6,2},{1... | collective-permute-start | bytes 3244040 | tf_op jit(solution)/shard_map/ppermute | solution.py:400
  37.0 8.8 %collective-permute-start.4 = (bf16[3,32,1024]{2,1,0:T(8,128)(2,1)S(1)}, bf16[3,32,1024]{2,1,0:T(8,128)(2,1)S(1)}, u32[]{:S(2)}, u32[]{:S(2)}) collective-permute-start(bf16[3,32,1024]{2,1,0:T(8,128)(2,1)S(1)} %slice.70), channel_id=1, source_target_pairs={{0,16},{16,0},{1,17},{17,1},{2,18},{18,2},{3,19},{19,3},{4,20},{20... | collective-permute-start | bytes 589832 | tf_op jit(solution)/shard_map/ppermute | solution.py:408
  37.6 8.8 %collective-permute-start.5 = (bf16[3,32,1024]{2,1,0:T(8,128)(2,1)S(1)}, bf16[3,32,1024]{2,1,0:T(8,128)(2,1)S(1)}, u32[]{:S(2)}, u32[]{:S(2)}) collective-permute-start(bf16[3,32,1024]{2,1,0:T(8,128)(2,1)S(1)} %slice.71), channel_id=1, source_target_pairs={{0,2},{1,3},{2,0},{3,1},{4,6},{5,7},{6,4},{7,5},{8,10},{9,11},{10,... | collective-permute-start | bytes 589832 | tf_op jit(solution)/shard_map/ppermute | solution.py:393
  40.4 5.9 %collective-permute-start.6 = (bf16[528,1024]{1,0:T(8,128)(2,1)S(1)}, bf16[528,1024]{1,0:T(8,128)(2,1)S(1)}, u32[]{:S(2)}, u32[]{:S(2)}) collective-permute-start(bf16[528,1024]{1,0:T(8,128)(2,1)S(1)} %shard_map.69.refs_7_), channel_id=1, source_target_pairs={{0,1},{1,0},{2,3},{3,2},{4,5},{5,4},{6,7},{7,6},{8,9},{9,8},{10,11... | collective-permute-start | bytes 3244040 | tf_op jit(solution)/shard_map/ppermute | solution.py:390
  44.5 2.7 %collective-permute-start.8 = (bf16[528,1024]{1,0:T(8,128)(2,1)S(1)}, bf16[528,1024]{1,0:T(8,128)(2,1)S(1)}, u32[]{:S(2)}, u32[]{:S(2)}) collective-permute-start(bf16[528,1024]{1,0:T(8,128)(2,1)S(1)} %collective-permute-done.7.refs_9_), channel_id=1, source_target_pairs={{0,1},{1,0},{2,3},{3,2},{4,5},{5,4},{6,7},{7,6},{8,9},{9,8},{10,11... | collective-permute-start | bytes 3244040 | tf_op jit(solution)/shard_map/ppermute | solution.py:390
  45.8 28.3 %collective-permute-start.11 = (bf16[528,1024]{1,0:T(8,128)(2,1)S(1)}, bf16[528,1024]{1,0:T(8,128)(2,1)S(1)}, u32[]{:S(2)}, u32[]{:S(2)}) collective-permute-start(bf16[528,1024]{1,0:T(8,128)(2,1)S(1)} %shard_map.75.refs_3_), channel_id=1, source_target_pairs={{0,1},{1,0},{2,3},{3,2},{4,5},{5,4},{6,7},{7,6},{8,9},{9,8},{10,11... | collective-permute-start | bytes 3244040 | tf_op jit(solution)/shard_map/ppermute | solution.py:390
  50.5 8.5 %collective-permute-start.9 = (bf16[128,1024]{1,0:T(8,128)(2,1)S(1)}, bf16[128,1024]{1,0:T(8,128)(2,1)S(1)}, u32[]{:S(2)}, u32[]{:S(2)}) collective-permute-start(bf16[128,1024]{1,0:T(8,128)(2,1)S(1)} %get-tuple-element.50), channel_id=1, source_target_pairs={{0,2},{1,3},{2,0},{3,1},{4,6},{5,7},{6,4},{7,5},{8,10},{9,11},{10,... | collective-permute-start | bytes 786440 | tf_op jit(solution)/shard_map/ppermute | solution.py:393
  56.7 14.5 %collective-permute-start.10 = (bf16[272,1024]{1,0:T(8,128)(2,1)S(1)}, bf16[272,1024]{1,0:T(8,128)(2,1)S(1)}, u32[]{:S(2)}, u32[]{:S(2)}) collective-permute-start(bf16[272,1024]{1,0:T(8,128)(2,1)S(1)} %get-tuple-element.53), channel_id=1, source_target_pairs={{0,2},{1,3},{2,0},{3,1},{4,6},{5,7},{6,4},{7,5},{8,10},{9,11},{10,... | collective-permute-start | bytes 1671176 | tf_op jit(solution)/shard_map/ppermute | solution.py:393
  59.1 29.4 %collective-permute-start.15 = (bf16[128,1024]{1,0:T(8,128)(2,1)S(1)}, bf16[128,1024]{1,0:T(8,128)(2,1)S(1)}, u32[]{:S(2)}, u32[]{:S(2)}) collective-permute-start(bf16[128,1024]{1,0:T(8,128)(2,1)S(1)} %fusion.1), channel_id=1, source_target_pairs={{0,8},{4,12},{8,0},{12,4},{1,9},{5,13},{9,1},{13,5},{2,10},{6,14},... | collective-permute-start | bytes 786440 | tf_op jit(solution)/shard_map/ppermute | solution.py:405
  68.9 5.2 %collective-permute-start.13 = (bf16[528,1024]{1,0:T(8,128)(2,1)S(1)}, bf16[528,1024]{1,0:T(8,128)(2,1)S(1)}, u32[]{:S(2)}, u32[]{:S(2)}) collective-permute-start(bf16[528,1024]{1,0:T(8,128)(2,1)S(1)} %collective-permute-done.12.refs_5_), channel_id=1, source_target_pairs={{0,1},{1,0},{2,3},{3,2},{4,5},{5,4},{6,7},{7,6},{8,9},{9,8},{10,11... | collective-permute-start | bytes 3244040 | tf_op jit(solution)/shard_map/ppermute | solution.py:390
  71.5 2.6 %copy-start = (bf16[6,256,1024]{2,1,0:T(8,128)(2,1)S(1)}, bf16[6,256,1024]{2,1,0:T(8,128)(2,1)}, u32[]{:S(2)}) copy-start(bf16[6,256,1024]{2,1,0:T(8,128)(2,1)} %refs_2_.1) | copy-start | bytes 9437188
  71.5 2.6 %copy-start.5 = (f32[6]{0:T(128)S(1)}, f32[6]{0:T(128)}, u32[]{:S(2)}) copy-start(f32[6]{0:T(128)} %refs_1_.1) | copy-start | bytes 76
  71.5 27.4 %collective-permute-start.16 = (bf16[272,1024]{1,0:T(8,128)(2,1)S(1)}, bf16[272,1024]{1,0:T(8,128)(2,1)S(1)}, u32[]{:S(2)}, u32[]{:S(2)}) collective-permute-start(bf16[272,1024]{1,0:T(8,128)(2,1)S(1)} %pad_maximum_fusion), channel_id=1, source_target_pairs={{0,8},{4,12},{8,0},{12,4},{1,9},{5,13},{9,1},{13,5},{2,10},{6,14},... | collective-permute-start | bytes 1671176 | tf_op jit(solution)/shard_map/ppermute | solution.py:405
  79.8 1.6 %copy-start.6 = (f32[3,128,1024]{2,1,0:T(8,128)}, f32[3,128,1024]{2,1,0:T(8,128)S(1)}, u32[]{:S(2)}) copy-start(f32[3,128,1024]{2,1,0:T(8,128)S(1)} %get-tuple-element.60.keep_ref) | copy-start | bytes 4718596
  79.8 19.1 %collective-permute-start.14 = (bf16[400,1024]{1,0:T(8,128)(2,1)S(1)}, bf16[400,1024]{1,0:T(8,128)(2,1)S(1)}, u32[]{:S(2)}, u32[]{:S(2)}) collective-permute-start(bf16[400,1024]{1,0:T(8,128)(2,1)S(1)} %get-tuple-element.62), channel_id=1, source_target_pairs={{0,2},{1,3},{2,0},{3,1},{4,6},{5,7},{6,4},{7,5},{8,10},{9,11},{10,... | collective-permute-start | bytes 2457608 | tf_op jit(solution)/shard_map/ppermute | solution.py:393
  81.3 6.3 %copy-start.2 = (s32[1,1024]{1,0:T(1,128)S(1)}, s32[1,1024]{1,0:T(1,128)}, u32[]{:S(2)}) copy-start(s32[1,1024]{1,0:T(1,128)} %copy-done.1) | copy-start | bytes 12292
  81.4 2.6 %collective-permute-start.18 = (f32[6,160]{1,0:T(8,128)S(1)}, f32[6,160]{1,0:T(8,128)S(1)}, u32[]{:S(2)}, u32[]{:S(2)}) collective-permute-start(f32[6,160]{1,0:T(8,128)S(1)} %get-tuple-element.72), channel_id=1, source_target_pairs={{0,1},{1,0},{2,3},{3,2},{4,5},{5,4},{6,7},{7,6},{8,9},{9,8},{10,11... | collective-permute-start | bytes 11528 | tf_op jit(solution)/shard_map/ppermute | solution.py:418
  81.5 4.2 %collective-permute-start.19 = (f32[6,160]{1,0:T(8,128)S(1)}, f32[6,160]{1,0:T(8,128)S(1)}, u32[]{:S(2)}, u32[]{:S(2)}) collective-permute-start(f32[6,160]{1,0:T(8,128)S(1)} %get-tuple-element.73), channel_id=1, source_target_pairs={{0,4},{1,5},{2,6},{3,7},{4,0},{5,1},{6,2},{7,3},{8,12},{9,13},{10,... | collective-permute-start | bytes 11528 | tf_op jit(solution)/shard_map/ppermute | solution.py:418
  84.0 3.1 %collective-permute-start.20 = (f32[6,160]{1,0:T(8,128)S(1)}, f32[6,160]{1,0:T(8,128)S(1)}, u32[]{:S(2)}, u32[]{:S(2)}) collective-permute-start(f32[6,160]{1,0:T(8,128)S(1)} %get-tuple-element.74), channel_id=1, source_target_pairs={{0,5},{1,4},{2,7},{3,6},{4,1},{5,0},{6,3},{7,2},{8,13},{9,12},{10,... | collective-permute-start | bytes 11528 | tf_op jit(solution)/shard_map/ppermute | solution.py:418
  87.6 11.3 %copy-start.7 = (f32[3,128,1024]{2,1,0:T(8,128)S(1)}, f32[3,128,1024]{2,1,0:T(8,128)}, u32[]{:S(2)}) copy-start(f32[3,128,1024]{2,1,0:T(8,128)} %copy-done.6) | copy-start | bytes 4718596
  100.1 2.5 %collective-permute-start.17 = (f32[3,72,1024]{2,1,0:T(8,128)S(1)}, f32[3,72,1024]{2,1,0:T(8,128)S(1)}, u32[]{:S(2)}, u32[]{:S(2)}) collective-permute-start(f32[3,72,1024]{2,1,0:T(8,128)S(1)} %get-tuple-element.65), channel_id=1, source_target_pairs={{0,1},{1,0},{2,3},{3,2},{4,5},{5,4},{6,7},{7,6},{8,9},{9,8},{10,11... | collective-permute-start | bytes 2654216 | tf_op jit(solution)/shard_map/ppermute | solution.py:390

commit v7 on v6

--- a/solution.py
+++ b/solution.py
@@ -292,12 +292,16 @@
             )
 
 
-def _finish_kernel(per_core, piece, code_ref, _, swap_ref, line_ref, lines_ref, out_ref, mass_ref, sem):
+def _finish_kernel(per_core, piece, code_ref, mine_ref, swap_ref, line_ref, lines_ref, out_ref, mass_ref, sems):
     other = 1 - code_ref[2]
-    copy = pltpu.make_async_copy(
-        swap_ref.at[:, pl.ds(0, piece)], out_ref.at[pl.ds(other * per_core, per_core)], sem
-    )
-    copy.start()
+    copies = [
+        pltpu.make_async_copy(mine_ref, out_ref.at[pl.ds(code_ref[2] * per_core, per_core)], sems.at[0]),
+        pltpu.make_async_copy(
+            swap_ref.at[:, pl.ds(0, piece)], out_ref.at[pl.ds(other * per_core, per_core)], sems.at[1]
+        ),
+    ]
+    for copy in copies:
+        copy.start()
     mine = lines_ref[:per_core]
     theirs = line_ref[:, 0]
     lines = jnp.where(
@@ -305,7 +309,8 @@
     )
     here = lax.rem(code_ref[2] + code_ref[1], 2)
     mass_ref[...] = jnp.where(here == 0, lines[:, :piece], lines[:, piece : 2 * piece])
-    copy.wait()
+    for copy in copies:
+        copy.wait()
 
 
 def _params():
@@ -602,8 +607,8 @@
                 behind(per_core),
             ]
         if mine:
-            out_specs = [one_cell((1, piece, width), lambda n, c: (c[2] * per_core + n, 0, 0))]
-            out_shape = [jax.ShapeDtypeStruct((cells_local, piece, width), jnp.float32)]
+            out_specs = [one_cell((1, piece, width), lambda n, c: (n, 0, 0))]
+            out_shape = [jax.ShapeDtypeStruct((per_core, piece, width), jnp.float32)]
         else:
             out_specs = [
                 one_cell((1, piece + 8, width), lambda n, c: (n, 0, 0)),
@@ -649,13 +654,12 @@
                 pl.BlockSpec((8, 128), lambda n, c: (0, 0)),
             ],
             out_specs=[anywhere, pl.BlockSpec((cells_local, piece), lambda n, c: (0, 0))],
-            scratch_shapes=[pltpu.SemaphoreType.DMA(())],
+            scratch_shapes=[pltpu.SemaphoreType.DMA((2,))],
         ),
         out_shape=[
-            jax.ShapeDtypeStruct(out.shape, jnp.float32),
+            jax.ShapeDtypeStruct((cells_local, piece, width), jnp.float32),
             jax.ShapeDtypeStruct((cells_local, piece), jnp.float32),
         ],
-        input_output_aliases={1: 0},
         compiler_params=_params(),
         cost_estimate=busy,
     )(code, out, swapped, swapped, lines_mine)

time: 105 us -> 105 us (level)
  waiting for transfers between devices: 48.9 us -> 50.1 us
    pallas_call x2, Pallas kernels: 3.66 us -> 2.49 us  [update(): pl.pallas_call(functools.partial(_update_kernel, per_core, chips, piece,...]
    ppermute x5, waiting for transfers between devices: 0.87 us -> 2.02 us  [hop_core(): return lax.ppermute(v, 'frame', [(i, i ^ 1) for i in range(frame_count)])]
  transfers between devices with their start and end apart: 21 -> 21, of which waited for: 10 -> 11; matrix products, arithmetic and copies ran while one was open for 3% -> 3% of each run, Pallas kernels for 21% -> 20%
where the time goes in v7:
time: 105 us
  waiting for transfers between devices  50.1 us (48%)
  Pallas kernels  24.8 us (24%)
  starting transfers between devices  24.6 us (23%)
  local copies, waits for them, and re-layouts  3.27 us (3%)
  other arithmetic  1.18 us (1%)
    ppermute x5, waiting for transfers between devices, hop_chip(): lax.ppermute(v, 'frame', [(a * cores + c, (a + s) % chips * cores + c) fo...  21.4 us
    ppermute x4, waiting for transfers between devices, hop_partner(): lax.ppermute(v, 'cell', [(i, (i + half) % cell_count) for i in range(cell...  13.5 us
    pallas_call x3, Pallas kernels, _cell_call(): pl.pallas_call(functools.partial(_cell_kernel, sources, window, reach, pi...  13.3 us
    ppermute x2, waiting for transfers between devices, hop_member(): lax.ppermute(v, 'cell', [(b * half + i, b * half + (i + s) % half) for b...  10.9 us
    ppermute x4, starting transfers between devices, hop_partner(): lax.ppermute(v, 'cell', [(i, (i + half) % cell_count) for i in range(cell...  9.72 us
    ppermute x5, starting transfers between devices, hop_chip(): lax.ppermute(v, 'frame', [(a * cores + c, (a + s) % chips * cores + c) fo...  6.6 us
    ppermute x3, starting transfers between devices, hop_any(): return lax.ppermute(v, ('cell', 'frame'), pairs)  3.46 us
    pallas_call x2, Pallas kernels, on_device(): pl.pallas_call(functools.partial(_pick_kernel, [seg(0, t)]), out_shape=[b...  2.51 us
  transfers between devices with their start and end apart: 21, of which 11 were waited for; matrix products, arithmetic and copies ran while one was open for 3% of the time, Pallas kernels for 20%

profile of v7, /device:TPU:0, one launch (start us, length us, event | category | flops | bytes accessed | tf_op | source)
XLA Modules:
  0.0 104.9 jit_solution(6808007603686589275)
XLA Ops:
  0.6 4.1 %collective-permute-start = (f32[6]{0:T(128)}, f32[6]{0:T(128)S(1)}, u32[]{:S(2)}, u32[]{:S(2)}) collective-permute-start(f32[6]{0:T(128)} %refs_1_.1), channel_id=1, source_target_pairs={{0,8},{4,12},{8,0},{12,4},{1,9},{5,13},{9,1},{13,5},{2,10},{6,14},... | collective-permute-start | bytes 80 | tf_op jit(solution)/shard_map/ppermute | solution.py:410
  4.7 1.0 constant_dynamic-slice_fusion
  6.7 1.6 %copy-done.3 = bf16[1024,1024]{1,0:T(8,128)(2,1)S(1)} copy-done((bf16[1024,1024]{1,0:T(8,128)(2,1)S(1)}, bf16[1024,1024]{1,0:T(8,128)(2,1)}, u32[]{:S(2)}) %copy-start.3) | copy-done | bytes 2097176
  8.3 2.0 %shard_map.67 = (s32[1,1024]{1,0:T(1,128)S(1)}, s32[1,1024]{1,0:T(1,128)S(1)}, f32[64,128]{1,0:T(8,128)S(1)}, bf16[528,1024]{1,0:T(8,128)(2,1)S(1)}) custom-call(s32[1,1024]{1,0:T(1,128)S(1)} %fusion.12.rel_ref, bf16[1024,1024]{1,0:T(8,128)(2,1)S(1)} %copy-done.3), custom_call_target="tpu_custom_call" | custom-call | flops 20000000000 | bytes 1000000000 | tf_op jit(solution)/shard_map/pallas_call | solution.py:459
  10.3 1.9 %collective-permute-start.7 = (bf16[528,1024]{1,0:T(8,128)(2,1)S(1)}, bf16[528,1024]{1,0:T(8,128)(2,1)S(1)}, u32[]{:S(2)}, u32[]{:S(2)}) collective-permute-start(bf16[528,1024]{1,0:T(8,128)(2,1)S(1)} %get-tuple-element.43), channel_id=1, source_target_pairs={{0,4},{4,0},{8,12},{12,8},{1,5},{5,1},{9,13},{13,9},{2,6},{6,2},{1... | collective-permute-start | bytes 3244040 | tf_op jit(solution)/shard_map/ppermute | solution.py:405
  12.3 13.5 %collective-permute-done.1.refs_2_ = bf16[3,64,1024]{2,1,0:T(8,128)(2,1)S(1)} collective-permute-done((bf16[3,64,1024]{2,1,0:T(8,128)(2,1)S(1)}, bf16[3,64,1024]{2,1,0:T(8,128)(2,1)S(1)}, u32[]{:S(2)}, u32[]{:S(2)}) %collective-permute-start.1) | collective-permute-done | bytes 393248 | tf_op jit(solution)/shard_map/ppermute | solution.py:410
  25.8 1.5 %collective-permute-start.2 = (bf16[3,64,1024]{2,1,0:T(8,128)(2,1)S(1)}, bf16[3,64,1024]{2,1,0:T(8,128)(2,1)S(1)}, u32[]{:S(2)}, u32[]{:S(2)}) collective-permute-start(bf16[3,64,1024]{2,1,0:T(8,128)(2,1)S(1)} %collective-permute-done.1.refs_2_), channel_id=1, source_target_pairs={{0,16},{16,0},{1,17},{17,1},{2,18},{18,2},{3,19},{19,3},{4,20},{20... | collective-permute-start | bytes 1179656 | tf_op jit(solution)/shard_map/ppermute | solution.py:413
  27.3 1.5 %collective-permute-start.3 = (bf16[3,64,1024]{2,1,0:T(8,128)(2,1)S(1)}, bf16[3,64,1024]{2,1,0:T(8,128)(2,1)S(1)}, u32[]{:S(2)}, u32[]{:S(2)}) collective-permute-start(bf16[3,64,1024]{2,1,0:T(8,128)(2,1)S(1)} %collective-permute-done.1.refs_2_), channel_id=1, source_target_pairs={{0,2},{1,3},{2,0},{3,1},{4,6},{5,7},{6,4},{7,5},{8,10},{9,11},{10,... | collective-permute-start | bytes 1179656 | tf_op jit(solution)/shard_map/ppermute | solution.py:398
  28.8 1.2 %shard_map.68 = bf16[528,1024]{1,0:T(8,128)(2,1)S(1)} custom-call(s32[1,1024]{1,0:T(1,128)S(1)} %get-tuple-element.58.flat_ref, f32[64,128]{1,0:T(8,128)S(1)} %get-tuple-element.41.meta_ref, bf16[1024,1024]{1,0:T(8,128)(2,1)S(1)} %copy-done.4), custom_call_target="tpu_custom_call" | custom-call | flops 20000000000 | bytes 1000000000 | tf_op jit(solution)/shard_map/pallas_call | solution.py:472
  30.2 6.8 %collective-permute-done.3.refs_4_ = bf16[3,64,1024]{2,1,0:T(8,128)(2,1)S(1)} collective-permute-done((bf16[3,64,1024]{2,1,0:T(8,128)(2,1)S(1)}, bf16[3,64,1024]{2,1,0:T(8,128)(2,1)S(1)}, u32[]{:S(2)}, u32[]{:S(2)}) %collective-permute-start.3) | collective-permute-done | bytes 393248 | tf_op jit(solution)/shard_map/ppermute | solution.py:398
  37.6 1.6 %collective-permute-start.5 = (bf16[3,32,1024]{2,1,0:T(8,128)(2,1)S(1)}, bf16[3,32,1024]{2,1,0:T(8,128)(2,1)S(1)}, u32[]{:S(2)}, u32[]{:S(2)}) collective-permute-start(bf16[3,32,1024]{2,1,0:T(8,128)(2,1)S(1)} %slice.71), channel_id=1, source_target_pairs={{0,2},{1,3},{2,0},{3,1},{4,6},{5,7},{6,4},{7,5},{8,10},{9,11},{10,... | collective-permute-start | bytes 589832 | tf_op jit(solution)/shard_map/ppermute | solution.py:398
  39.1 1.3 %shard_map.69.refs_7_ = bf16[528,1024]{1,0:T(8,128)(2,1)S(1)} custom-call(s32[1,1024]{1,0:T(1,128)S(1)} %get-tuple-element.58.flat_ref, f32[64,128]{1,0:T(8,128)S(1)} %get-tuple-element.41.meta_ref, bf16[1024,1024]{1,0:T(8,128)(2,1)S(1)} %copy-done.4), custom_call_target="tpu_custom_call" | custom-call | flops 20000000000 | bytes 1000000000 | tf_op jit(solution)/shard_map/pallas_call | solution.py:482
  40.5 4.0 %collective-permute-done.7.refs_9_ = bf16[528,1024]{1,0:T(8,128)(2,1)S(1)} collective-permute-done((bf16[528,1024]{1,0:T(8,128)(2,1)S(1)}, bf16[528,1024]{1,0:T(8,128)(2,1)S(1)}, u32[]{:S(2)}, u32[]{:S(2)}) %collective-permute-start.7) | collective-permute-done | bytes 1081376 | tf_op jit(solution)/shard_map/ppermute | solution.py:405
  44.5 1.3 %shard_map.75.refs_3_ = bf16[528,1024]{1,0:T(8,128)(2,1)S(1)} custom-call(s32[1,1024]{1,0:T(1,128)S(1)} %get-tuple-element.58.flat_ref, f32[64,128]{1,0:T(8,128)S(1)} %get-tuple-element.41.meta_ref, bf16[1024,1024]{1,0:T(8,128)(2,1)S(1)} %copy-done.4), custom_call_target="tpu_custom_call" | custom-call | flops 20000000000 | bytes 1000000000 | tf_op jit(solution)/shard_map/pallas_call | solution.py:482
  47.2 3.3 %shard_map.70 = (f32[1,128,1024]{2,1,0:T(8,128)S(1)}, f32[1,8,256]{2,1,0:T(8,128)S(1)}, f32[1,8,640]{2,1,0:T(8,128)S(1)}, bf16[128,1024]{1,0:T(8,128)(2,1)S(1)}) custom-call(s32[3]{0:T(128)S(1)} %pad_add_fusion.refs_0_.code_ref, f32[6]{0:T(128)S(1)} %collective-permute-done.refs_1_, bf16[3,64,1024]{2,1,0:T(8,128)(2,1)S(1)} %collective-permute-done.1.refs_2_, ...), custom_call_target="tpu_custom_call" | custom-call | flops 20000000000 | bytes 1 | tf_op jit(solution)/shard_map/pallas_call | solution.py:333
  50.5 1.8 %collective-permute-start.9 = (bf16[128,1024]{1,0:T(8,128)(2,1)S(1)}, bf16[128,1024]{1,0:T(8,128)(2,1)S(1)}, u32[]{:S(2)}, u32[]{:S(2)}) collective-permute-start(bf16[128,1024]{1,0:T(8,128)(2,1)S(1)} %get-tuple-element.50), channel_id=1, source_target_pairs={{0,2},{1,3},{2,0},{3,1},{4,6},{5,7},{6,4},{7,5},{8,10},{9,11},{10,... | collective-permute-start | bytes 786440 | tf_op jit(solution)/shard_map/ppermute | solution.py:398
  52.4 4.3 %shard_map.72 = (f32[2,128,1024]{2,1,0:T(8,128)S(1)}, f32[2,8,256]{2,1,0:T(8,128)S(1)}, f32[2,8,640]{2,1,0:T(8,128)S(1)}, bf16[272,1024]{1,0:T(8,128)(2,1)S(1)}) custom-call(s32[3]{0:T(128)S(1)} %pad_add_fusion.refs_0_.code_ref, f32[6]{0:T(128)S(1)} %collective-permute-done.refs_1_, bf16[3,64,1024]{2,1,0:T(8,128)(2,1)S(1)} %collective-permute-done.1.refs_2_, ...), custom_call_target="tpu_custom_call" | custom-call | flops 20000000000 | bytes 1 | tf_op jit(solution)/shard_map/pallas_call | solution.py:333
  57.0 2.0 %collective-permute-done.9 = bf16[128,1024]{1,0:T(8,128)(2,1)S(1)} collective-permute-done((bf16[128,1024]{1,0:T(8,128)(2,1)S(1)}, bf16[128,1024]{1,0:T(8,128)(2,1)S(1)}, u32[]{:S(2)}, u32[]{:S(2)}) %collective-permute-start.9) | collective-permute-done | bytes 262176 | tf_op jit(solution)/shard_map/ppermute | solution.py:398
  59.1 2.9 %collective-permute-start.15 = (bf16[128,1024]{1,0:T(8,128)(2,1)S(1)}, bf16[128,1024]{1,0:T(8,128)(2,1)S(1)}, u32[]{:S(2)}, u32[]{:S(2)}) collective-permute-start(bf16[128,1024]{1,0:T(8,128)(2,1)S(1)} %fusion.1), channel_id=1, source_target_pairs={{0,8},{4,12},{8,0},{12,4},{1,9},{5,13},{9,1},{13,5},{2,10},{6,14},... | collective-permute-start | bytes 786440 | tf_op jit(solution)/shard_map/ppermute | solution.py:410
  62.0 6.9 %collective-permute-done.12.refs_5_ = bf16[528,1024]{1,0:T(8,128)(2,1)S(1)} collective-permute-done((bf16[528,1024]{1,0:T(8,128)(2,1)S(1)}, bf16[528,1024]{1,0:T(8,128)(2,1)S(1)}, u32[]{:S(2)}, u32[]{:S(2)}) %collective-permute-start.12) | collective-permute-done | bytes 1081376 | tf_op jit(solution)/shard_map/ppermute | solution.py:405
  68.9 2.3 %collective-permute-done.10 = bf16[272,1024]{1,0:T(8,128)(2,1)S(1)} collective-permute-done((bf16[272,1024]{1,0:T(8,128)(2,1)S(1)}, bf16[272,1024]{1,0:T(8,128)(2,1)S(1)}, u32[]{:S(2)}, u32[]{:S(2)}) %collective-permute-start.10) | collective-permute-done | bytes 557088 | tf_op jit(solution)/shard_map/ppermute | solution.py:398
  71.5 2.6 %collective-permute-start.16 = (bf16[272,1024]{1,0:T(8,128)(2,1)S(1)}, bf16[272,1024]{1,0:T(8,128)(2,1)S(1)}, u32[]{:S(2)}, u32[]{:S(2)}) collective-permute-start(bf16[272,1024]{1,0:T(8,128)(2,1)S(1)} %pad_maximum_fusion), channel_id=1, source_target_pairs={{0,8},{4,12},{8,0},{12,4},{1,9},{5,13},{9,1},{13,5},{2,10},{6,14},... | collective-permute-start | bytes 1671176 | tf_op jit(solution)/shard_map/ppermute | solution.py:410
  74.1 5.7 %shard_map.76 = (f32[3,128,1024]{2,1,0:T(8,128)S(1)}, f32[3,8,256]{2,1,0:T(8,128)S(1)}, f32[3,8,640]{2,1,0:T(8,128)S(1)}, bf16[400,1024]{1,0:T(8,128)(2,1)S(1)}) custom-call(s32[3]{0:T(128)S(1)} %pad_add_fusion.refs_0_.code_ref, f32[6]{0:T(128)S(1)} %copy-done.5, bf16[6,256,1024]{2,1,0:T(8,128)(2,1)S(1)} %copy-done, ...), custom_call_target="tpu_custom_call" | custom-call | flops 20000000000 | bytes 1 | tf_op jit(solution)/shard_map/pallas_call | solution.py:333
  79.8 1.4 %collective-permute-start.14 = (bf16[400,1024]{1,0:T(8,128)(2,1)S(1)}, bf16[400,1024]{1,0:T(8,128)(2,1)S(1)}, u32[]{:S(2)}, u32[]{:S(2)}) collective-permute-start(bf16[400,1024]{1,0:T(8,128)(2,1)S(1)} %get-tuple-element.62), channel_id=1, source_target_pairs={{0,2},{1,3},{2,0},{3,1},{4,6},{5,7},{6,4},{7,5},{8,10},{9,11},{10,... | collective-permute-start | bytes 2457608 | tf_op jit(solution)/shard_map/ppermute | solution.py:398
  81.5 2.5 %collective-permute-start.19 = (f32[6,160]{1,0:T(8,128)S(1)}, f32[6,160]{1,0:T(8,128)S(1)}, u32[]{:S(2)}, u32[]{:S(2)}) collective-permute-start(f32[6,160]{1,0:T(8,128)S(1)} %get-tuple-element.73), channel_id=1, source_target_pairs={{0,4},{1,5},{2,6},{3,7},{4,0},{5,1},{6,2},{7,3},{8,12},{9,13},{10,... | collective-permute-start | bytes 11528 | tf_op jit(solution)/shard_map/ppermute | solution.py:423
  85.6 1.4 %collective-permute-done.20 = f32[6,160]{1,0:T(8,128)S(1)} collective-permute-done((f32[6,160]{1,0:T(8,128)S(1)}, f32[6,160]{1,0:T(8,128)S(1)}, u32[]{:S(2)}, u32[]{:S(2)}) %collective-permute-start.20) | collective-permute-done | bytes 3872 | tf_op jit(solution)/shard_map/ppermute | solution.py:423
  87.6 0.9 shard_map.81
  88.5 10.3 %collective-permute-done.14.refs_0_.refs_1_ = bf16[400,1024]{1,0:T(8,128)(2,1)S(1)} collective-permute-done((bf16[400,1024]{1,0:T(8,128)(2,1)S(1)}, bf16[400,1024]{1,0:T(8,128)(2,1)S(1)}, u32[]{:S(2)}, u32[]{:S(2)}) %collective-permute-start.14) | collective-permute-done | bytes 819232 | tf_op jit(solution)/shard_map/ppermute | solution.py:398
  98.9 1.2 %shard_map.78 = (f32[3,72,1024]{2,1,0:T(8,128)S(1)}, f32[8,128]{1,0:T(8,128)S(1)}) custom-call(s32[3]{0:T(128)S(1)} %pad_add_fusion.refs_0_.code_ref, f32[3,128,1024]{2,1,0:T(8,128)S(1)} %copy-done.7, f32[3,8,256]{2,1,0:T(8,128)S(1)} %get-tuple-element.61.mass_ref, bf16[400,1024]{1,0:T(8,128)(2,1)S(1)} %collective-permute-done.14.refs_0_.refs_1_, ...), custom_call_target="tpu_custom_call" | custom-call | flops 20000000000 | bytes 1 | tf_op jit(solution)/shard_map/pallas_call | solution.py:621
  100.2 1.2 %shard_map.77.mine_ref = f32[3,64,1024]{2,1,0:T(8,128)S(1)} custom-call(s32[3]{0:T(128)S(1)} %pad_add_fusion.refs_0_.code_ref, f32[3,128,1024]{2,1,0:T(8,128)S(1)} %copy-done.7, f32[3,8,256]{2,1,0:T(8,128)S(1)} %get-tuple-element.61.mass_ref, bf16[400,1024]{1,0:T(8,128)(2,1)S(1)} %collective-permute-done.14.refs_0_.refs_1_, ...), custom_call_target="tpu_custom_call" | custom-call | flops 20000000000 | bytes 1 | tf_op jit(solution)/shard_map/pallas_call | solution.py:621
  101.5 1.2 %collective-permute-done.17.swap_ref.line_ref = f32[3,72,1024]{2,1,0:T(8,128)S(1)} collective-permute-done((f32[3,72,1024]{2,1,0:T(8,128)S(1)}, f32[3,72,1024]{2,1,0:T(8,128)S(1)}, u32[]{:S(2)}, u32[]{:S(2)}) %collective-permute-start.17) | collective-permute-done | bytes 884768 | tf_op jit(solution)/shard_map/ppermute | solution.py:395
  102.6 2.3 %shard_map.79 = (f32[6,64,1024]{2,1,0:T(8,128)}, f32[6,64]{1,0:T(8,128)}) custom-call(s32[3]{0:T(128)S(1)} %pad_add_fusion.refs_0_.code_ref, f32[3,64,1024]{2,1,0:T(8,128)S(1)} %shard_map.77.mine_ref, f32[3,72,1024]{2,1,0:T(8,128)S(1)} %collective-permute-done.17.swap_ref.line_ref, f32[3,72,1024]{2,1,0:T(8,128)S(1)} %collective-permute-done.17.swap_ref.line_ref, ...), custom_call_target="tpu_custom_call" | custom-call | flops 20000000000 | bytes 1 | tf_op jit(solution)/shard_map/pallas_call | solution.py:645
  (64 shorter events, 6.3 us)
Async XLA Ops:
  0.6 38.5 %collective-permute-start = (f32[6]{0:T(128)}, f32[6]{0:T(128)S(1)}, u32[]{:S(2)}, u32[]{:S(2)}) collective-permute-start(f32[6]{0:T(128)} %refs_1_.1), channel_id=1, source_target_pairs={{0,8},{4,12},{8,0},{12,4},{1,9},{5,13},{9,1},{13,5},{2,10},{6,14},... | collective-permute-start | bytes 80 | tf_op jit(solution)/shard_map/ppermute | solution.py:410
  5.8 20.1 %collective-permute-start.1 = (bf16[3,64,1024]{2,1,0:T(8,128)(2,1)S(1)}, bf16[3,64,1024]{2,1,0:T(8,128)(2,1)S(1)}, u32[]{:S(2)}, u32[]{:S(2)}) collective-permute-start(bf16[3,64,1024]{2,1,0:T(8,128)(2,1)S(1)} %constant_dynamic-slice_fusion), channel_id=1, source_target_pairs={{0,8},{4,12},{8,0},{12,4},{1,9},{5,13},{9,1},{13,5},{2,10},{6,14},... | collective-permute-start | bytes 1179656 | tf_op jit(solution)/shard_map/ppermute | solution.py:410
  6.7 1.6 %copy-start.3 = (bf16[1024,1024]{1,0:T(8,128)(2,1)S(1)}, bf16[1024,1024]{1,0:T(8,128)(2,1)}, u32[]{:S(2)}) copy-start(bf16[1024,1024]{1,0:T(8,128)(2,1)} %frames_ref.7) | copy-start | bytes 6291460
  8.3 2.0 %copy-start.1 = (s32[1,1024]{1,0:T(1,128)}, s32[1,1024]{1,0:T(1,128)S(1)}, u32[]{:S(2)}) copy-start(s32[1,1024]{1,0:T(1,128)S(1)} %fusion.12.rel_ref) | copy-start | bytes 12292
  8.3 20.6 %copy-start.4 = (bf16[1024,1024]{1,0:T(8,128)(2,1)S(1)}, bf16[1024,1024]{1,0:T(8,128)(2,1)}, u32[]{:S(2)}) copy-start(bf16[1024,1024]{1,0:T(8,128)(2,1)} %frames_ref.7) | copy-start | bytes 6291460
  10.3 34.2 %collective-permute-start.7 = (bf16[528,1024]{1,0:T(8,128)(2,1)S(1)}, bf16[528,1024]{1,0:T(8,128)(2,1)S(1)}, u32[]{:S(2)}, u32[]{:S(2)}) collective-permute-start(bf16[528,1024]{1,0:T(8,128)(2,1)S(1)} %get-tuple-element.43), channel_id=1, source_target_pairs={{0,4},{4,0},{8,12},{12,8},{1,5},{5,1},{9,13},{13,9},{2,6},{6,2},{1... | collective-permute-start | bytes 3244040 | tf_op jit(solution)/shard_map/ppermute | solution.py:405
  25.8 11.7 %collective-permute-start.2 = (bf16[3,64,1024]{2,1,0:T(8,128)(2,1)S(1)}, bf16[3,64,1024]{2,1,0:T(8,128)(2,1)S(1)}, u32[]{:S(2)}, u32[]{:S(2)}) collective-permute-start(bf16[3,64,1024]{2,1,0:T(8,128)(2,1)S(1)} %collective-permute-done.1.refs_2_), channel_id=1, source_target_pairs={{0,16},{16,0},{1,17},{17,1},{2,18},{18,2},{3,19},{19,3},{4,20},{20... | collective-permute-start | bytes 1179656 | tf_op jit(solution)/shard_map/ppermute | solution.py:413
  27.3 9.6 %collective-permute-start.3 = (bf16[3,64,1024]{2,1,0:T(8,128)(2,1)S(1)}, bf16[3,64,1024]{2,1,0:T(8,128)(2,1)S(1)}, u32[]{:S(2)}, u32[]{:S(2)}) collective-permute-start(bf16[3,64,1024]{2,1,0:T(8,128)(2,1)S(1)} %collective-permute-done.1.refs_2_), channel_id=1, source_target_pairs={{0,2},{1,3},{2,0},{3,1},{4,6},{5,7},{6,4},{7,5},{8,10},{9,11},{10,... | collective-permute-start | bytes 1179656 | tf_op jit(solution)/shard_map/ppermute | solution.py:398
  30.1 38.8 %collective-permute-start.12 = (bf16[528,1024]{1,0:T(8,128)(2,1)S(1)}, bf16[528,1024]{1,0:T(8,128)(2,1)S(1)}, u32[]{:S(2)}, u32[]{:S(2)}) collective-permute-start(bf16[528,1024]{1,0:T(8,128)(2,1)S(1)} %shard_map.68), channel_id=1, source_target_pairs={{0,4},{4,0},{8,12},{12,8},{1,5},{5,1},{9,13},{13,9},{2,6},{6,2},{1... | collective-permute-start | bytes 3244040 | tf_op jit(solution)/shard_map/ppermute | solution.py:405
  37.0 8.8 %collective-permute-start.4 = (bf16[3,32,1024]{2,1,0:T(8,128)(2,1)S(1)}, bf16[3,32,1024]{2,1,0:T(8,128)(2,1)S(1)}, u32[]{:S(2)}, u32[]{:S(2)}) collective-permute-start(bf16[3,32,1024]{2,1,0:T(8,128)(2,1)S(1)} %slice.70), channel_id=1, source_target_pairs={{0,16},{16,0},{1,17},{17,1},{2,18},{18,2},{3,19},{19,3},{4,20},{20... | collective-permute-start | bytes 589832 | tf_op jit(solution)/shard_map/ppermute | solution.py:413
  37.6 8.8 %collective-permute-start.5 = (bf16[3,32,1024]{2,1,0:T(8,128)(2,1)S(1)}, bf16[3,32,1024]{2,1,0:T(8,128)(2,1)S(1)}, u32[]{:S(2)}, u32[]{:S(2)}) collective-permute-start(bf16[3,32,1024]{2,1,0:T(8,128)(2,1)S(1)} %slice.71), channel_id=1, source_target_pairs={{0,2},{1,3},{2,0},{3,1},{4,6},{5,7},{6,4},{7,5},{8,10},{9,11},{10,... | collective-permute-start | bytes 589832 | tf_op jit(solution)/shard_map/ppermute | solution.py:398
  40.4 5.9 %collective-permute-start.6 = (bf16[528,1024]{1,0:T(8,128)(2,1)S(1)}, bf16[528,1024]{1,0:T(8,128)(2,1)S(1)}, u32[]{:S(2)}, u32[]{:S(2)}) collective-permute-start(bf16[528,1024]{1,0:T(8,128)(2,1)S(1)} %shard_map.69.refs_7_), channel_id=1, source_target_pairs={{0,1},{1,0},{2,3},{3,2},{4,5},{5,4},{6,7},{7,6},{8,9},{9,8},{10,11... | collective-permute-start | bytes 3244040 | tf_op jit(solution)/shard_map/ppermute | solution.py:395
  44.5 2.7 %collective-permute-start.8 = (bf16[528,1024]{1,0:T(8,128)(2,1)S(1)}, bf16[528,1024]{1,0:T(8,128)(2,1)S(1)}, u32[]{:S(2)}, u32[]{:S(2)}) collective-permute-start(bf16[528,1024]{1,0:T(8,128)(2,1)S(1)} %collective-permute-done.7.refs_9_), channel_id=1, source_target_pairs={{0,1},{1,0},{2,3},{3,2},{4,5},{5,4},{6,7},{7,6},{8,9},{9,8},{10,11... | collective-permute-start | bytes 3244040 | tf_op jit(solution)/shard_map/ppermute | solution.py:395
  45.8 28.3 %collective-permute-start.11 = (bf16[528,1024]{1,0:T(8,128)(2,1)S(1)}, bf16[528,1024]{1,0:T(8,128)(2,1)S(1)}, u32[]{:S(2)}, u32[]{:S(2)}) collective-permute-start(bf16[528,1024]{1,0:T(8,128)(2,1)S(1)} %shard_map.75.refs_3_), channel_id=1, source_target_pairs={{0,1},{1,0},{2,3},{3,2},{4,5},{5,4},{6,7},{7,6},{8,9},{9,8},{10,11... | collective-permute-start | bytes 3244040 | tf_op jit(solution)/shard_map/ppermute | solution.py:395
  50.5 8.5 %collective-permute-start.9 = (bf16[128,1024]{1,0:T(8,128)(2,1)S(1)}, bf16[128,1024]{1,0:T(8,128)(2,1)S(1)}, u32[]{:S(2)}, u32[]{:S(2)}) collective-permute-start(bf16[128,1024]{1,0:T(8,128)(2,1)S(1)} %get-tuple-element.50), channel_id=1, source_target_pairs={{0,2},{1,3},{2,0},{3,1},{4,6},{5,7},{6,4},{7,5},{8,10},{9,11},{10,... | collective-permute-start | bytes 786440 | tf_op jit(solution)/shard_map/ppermute | solution.py:398
  56.7 14.5 %collective-permute-start.10 = (bf16[272,1024]{1,0:T(8,128)(2,1)S(1)}, bf16[272,1024]{1,0:T(8,128)(2,1)S(1)}, u32[]{:S(2)}, u32[]{:S(2)}) collective-permute-start(bf16[272,1024]{1,0:T(8,128)(2,1)S(1)} %get-tuple-element.53), channel_id=1, source_target_pairs={{0,2},{1,3},{2,0},{3,1},{4,6},{5,7},{6,4},{7,5},{8,10},{9,11},{10,... | collective-permute-start | bytes 1671176 | tf_op jit(solution)/shard_map/ppermute | solution.py:398
  59.1 29.4 %collective-permute-start.15 = (bf16[128,1024]{1,0:T(8,128)(2,1)S(1)}, bf16[128,1024]{1,0:T(8,128)(2,1)S(1)}, u32[]{:S(2)}, u32[]{:S(2)}) collective-permute-start(bf16[128,1024]{1,0:T(8,128)(2,1)S(1)} %fusion.1), channel_id=1, source_target_pairs={{0,8},{4,12},{8,0},{12,4},{1,9},{5,13},{9,1},{13,5},{2,10},{6,14},... | collective-permute-start | bytes 786440 | tf_op jit(solution)/shard_map/ppermute | solution.py:410
  68.9 5.2 %collective-permute-start.13 = (bf16[528,1024]{1,0:T(8,128)(2,1)S(1)}, bf16[528,1024]{1,0:T(8,128)(2,1)S(1)}, u32[]{:S(2)}, u32[]{:S(2)}) collective-permute-start(bf16[528,1024]{1,0:T(8,128)(2,1)S(1)} %collective-permute-done.12.refs_5_), channel_id=1, source_target_pairs={{0,1},{1,0},{2,3},{3,2},{4,5},{5,4},{6,7},{7,6},{8,9},{9,8},{10,11... | collective-permute-start | bytes 3244040 | tf_op jit(solution)/shard_map/ppermute | solution.py:395
  71.5 2.6 %copy-start = (bf16[6,256,1024]{2,1,0:T(8,128)(2,1)S(1)}, bf16[6,256,1024]{2,1,0:T(8,128)(2,1)}, u32[]{:S(2)}) copy-start(bf16[6,256,1024]{2,1,0:T(8,128)(2,1)} %refs_2_.1) | copy-start | bytes 9437188
  71.5 2.6 %copy-start.5 = (f32[6]{0:T(128)S(1)}, f32[6]{0:T(128)}, u32[]{:S(2)}) copy-start(f32[6]{0:T(128)} %refs_1_.1) | copy-start | bytes 76
  71.5 27.4 %collective-permute-start.16 = (bf16[272,1024]{1,0:T(8,128)(2,1)S(1)}, bf16[272,1024]{1,0:T(8,128)(2,1)S(1)}, u32[]{:S(2)}, u32[]{:S(2)}) collective-permute-start(bf16[272,1024]{1,0:T(8,128)(2,1)S(1)} %pad_maximum_fusion), channel_id=1, source_target_pairs={{0,8},{4,12},{8,0},{12,4},{1,9},{5,13},{9,1},{13,5},{2,10},{6,14},... | collective-permute-start | bytes 1671176 | tf_op jit(solution)/shard_map/ppermute | solution.py:410
  79.8 1.6 %copy-start.6 = (f32[3,128,1024]{2,1,0:T(8,128)}, f32[3,128,1024]{2,1,0:T(8,128)S(1)}, u32[]{:S(2)}) copy-start(f32[3,128,1024]{2,1,0:T(8,128)S(1)} %get-tuple-element.60.keep_ref) | copy-start | bytes 4718596
  79.8 19.1 %collective-permute-start.14 = (bf16[400,1024]{1,0:T(8,128)(2,1)S(1)}, bf16[400,1024]{1,0:T(8,128)(2,1)S(1)}, u32[]{:S(2)}, u32[]{:S(2)}) collective-permute-start(bf16[400,1024]{1,0:T(8,128)(2,1)S(1)} %get-tuple-element.62), channel_id=1, source_target_pairs={{0,2},{1,3},{2,0},{3,1},{4,6},{5,7},{6,4},{7,5},{8,10},{9,11},{10,... | collective-permute-start | bytes 2457608 | tf_op jit(solution)/shard_map/ppermute | solution.py:398
  81.3 6.3 %copy-start.2 = (s32[1,1024]{1,0:T(1,128)S(1)}, s32[1,1024]{1,0:T(1,128)}, u32[]{:S(2)}) copy-start(s32[1,1024]{1,0:T(1,128)} %copy-done.1) | copy-start | bytes 12292
  81.4 2.6 %collective-permute-start.18 = (f32[6,160]{1,0:T(8,128)S(1)}, f32[6,160]{1,0:T(8,128)S(1)}, u32[]{:S(2)}, u32[]{:S(2)}) collective-permute-start(f32[6,160]{1,0:T(8,128)S(1)} %get-tuple-element.72), channel_id=1, source_target_pairs={{0,1},{1,0},{2,3},{3,2},{4,5},{5,4},{6,7},{7,6},{8,9},{9,8},{10,11... | collective-permute-start | bytes 11528 | tf_op jit(solution)/shard_map/ppermute | solution.py:423
  81.5 4.2 %collective-permute-start.19 = (f32[6,160]{1,0:T(8,128)S(1)}, f32[6,160]{1,0:T(8,128)S(1)}, u32[]{:S(2)}, u32[]{:S(2)}) collective-permute-start(f32[6,160]{1,0:T(8,128)S(1)} %get-tuple-element.73), channel_id=1, source_target_pairs={{0,4},{1,5},{2,6},{3,7},{4,0},{5,1},{6,2},{7,3},{8,12},{9,13},{10,... | collective-permute-start | bytes 11528 | tf_op jit(solution)/shard_map/ppermute | solution.py:423
  84.0 3.1 %collective-permute-start.20 = (f32[6,160]{1,0:T(8,128)S(1)}, f32[6,160]{1,0:T(8,128)S(1)}, u32[]{:S(2)}, u32[]{:S(2)}) collective-permute-start(f32[6,160]{1,0:T(8,128)S(1)} %get-tuple-element.74), channel_id=1, source_target_pairs={{0,5},{1,4},{2,7},{3,6},{4,1},{5,0},{6,3},{7,2},{8,13},{9,12},{10,... | collective-permute-start | bytes 11528 | tf_op jit(solution)/shard_map/ppermute | solution.py:423
  87.6 11.3 %copy-start.7 = (f32[3,128,1024]{2,1,0:T(8,128)S(1)}, f32[3,128,1024]{2,1,0:T(8,128)}, u32[]{:S(2)}) copy-start(f32[3,128,1024]{2,1,0:T(8,128)} %copy-done.6) | copy-start | bytes 4718596
  100.1 2.5 %collective-permute-start.17 = (f32[3,72,1024]{2,1,0:T(8,128)S(1)}, f32[3,72,1024]{2,1,0:T(8,128)S(1)}, u32[]{:S(2)}, u32[]{:S(2)}) collective-permute-start(f32[3,72,1024]{2,1,0:T(8,128)S(1)} %get-tuple-element.65), channel_id=1, source_target_pairs={{0,1},{1,0},{2,3},{3,2},{4,5},{5,4},{6,7},{7,6},{8,9},{9,8},{10,11... | collective-permute-start | bytes 2654216 | tf_op jit(solution)/shard_map/ppermute | solution.py:395

commit v8 on v6

--- a/solution.py
+++ b/solution.py
@@ -351,7 +351,7 @@
             ],
         ),
         out_shape=out_shape,
-        compiler_params=pltpu.CompilerParams(vmem_limit_bytes=44 * 1024 * 1024),
+        compiler_params=pltpu.CompilerParams(vmem_limit_bytes=28 * 1024 * 1024),
         cost_estimate=busy,
     )(code, sharp, *arrays, *row_blocks, *earlier)
 

time: 105 us -> 105 us (level)
  no operation moved by 1% of the time
where the time goes in v8:
time: 105 us
  waiting for transfers between devices  48.9 us (47%)
  Pallas kernels  25.7 us (24%)
  starting transfers between devices  24.6 us (23%)
  local copies, waits for them, and re-layouts  3.27 us (3%)
  other arithmetic  1.18 us (1%)
    ppermute x5, waiting for transfers between devices, hop_chip(): lax.ppermute(v, 'frame', [(a * cores + c, (a + s) % chips * cores + c) fo...  21.4 us
    ppermute x4, waiting for transfers between devices, hop_partner(): lax.ppermute(v, 'cell', [(i, (i + half) % cell_count) for i in range(cell...  13.5 us
    pallas_call x3, Pallas kernels, _cell_call(): pl.pallas_call(functools.partial(_cell_kernel, sources, window, reach, pi...  13.3 us
    ppermute x2, waiting for transfers between devices, hop_member(): lax.ppermute(v, 'cell', [(b * half + i, b * half + (i + s) % half) for b...  10.9 us
    ppermute x4, starting transfers between devices, hop_partner(): lax.ppermute(v, 'cell', [(i, (i + half) % cell_count) for i in range(cell...  9.72 us
    ppermute x5, starting transfers between devices, hop_chip(): lax.ppermute(v, 'frame', [(a * cores + c, (a + s) % chips * cores + c) fo...  6.6 us
    pallas_call x2, Pallas kernels, update(): pl.pallas_call(functools.partial(_update_kernel, per_core, chips, piece,...  3.66 us
    ppermute x3, starting transfers between devices, hop_any(): return lax.ppermute(v, ('cell', 'frame'), pairs)  3.46 us
  transfers between devices with their start and end apart: 21, of which 10 were waited for; matrix products, arithmetic and copies ran while one was open for 3% of the time, Pallas kernels for 21%

profile of v8, /device:TPU:0, one launch (start us, length us, event | category | flops | bytes accessed | tf_op | source)
XLA Modules:
  0.0 104.7 jit_solution(2356822073979083916)
XLA Ops:
  0.6 4.1 %collective-permute-start = (f32[6]{0:T(128)}, f32[6]{0:T(128)S(1)}, u32[]{:S(2)}, u32[]{:S(2)}) collective-permute-start(f32[6]{0:T(128)} %refs_1_.1), channel_id=1, source_target_pairs={{0,8},{4,12},{8,0},{12,4},{1,9},{5,13},{9,1},{13,5},{2,10},{6,14},... | collective-permute-start | bytes 80 | tf_op jit(solution)/shard_map/ppermute | solution.py:405
  4.7 1.0 constant_dynamic-slice_fusion
  6.7 1.6 %copy-done.3 = bf16[1024,1024]{1,0:T(8,128)(2,1)S(1)} copy-done((bf16[1024,1024]{1,0:T(8,128)(2,1)S(1)}, bf16[1024,1024]{1,0:T(8,128)(2,1)}, u32[]{:S(2)}) %copy-start.3) | copy-done | bytes 2097176
  8.3 2.0 %shard_map.67 = (s32[1,1024]{1,0:T(1,128)S(1)}, s32[1,1024]{1,0:T(1,128)S(1)}, f32[64,128]{1,0:T(8,128)S(1)}, bf16[528,1024]{1,0:T(8,128)(2,1)S(1)}) custom-call(s32[1,1024]{1,0:T(1,128)S(1)} %fusion.12.rel_ref, bf16[1024,1024]{1,0:T(8,128)(2,1)S(1)} %copy-done.3), custom_call_target="tpu_custom_call" | custom-call | flops 20000000000 | bytes 1000000000 | tf_op jit(solution)/shard_map/pallas_call | solution.py:454
  10.3 1.9 %collective-permute-start.7 = (bf16[528,1024]{1,0:T(8,128)(2,1)S(1)}, bf16[528,1024]{1,0:T(8,128)(2,1)S(1)}, u32[]{:S(2)}, u32[]{:S(2)}) collective-permute-start(bf16[528,1024]{1,0:T(8,128)(2,1)S(1)} %get-tuple-element.43), channel_id=1, source_target_pairs={{0,4},{4,0},{8,12},{12,8},{1,5},{5,1},{9,13},{13,9},{2,6},{6,2},{1... | collective-permute-start | bytes 3244040 | tf_op jit(solution)/shard_map/ppermute | solution.py:400
  12.3 13.5 %collective-permute-done.1.refs_2_ = bf16[3,64,1024]{2,1,0:T(8,128)(2,1)S(1)} collective-permute-done((bf16[3,64,1024]{2,1,0:T(8,128)(2,1)S(1)}, bf16[3,64,1024]{2,1,0:T(8,128)(2,1)S(1)}, u32[]{:S(2)}, u32[]{:S(2)}) %collective-permute-start.1) | collective-permute-done | bytes 393248 | tf_op jit(solution)/shard_map/ppermute | solution.py:405
  25.8 1.5 %collective-permute-start.2 = (bf16[3,64,1024]{2,1,0:T(8,128)(2,1)S(1)}, bf16[3,64,1024]{2,1,0:T(8,128)(2,1)S(1)}, u32[]{:S(2)}, u32[]{:S(2)}) collective-permute-start(bf16[3,64,1024]{2,1,0:T(8,128)(2,1)S(1)} %collective-permute-done.1.refs_2_), channel_id=1, source_target_pairs={{0,16},{16,0},{1,17},{17,1},{2,18},{18,2},{3,19},{19,3},{4,20},{20... | collective-permute-start | bytes 1179656 | tf_op jit(solution)/shard_map/ppermute | solution.py:408
  27.3 1.5 %collective-permute-start.3 = (bf16[3,64,1024]{2,1,0:T(8,128)(2,1)S(1)}, bf16[3,64,1024]{2,1,0:T(8,128)(2,1)S(1)}, u32[]{:S(2)}, u32[]{:S(2)}) collective-permute-start(bf16[3,64,1024]{2,1,0:T(8,128)(2,1)S(1)} %collective-permute-done.1.refs_2_), channel_id=1, source_target_pairs={{0,2},{1,3},{2,0},{3,1},{4,6},{5,7},{6,4},{7,5},{8,10},{9,11},{10,... | collective-permute-start | bytes 1179656 | tf_op jit(solution)/shard_map/ppermute | solution.py:393
  28.8 1.2 %shard_map.68 = bf16[528,1024]{1,0:T(8,128)(2,1)S(1)} custom-call(s32[1,1024]{1,0:T(1,128)S(1)} %get-tuple-element.58.flat_ref, f32[64,128]{1,0:T(8,128)S(1)} %get-tuple-element.41.meta_ref, bf16[1024,1024]{1,0:T(8,128)(2,1)S(1)} %copy-done.4), custom_call_target="tpu_custom_call" | custom-call | flops 20000000000 | bytes 1000000000 | tf_op jit(solution)/shard_map/pallas_call | solution.py:467
  30.2 6.8 %collective-permute-done.3.refs_4_ = bf16[3,64,1024]{2,1,0:T(8,128)(2,1)S(1)} collective-permute-done((bf16[3,64,1024]{2,1,0:T(8,128)(2,1)S(1)}, bf16[3,64,1024]{2,1,0:T(8,128)(2,1)S(1)}, u32[]{:S(2)}, u32[]{:S(2)}) %collective-permute-start.3) | collective-permute-done | bytes 393248 | tf_op jit(solution)/shard_map/ppermute | solution.py:393
  37.6 1.6 %collective-permute-start.5 = (bf16[3,32,1024]{2,1,0:T(8,128)(2,1)S(1)}, bf16[3,32,1024]{2,1,0:T(8,128)(2,1)S(1)}, u32[]{:S(2)}, u32[]{:S(2)}) collective-permute-start(bf16[3,32,1024]{2,1,0:T(8,128)(2,1)S(1)} %slice.71), channel_id=1, source_target_pairs={{0,2},{1,3},{2,0},{3,1},{4,6},{5,7},{6,4},{7,5},{8,10},{9,11},{10,... | collective-permute-start | bytes 589832 | tf_op jit(solution)/shard_map/ppermute | solution.py:393
  39.1 1.3 %shard_map.69.refs_7_ = bf16[528,1024]{1,0:T(8,128)(2,1)S(1)} custom-call(s32[1,1024]{1,0:T(1,128)S(1)} %get-tuple-element.58.flat_ref, f32[64,128]{1,0:T(8,128)S(1)} %get-tuple-element.41.meta_ref, bf16[1024,1024]{1,0:T(8,128)(2,1)S(1)} %copy-done.4), custom_call_target="tpu_custom_call" | custom-call | flops 20000000000 | bytes 1000000000 | tf_op jit(solution)/shard_map/pallas_call | solution.py:477
  40.5 4.0 %collective-permute-done.7.refs_9_ = bf16[528,1024]{1,0:T(8,128)(2,1)S(1)} collective-permute-done((bf16[528,1024]{1,0:T(8,128)(2,1)S(1)}, bf16[528,1024]{1,0:T(8,128)(2,1)S(1)}, u32[]{:S(2)}, u32[]{:S(2)}) %collective-permute-start.7) | collective-permute-done | bytes 1081376 | tf_op jit(solution)/shard_map/ppermute | solution.py:400
  44.5 1.3 %shard_map.75.refs_3_ = bf16[528,1024]{1,0:T(8,128)(2,1)S(1)} custom-call(s32[1,1024]{1,0:T(1,128)S(1)} %get-tuple-element.58.flat_ref, f32[64,128]{1,0:T(8,128)S(1)} %get-tuple-element.41.meta_ref, bf16[1024,1024]{1,0:T(8,128)(2,1)S(1)} %copy-done.4), custom_call_target="tpu_custom_call" | custom-call | flops 20000000000 | bytes 1000000000 | tf_op jit(solution)/shard_map/pallas_call | solution.py:477
  46.4 0.9 collective-permute-done.8.refs_10_
  47.2 3.3 %shard_map.70 = (f32[1,128,1024]{2,1,0:T(8,128)S(1)}, f32[1,8,256]{2,1,0:T(8,128)S(1)}, f32[1,8,640]{2,1,0:T(8,128)S(1)}, bf16[128,1024]{1,0:T(8,128)(2,1)S(1)}) custom-call(s32[3]{0:T(128)S(1)} %pad_add_fusion.refs_0_.code_ref, f32[6]{0:T(128)S(1)} %collective-permute-done.refs_1_, bf16[3,64,1024]{2,1,0:T(8,128)(2,1)S(1)} %collective-permute-done.1.refs_2_, ...), custom_call_target="tpu_custom_call" | custom-call | flops 20000000000 | bytes 1 | tf_op jit(solution)/shard_map/pallas_call | solution.py:328
  50.5 1.8 %collective-permute-start.9 = (bf16[128,1024]{1,0:T(8,128)(2,1)S(1)}, bf16[128,1024]{1,0:T(8,128)(2,1)S(1)}, u32[]{:S(2)}, u32[]{:S(2)}) collective-permute-start(bf16[128,1024]{1,0:T(8,128)(2,1)S(1)} %get-tuple-element.50), channel_id=1, source_target_pairs={{0,2},{1,3},{2,0},{3,1},{4,6},{5,7},{6,4},{7,5},{8,10},{9,11},{10,... | collective-permute-start | bytes 786440 | tf_op jit(solution)/shard_map/ppermute | solution.py:393
  52.4 4.3 %shard_map.72 = (f32[2,128,1024]{2,1,0:T(8,128)S(1)}, f32[2,8,256]{2,1,0:T(8,128)S(1)}, f32[2,8,640]{2,1,0:T(8,128)S(1)}, bf16[272,1024]{1,0:T(8,128)(2,1)S(1)}) custom-call(s32[3]{0:T(128)S(1)} %pad_add_fusion.refs_0_.code_ref, f32[6]{0:T(128)S(1)} %collective-permute-done.refs_1_, bf16[3,64,1024]{2,1,0:T(8,128)(2,1)S(1)} %collective-permute-done.1.refs_2_, ...), custom_call_target="tpu_custom_call" | custom-call | flops 20000000000 | bytes 1 | tf_op jit(solution)/shard_map/pallas_call | solution.py:328
  57.0 2.0 %collective-permute-done.9 = bf16[128,1024]{1,0:T(8,128)(2,1)S(1)} collective-permute-done((bf16[128,1024]{1,0:T(8,128)(2,1)S(1)}, bf16[128,1024]{1,0:T(8,128)(2,1)S(1)}, u32[]{:S(2)}, u32[]{:S(2)}) %collective-permute-start.9) | collective-permute-done | bytes 262176 | tf_op jit(solution)/shard_map/ppermute | solution.py:393
  59.1 2.9 %collective-permute-start.15 = (bf16[128,1024]{1,0:T(8,128)(2,1)S(1)}, bf16[128,1024]{1,0:T(8,128)(2,1)S(1)}, u32[]{:S(2)}, u32[]{:S(2)}) collective-permute-start(bf16[128,1024]{1,0:T(8,128)(2,1)S(1)} %fusion.1), channel_id=1, source_target_pairs={{0,8},{4,12},{8,0},{12,4},{1,9},{5,13},{9,1},{13,5},{2,10},{6,14},... | collective-permute-start | bytes 786440 | tf_op jit(solution)/shard_map/ppermute | solution.py:405
  62.0 6.9 %collective-permute-done.12.refs_5_ = bf16[528,1024]{1,0:T(8,128)(2,1)S(1)} collective-permute-done((bf16[528,1024]{1,0:T(8,128)(2,1)S(1)}, bf16[528,1024]{1,0:T(8,128)(2,1)S(1)}, u32[]{:S(2)}, u32[]{:S(2)}) %collective-permute-start.12) | collective-permute-done | bytes 1081376 | tf_op jit(solution)/shard_map/ppermute | solution.py:400
  68.9 2.3 %collective-permute-done.10 = bf16[272,1024]{1,0:T(8,128)(2,1)S(1)} collective-permute-done((bf16[272,1024]{1,0:T(8,128)(2,1)S(1)}, bf16[272,1024]{1,0:T(8,128)(2,1)S(1)}, u32[]{:S(2)}, u32[]{:S(2)}) %collective-permute-start.10) | collective-permute-done | bytes 557088 | tf_op jit(solution)/shard_map/ppermute | solution.py:393
  71.5 2.6 %collective-permute-start.16 = (bf16[272,1024]{1,0:T(8,128)(2,1)S(1)}, bf16[272,1024]{1,0:T(8,128)(2,1)S(1)}, u32[]{:S(2)}, u32[]{:S(2)}) collective-permute-start(bf16[272,1024]{1,0:T(8,128)(2,1)S(1)} %pad_maximum_fusion), channel_id=1, source_target_pairs={{0,8},{4,12},{8,0},{12,4},{1,9},{5,13},{9,1},{13,5},{2,10},{6,14},... | collective-permute-start | bytes 1671176 | tf_op jit(solution)/shard_map/ppermute | solution.py:405
  74.1 5.7 %shard_map.76 = (f32[3,128,1024]{2,1,0:T(8,128)S(1)}, f32[3,8,256]{2,1,0:T(8,128)S(1)}, f32[3,8,640]{2,1,0:T(8,128)S(1)}, bf16[400,1024]{1,0:T(8,128)(2,1)S(1)}) custom-call(s32[3]{0:T(128)S(1)} %pad_add_fusion.refs_0_.code_ref, f32[6]{0:T(128)S(1)} %copy-done.5, bf16[6,256,1024]{2,1,0:T(8,128)(2,1)S(1)} %copy-done, ...), custom_call_target="tpu_custom_call" | custom-call | flops 20000000000 | bytes 1 | tf_op jit(solution)/shard_map/pallas_call | solution.py:328
  79.8 1.4 %collective-permute-start.14 = (bf16[400,1024]{1,0:T(8,128)(2,1)S(1)}, bf16[400,1024]{1,0:T(8,128)(2,1)S(1)}, u32[]{:S(2)}, u32[]{:S(2)}) collective-permute-start(bf16[400,1024]{1,0:T(8,128)(2,1)S(1)} %get-tuple-element.62), channel_id=1, source_target_pairs={{0,2},{1,3},{2,0},{3,1},{4,6},{5,7},{6,4},{7,5},{8,10},{9,11},{10,... | collective-permute-start | bytes 2457608 | tf_op jit(solution)/shard_map/ppermute | solution.py:393
  81.5 2.5 %collective-permute-start.19 = (f32[6,160]{1,0:T(8,128)S(1)}, f32[6,160]{1,0:T(8,128)S(1)}, u32[]{:S(2)}, u32[]{:S(2)}) collective-permute-start(f32[6,160]{1,0:T(8,128)S(1)} %get-tuple-element.73), channel_id=1, source_target_pairs={{0,4},{1,5},{2,6},{3,7},{4,0},{5,1},{6,2},{7,3},{8,12},{9,13},{10,... | collective-permute-start | bytes 11528 | tf_op jit(solution)/shard_map/ppermute | solution.py:418
  85.6 1.4 %collective-permute-done.20 = f32[6,160]{1,0:T(8,128)S(1)} collective-permute-done((f32[6,160]{1,0:T(8,128)S(1)}, f32[6,160]{1,0:T(8,128)S(1)}, u32[]{:S(2)}, u32[]{:S(2)}) %collective-permute-start.20) | collective-permute-done | bytes 3872 | tf_op jit(solution)/shard_map/ppermute | solution.py:418
  87.6 0.9 shard_map.81
  88.5 10.3 %collective-permute-done.14.refs_0_.refs_1_ = bf16[400,1024]{1,0:T(8,128)(2,1)S(1)} collective-permute-done((bf16[400,1024]{1,0:T(8,128)(2,1)S(1)}, bf16[400,1024]{1,0:T(8,128)(2,1)S(1)}, u32[]{:S(2)}, u32[]{:S(2)}) %collective-permute-start.14) | collective-permute-done | bytes 819232 | tf_op jit(solution)/shard_map/ppermute | solution.py:393
  98.9 1.2 %shard_map.78 = (f32[3,72,1024]{2,1,0:T(8,128)S(1)}, f32[8,128]{1,0:T(8,128)S(1)}) custom-call(s32[3]{0:T(128)S(1)} %pad_add_fusion.refs_0_.code_ref, f32[3,128,1024]{2,1,0:T(8,128)S(1)} %copy-done.7, f32[3,8,256]{2,1,0:T(8,128)S(1)} %get-tuple-element.61.mass_ref, bf16[400,1024]{1,0:T(8,128)(2,1)S(1)} %collective-permute-done.14.refs_0_.refs_1_, ...), custom_call_target="tpu_custom_call" | custom-call | flops 20000000000 | bytes 1 | tf_op jit(solution)/shard_map/pallas_call | solution.py:616
  100.2 2.4 %shard_map.77._ = f32[6,64,1024]{2,1,0:T(8,128)} custom-call(s32[3]{0:T(128)S(1)} %pad_add_fusion.refs_0_.code_ref, f32[3,128,1024]{2,1,0:T(8,128)S(1)} %copy-done.7, f32[3,8,256]{2,1,0:T(8,128)S(1)} %get-tuple-element.61.mass_ref, bf16[400,1024]{1,0:T(8,128)(2,1)S(1)} %collective-permute-done.14.refs_0_.refs_1_, ...), custom_call_target="tpu_custom_call" | custom-call | flops 20000000000 | bytes 1 | tf_op jit(solution)/shard_map/pallas_call | solution.py:616
  102.6 2.0 %shard_map.79 = (f32[6,64,1024]{2,1,0:T(8,128)}, f32[6,64]{1,0:T(8,128)}) custom-call(s32[3]{0:T(128)S(1)} %pad_add_fusion.refs_0_.code_ref, f32[6,64,1024]{2,1,0:T(8,128)} %shard_map.77._, f32[3,72,1024]{2,1,0:T(8,128)S(1)} %collective-permute-done.17.swap_ref.line_ref, ...), custom_call_target="tpu_custom_call", output_to_operand_aliasing={{0}: (1, {})} | custom-call | flops 20000000000 | bytes 1 | tf_op jit(solution)/shard_map/pallas_call | solution.py:640
  (64 shorter events, 5.5 us)
Async XLA Ops:
  0.6 38.5 %collective-permute-start = (f32[6]{0:T(128)}, f32[6]{0:T(128)S(1)}, u32[]{:S(2)}, u32[]{:S(2)}) collective-permute-start(f32[6]{0:T(128)} %refs_1_.1), channel_id=1, source_target_pairs={{0,8},{4,12},{8,0},{12,4},{1,9},{5,13},{9,1},{13,5},{2,10},{6,14},... | collective-permute-start | bytes 80 | tf_op jit(solution)/shard_map/ppermute | solution.py:405
  5.8 20.1 %collective-permute-start.1 = (bf16[3,64,1024]{2,1,0:T(8,128)(2,1)S(1)}, bf16[3,64,1024]{2,1,0:T(8,128)(2,1)S(1)}, u32[]{:S(2)}, u32[]{:S(2)}) collective-permute-start(bf16[3,64,1024]{2,1,0:T(8,128)(2,1)S(1)} %constant_dynamic-slice_fusion), channel_id=1, source_target_pairs={{0,8},{4,12},{8,0},{12,4},{1,9},{5,13},{9,1},{13,5},{2,10},{6,14},... | collective-permute-start | bytes 1179656 | tf_op jit(solution)/shard_map/ppermute | solution.py:405
  6.7 1.6 %copy-start.3 = (bf16[1024,1024]{1,0:T(8,128)(2,1)S(1)}, bf16[1024,1024]{1,0:T(8,128)(2,1)}, u32[]{:S(2)}) copy-start(bf16[1024,1024]{1,0:T(8,128)(2,1)} %frames_ref.7) | copy-start | bytes 6291460
  8.3 2.0 %copy-start.1 = (s32[1,1024]{1,0:T(1,128)}, s32[1,1024]{1,0:T(1,128)S(1)}, u32[]{:S(2)}) copy-start(s32[1,1024]{1,0:T(1,128)S(1)} %fusion.12.rel_ref) | copy-start | bytes 12292
  8.3 20.6 %copy-start.4 = (bf16[1024,1024]{1,0:T(8,128)(2,1)S(1)}, bf16[1024,1024]{1,0:T(8,128)(2,1)}, u32[]{:S(2)}) copy-start(bf16[1024,1024]{1,0:T(8,128)(2,1)} %frames_ref.7) | copy-start | bytes 6291460
  10.3 34.2 %collective-permute-start.7 = (bf16[528,1024]{1,0:T(8,128)(2,1)S(1)}, bf16[528,1024]{1,0:T(8,128)(2,1)S(1)}, u32[]{:S(2)}, u32[]{:S(2)}) collective-permute-start(bf16[528,1024]{1,0:T(8,128)(2,1)S(1)} %get-tuple-element.43), channel_id=1, source_target_pairs={{0,4},{4,0},{8,12},{12,8},{1,5},{5,1},{9,13},{13,9},{2,6},{6,2},{1... | collective-permute-start | bytes 3244040 | tf_op jit(solution)/shard_map/ppermute | solution.py:400
  25.8 11.7 %collective-permute-start.2 = (bf16[3,64,1024]{2,1,0:T(8,128)(2,1)S(1)}, bf16[3,64,1024]{2,1,0:T(8,128)(2,1)S(1)}, u32[]{:S(2)}, u32[]{:S(2)}) collective-permute-start(bf16[3,64,1024]{2,1,0:T(8,128)(2,1)S(1)} %collective-permute-done.1.refs_2_), channel_id=1, source_target_pairs={{0,16},{16,0},{1,17},{17,1},{2,18},{18,2},{3,19},{19,3},{4,20},{20... | collective-permute-start | bytes 1179656 | tf_op jit(solution)/shard_map/ppermute | solution.py:408
  27.3 9.6 %collective-permute-start.3 = (bf16[3,64,1024]{2,1,0:T(8,128)(2,1)S(1)}, bf16[3,64,1024]{2,1,0:T(8,128)(2,1)S(1)}, u32[]{:S(2)}, u32[]{:S(2)}) collective-permute-start(bf16[3,64,1024]{2,1,0:T(8,128)(2,1)S(1)} %collective-permute-done.1.refs_2_), channel_id=1, source_target_pairs={{0,2},{1,3},{2,0},{3,1},{4,6},{5,7},{6,4},{7,5},{8,10},{9,11},{10,... | collective-permute-start | bytes 1179656 | tf_op jit(solution)/shard_map/ppermute | solution.py:393
  30.1 38.8 %collective-permute-start.12 = (bf16[528,1024]{1,0:T(8,128)(2,1)S(1)}, bf16[528,1024]{1,0:T(8,128)(2,1)S(1)}, u32[]{:S(2)}, u32[]{:S(2)}) collective-permute-start(bf16[528,1024]{1,0:T(8,128)(2,1)S(1)} %shard_map.68), channel_id=1, source_target_pairs={{0,4},{4,0},{8,12},{12,8},{1,5},{5,1},{9,13},{13,9},{2,6},{6,2},{1... | collective-permute-start | bytes 3244040 | tf_op jit(solution)/shard_map/ppermute | solution.py:400
  37.0 8.8 %collective-permute-start.4 = (bf16[3,32,1024]{2,1,0:T(8,128)(2,1)S(1)}, bf16[3,32,1024]{2,1,0:T(8,128)(2,1)S(1)}, u32[]{:S(2)}, u32[]{:S(2)}) collective-permute-start(bf16[3,32,1024]{2,1,0:T(8,128)(2,1)S(1)} %slice.70), channel_id=1, source_target_pairs={{0,16},{16,0},{1,17},{17,1},{2,18},{18,2},{3,19},{19,3},{4,20},{20... | collective-permute-start | bytes 589832 | tf_op jit(solution)/shard_map/ppermute | solution.py:408
  37.6 8.8 %collective-permute-start.5 = (bf16[3,32,1024]{2,1,0:T(8,128)(2,1)S(1)}, bf16[3,32,1024]{2,1,0:T(8,128)(2,1)S(1)}, u32[]{:S(2)}, u32[]{:S(2)}) collective-permute-start(bf16[3,32,1024]{2,1,0:T(8,128)(2,1)S(1)} %slice.71), channel_id=1, source_target_pairs={{0,2},{1,3},{2,0},{3,1},{4,6},{5,7},{6,4},{7,5},{8,10},{9,11},{10,... | collective-permute-start | bytes 589832 | tf_op jit(solution)/shard_map/ppermute | solution.py:393
  40.4 5.9 %collective-permute-start.6 = (bf16[528,1024]{1,0:T(8,128)(2,1)S(1)}, bf16[528,1024]{1,0:T(8,128)(2,1)S(1)}, u32[]{:S(2)}, u32[]{:S(2)}) collective-permute-start(bf16[528,1024]{1,0:T(8,128)(2,1)S(1)} %shard_map.69.refs_7_), channel_id=1, source_target_pairs={{0,1},{1,0},{2,3},{3,2},{4,5},{5,4},{6,7},{7,6},{8,9},{9,8},{10,11... | collective-permute-start | bytes 3244040 | tf_op jit(solution)/shard_map/ppermute | solution.py:390
  44.5 2.7 %collective-permute-start.8 = (bf16[528,1024]{1,0:T(8,128)(2,1)S(1)}, bf16[528,1024]{1,0:T(8,128)(2,1)S(1)}, u32[]{:S(2)}, u32[]{:S(2)}) collective-permute-start(bf16[528,1024]{1,0:T(8,128)(2,1)S(1)} %collective-permute-done.7.refs_9_), channel_id=1, source_target_pairs={{0,1},{1,0},{2,3},{3,2},{4,5},{5,4},{6,7},{7,6},{8,9},{9,8},{10,11... | collective-permute-start | bytes 3244040 | tf_op jit(solution)/shard_map/ppermute | solution.py:390
  45.8 28.3 %collective-permute-start.11 = (bf16[528,1024]{1,0:T(8,128)(2,1)S(1)}, bf16[528,1024]{1,0:T(8,128)(2,1)S(1)}, u32[]{:S(2)}, u32[]{:S(2)}) collective-permute-start(bf16[528,1024]{1,0:T(8,128)(2,1)S(1)} %shard_map.75.refs_3_), channel_id=1, source_target_pairs={{0,1},{1,0},{2,3},{3,2},{4,5},{5,4},{6,7},{7,6},{8,9},{9,8},{10,11... | collective-permute-start | bytes 3244040 | tf_op jit(solution)/shard_map/ppermute | solution.py:390
  50.5 8.5 %collective-permute-start.9 = (bf16[128,1024]{1,0:T(8,128)(2,1)S(1)}, bf16[128,1024]{1,0:T(8,128)(2,1)S(1)}, u32[]{:S(2)}, u32[]{:S(2)}) collective-permute-start(bf16[128,1024]{1,0:T(8,128)(2,1)S(1)} %get-tuple-element.50), channel_id=1, source_target_pairs={{0,2},{1,3},{2,0},{3,1},{4,6},{5,7},{6,4},{7,5},{8,10},{9,11},{10,... | collective-permute-start | bytes 786440 | tf_op jit(solution)/shard_map/ppermute | solution.py:393
  56.7 14.5 %collective-permute-start.10 = (bf16[272,1024]{1,0:T(8,128)(2,1)S(1)}, bf16[272,1024]{1,0:T(8,128)(2,1)S(1)}, u32[]{:S(2)}, u32[]{:S(2)}) collective-permute-start(bf16[272,1024]{1,0:T(8,128)(2,1)S(1)} %get-tuple-element.53), channel_id=1, source_target_pairs={{0,2},{1,3},{2,0},{3,1},{4,6},{5,7},{6,4},{7,5},{8,10},{9,11},{10,... | collective-permute-start | bytes 1671176 | tf_op jit(solution)/shard_map/ppermute | solution.py:393
  59.1 29.4 %collective-permute-start.15 = (bf16[128,1024]{1,0:T(8,128)(2,1)S(1)}, bf16[128,1024]{1,0:T(8,128)(2,1)S(1)}, u32[]{:S(2)}, u32[]{:S(2)}) collective-permute-start(bf16[128,1024]{1,0:T(8,128)(2,1)S(1)} %fusion.1), channel_id=1, source_target_pairs={{0,8},{4,12},{8,0},{12,4},{1,9},{5,13},{9,1},{13,5},{2,10},{6,14},... | collective-permute-start | bytes 786440 | tf_op jit(solution)/shard_map/ppermute | solution.py:405
  68.9 5.2 %collective-permute-start.13 = (bf16[528,1024]{1,0:T(8,128)(2,1)S(1)}, bf16[528,1024]{1,0:T(8,128)(2,1)S(1)}, u32[]{:S(2)}, u32[]{:S(2)}) collective-permute-start(bf16[528,1024]{1,0:T(8,128)(2,1)S(1)} %collective-permute-done.12.refs_5_), channel_id=1, source_target_pairs={{0,1},{1,0},{2,3},{3,2},{4,5},{5,4},{6,7},{7,6},{8,9},{9,8},{10,11... | collective-permute-start | bytes 3244040 | tf_op jit(solution)/shard_map/ppermute | solution.py:390
  71.5 2.6 %copy-start = (bf16[6,256,1024]{2,1,0:T(8,128)(2,1)S(1)}, bf16[6,256,1024]{2,1,0:T(8,128)(2,1)}, u32[]{:S(2)}) copy-start(bf16[6,256,1024]{2,1,0:T(8,128)(2,1)} %refs_2_.1) | copy-start | bytes 9437188
  71.5 2.6 %copy-start.5 = (f32[6]{0:T(128)S(1)}, f32[6]{0:T(128)}, u32[]{:S(2)}) copy-start(f32[6]{0:T(128)} %refs_1_.1) | copy-start | bytes 76
  71.5 27.4 %collective-permute-start.16 = (bf16[272,1024]{1,0:T(8,128)(2,1)S(1)}, bf16[272,1024]{1,0:T(8,128)(2,1)S(1)}, u32[]{:S(2)}, u32[]{:S(2)}) collective-permute-start(bf16[272,1024]{1,0:T(8,128)(2,1)S(1)} %pad_maximum_fusion), channel_id=1, source_target_pairs={{0,8},{4,12},{8,0},{12,4},{1,9},{5,13},{9,1},{13,5},{2,10},{6,14},... | collective-permute-start | bytes 1671176 | tf_op jit(solution)/shard_map/ppermute | solution.py:405
  79.8 1.6 %copy-start.6 = (f32[3,128,1024]{2,1,0:T(8,128)}, f32[3,128,1024]{2,1,0:T(8,128)S(1)}, u32[]{:S(2)}) copy-start(f32[3,128,1024]{2,1,0:T(8,128)S(1)} %get-tuple-element.60.keep_ref) | copy-start | bytes 4718596
  79.8 19.1 %collective-permute-start.14 = (bf16[400,1024]{1,0:T(8,128)(2,1)S(1)}, bf16[400,1024]{1,0:T(8,128)(2,1)S(1)}, u32[]{:S(2)}, u32[]{:S(2)}) collective-permute-start(bf16[400,1024]{1,0:T(8,128)(2,1)S(1)} %get-tuple-element.62), channel_id=1, source_target_pairs={{0,2},{1,3},{2,0},{3,1},{4,6},{5,7},{6,4},{7,5},{8,10},{9,11},{10,... | collective-permute-start | bytes 2457608 | tf_op jit(solution)/shard_map/ppermute | solution.py:393
  81.3 6.3 %copy-start.2 = (s32[1,1024]{1,0:T(1,128)S(1)}, s32[1,1024]{1,0:T(1,128)}, u32[]{:S(2)}) copy-start(s32[1,1024]{1,0:T(1,128)} %copy-done.1) | copy-start | bytes 12292
  81.4 2.6 %collective-permute-start.18 = (f32[6,160]{1,0:T(8,128)S(1)}, f32[6,160]{1,0:T(8,128)S(1)}, u32[]{:S(2)}, u32[]{:S(2)}) collective-permute-start(f32[6,160]{1,0:T(8,128)S(1)} %get-tuple-element.72), channel_id=1, source_target_pairs={{0,1},{1,0},{2,3},{3,2},{4,5},{5,4},{6,7},{7,6},{8,9},{9,8},{10,11... | collective-permute-start | bytes 11528 | tf_op jit(solution)/shard_map/ppermute | solution.py:418
  81.5 4.2 %collective-permute-start.19 = (f32[6,160]{1,0:T(8,128)S(1)}, f32[6,160]{1,0:T(8,128)S(1)}, u32[]{:S(2)}, u32[]{:S(2)}) collective-permute-start(f32[6,160]{1,0:T(8,128)S(1)} %get-tuple-element.73), channel_id=1, source_target_pairs={{0,4},{1,5},{2,6},{3,7},{4,0},{5,1},{6,2},{7,3},{8,12},{9,13},{10,... | collective-permute-start | bytes 11528 | tf_op jit(solution)/shard_map/ppermute | solution.py:418
  84.0 3.1 %collective-permute-start.20 = (f32[6,160]{1,0:T(8,128)S(1)}, f32[6,160]{1,0:T(8,128)S(1)}, u32[]{:S(2)}, u32[]{:S(2)}) collective-permute-start(f32[6,160]{1,0:T(8,128)S(1)} %get-tuple-element.74), channel_id=1, source_target_pairs={{0,5},{1,4},{2,7},{3,6},{4,1},{5,0},{6,3},{7,2},{8,13},{9,12},{10,... | collective-permute-start | bytes 11528 | tf_op jit(solution)/shard_map/ppermute | solution.py:418
  87.6 11.3 %copy-start.7 = (f32[3,128,1024]{2,1,0:T(8,128)S(1)}, f32[3,128,1024]{2,1,0:T(8,128)}, u32[]{:S(2)}) copy-start(f32[3,128,1024]{2,1,0:T(8,128)} %copy-done.6) | copy-start | bytes 4718596
  100.1 2.5 %collective-permute-start.17 = (f32[3,72,1024]{2,1,0:T(8,128)S(1)}, f32[3,72,1024]{2,1,0:T(8,128)S(1)}, u32[]{:S(2)}, u32[]{:S(2)}) collective-permute-start(f32[3,72,1024]{2,1,0:T(8,128)S(1)} %get-tuple-element.65), channel_id=1, source_target_pairs={{0,1},{1,0},{2,3},{3,2},{4,5},{5,4},{6,7},{7,6},{8,9},{9,8},{10,11... | collective-permute-start | bytes 2654216 | tf_op jit(solution)/shard_map/ppermute | solution.py:390
